TPU v7x, 32 devices: a whole 2x2x4 slice. The times are simulated.
32 devices in a mesh: grp: 2 (over y), col: 16 (over z, x, core).
Axes of the slice: x: 2, y: 2, z: 4, core: 2. Of those that a mesh axis runs over, the one named last changes fastest.
Arguments:
- doc_factors: float32 [1024, 256], P(('grp', 'col')), may hold values from -1.5 to 1.5
- ngram_factors: float32 [8192, 256], P('col'), may hold values from -1.5 to 1.5
- block_docs: int32 [2, 16, 16], P('grp', 'col'), may hold values from 0 to 3, as said below
- block_ngrams: int32 [2, 16, 16], P('grp', 'col'), may hold values from 0 to 3, as said below
- block_counts: int32 [2, 16], P('grp', 'col'), may hold values from 4 to 16, as said below
- pmi: bfloat16 [2, 16, 16, 128, 128], P('grp', 'col'), may hold values from -6 to 6
- weights: bfloat16 [2, 16, 16, 128, 128], P('grp', 'col'), may hold values from 0.049804688 to 1
Outputs:
- doc_out: float32 [1024, 256], P(('grp', 'col'))
- ngram_out: float32 [8192, 256], P('col')
Inputs may be any that keep to these rules, and one draw needn't show every extreme that they name: `block_docs`: within one device's slots every pair (document block, n-gram block) appears exactly once. `block_ngrams`: paired with block_docs as stated there. `block_counts`: some device has all 16 slots live.
All inputs are finite; a program needn't handle non-finite values.
Results may differ from a plain program's by a relative error of at most 0.0086.
Values may be sent and summed in bfloat16 or wider, within the bound.
No kernel may reach another device: no remote copies, remote signals or barrier semaphores. Data moves between devices by JAX's collectives and lax.ppermute only.
A program may use at most 64 MiB of HBM per device.

v0:
```python
import math

import jax
import jax.numpy as jnp
from jax import lax
from jax.sharding import PartitionSpec as P

R = 256
BLK = 128


def local_grads(group_half, ngram_now, docs, ngrams, count, tiles, scales):
    highest = lax.Precision.HIGHEST
    doc_blocks = group_half.reshape(-1, BLK, R)
    ngram_blocks = ngram_now.astype(jnp.bfloat16).reshape(-1, BLK, R)
    left = jnp.take(doc_blocks, docs, axis=0)
    right = jnp.take(ngram_blocks, ngrams, axis=0)
    scores = jnp.einsum("kir,kjr->kij", left, right, preferred_element_type=jnp.float32)
    live = (jnp.arange(docs.shape[0], dtype=jnp.int32) < count).astype(jnp.float32)
    err = (
        live[:, None, None] * scales.astype(jnp.float32) * (scores - tiles.astype(jnp.float32))
    ).astype(jnp.bfloat16)
    doc_terms = jnp.einsum("kij,kjr->kir", err, right, preferred_element_type=jnp.float32)
    ngram_terms = jnp.einsum("kij,kir->kjr", err, left, preferred_element_type=jnp.float32)
    doc_onehot = (
        docs[:, None] == jnp.arange(doc_blocks.shape[0], dtype=jnp.int32)[None, :]
    ).astype(jnp.float32)
    ngram_onehot = (
        ngrams[:, None] == jnp.arange(ngram_blocks.shape[0], dtype=jnp.int32)[None, :]
    ).astype(jnp.float32)
    grad_doc = jnp.einsum("kd,kir->dir", doc_onehot, doc_terms, precision=highest).reshape(-1, R)
    grad_ngram = jnp.einsum("kn,kjr->njr", ngram_onehot, ngram_terms, precision=highest).reshape(
        -1, R
    )
    return (grad_doc, grad_ngram)


def shards(doc_factors, ngram_factors, block_docs, block_ngrams, block_counts, pmi, weights):
    docs = block_docs.reshape(-1)
    ngrams = block_ngrams.reshape(-1)
    count = block_counts.reshape(())
    tiles = pmi.reshape(-1, BLK, BLK)
    scales = weights.reshape(-1, BLK, BLK)
    shard_count = lax.axis_size("col")
    group_count = lax.axis_size("grp")
    doc_total = doc_factors.shape[0] * shard_count * group_count
    ngram_total = ngram_factors.shape[0] * shard_count
    width = doc_factors.shape[1]
    doc_base = math.sqrt(ngram_total) + 1.5 * math.sqrt(width)
    ngram_base = math.sqrt(doc_total) + 1.5 * math.sqrt(width)
    doc_rate = 100.0 / (doc_base * doc_base)
    ngram_rate = 100.0 / (ngram_base * ngram_base)
    ngram_now = ngram_factors
    doc_now = doc_factors
    for step in range(2):
        group_half = lax.all_gather(doc_now.astype(jnp.bfloat16), "col", axis=0, tiled=True)
        grad_doc, grad_ngram = local_grads(
            group_half, ngram_now, docs, ngrams, count, tiles, scales
        )
        own_grad = lax.psum_scatter(grad_doc, "col", scatter_dimension=0, tiled=True)
        doc_now = doc_now - doc_rate * own_grad
        summed = lax.psum(grad_ngram, "grp")
        ngram_now = ngram_now - ngram_rate * summed
    return (doc_now, ngram_now)


def solution(mesh):
    return jax.shard_map(
        shards,
        mesh=mesh,
        in_specs=(
            P(("grp", "col"), None),
            P("col", None),
            P("grp", "col", None),
            P("grp", "col", None),
            P("grp", "col"),
            P("grp", "col", None, None, None),
            P("grp", "col", None, None, None),
        ),
        out_specs=(P(("grp", "col"), None), P("col", None)),
        check_vma=False,
    )
```

profile of v0, /device:TPU:0, one launch (start us, length us, event | category | flops | bytes accessed | tf_op | source)
XLA Modules:
  0.0 193.2 jit_solution(15865118345700596362)
XLA Ops:
  8.0 0.0 all-reduce.3.cloned.1.call-start
  8.0 0.7 compare_select_fusion.1
  8.7 0.7 compare_select_fusion
  9.4 0.7 compare_and_fusion
  10.7 0.8 convert_element_type.47
  11.5 23.8 %all_gather.6 = bf16[512,256]{1,0:T(8,128)(2,1)S(1)} all-gather(bf16[32,256]{1,0:T(8,128)(2,1)S(1)} %convert_element_type.47), channel_id=1, replica_groups=mesh['grp'=2,'col'=16] {'col'}, dimensions={0}, use_global_device_ids=true | all-gather | bytes 278528 | tf_op jit(solution)/shard_map/all_gather | solution.py:56
  35.2 1.1 convert_element_type.48
  36.3 0.6 gather_fusion.1
  36.9 0.6 gather_fusion
  37.6 1.8 fusion.10
  39.3 0.0 copy-start.4
  39.3 0.5 fusion.12
  39.9 0.1 copy-done.4
  40.0 2.0 %fusion.4 = f32[4,128,256]{2,0,1:T(4,128)S(1)} fusion(f32[16,128,256]{2,1,0:T(8,128)S(1)} %fusion.12, s32[16]{0:T(128)S(1)} %bitcast.46), kind=kOutput, calls=%fused_computation.8 | convolution fusion | flops 25165888 | bytes 2621504 | tf_op jit(solution)/shard_map/kn,kjr->njr/dot_general | solution.py:32
  42.0 0.9 copy.10
  42.9 0.0 all-reduce.3.cloned.1.call-update
  42.9 0.0 reduce-scatter.3.cloned.1.call-start
  42.9 0.5 fusion.14
  43.4 0.1 copy-done.5
  43.5 2.0 %fusion.6 = f32[4,128,256]{2,0,1:T(4,128)S(1)} fusion(f32[16,128,256]{2,1,0:T(8,128)S(1)} %fusion.14, s32[16]{0:T(128)S(1)} %bitcast.48), kind=kOutput, calls=%fused_computation.10 | convolution fusion | flops 25165888 | bytes 2621504 | tf_op jit(solution)/shard_map/kd,kir->dir/dot_general | solution.py:31
  45.5 0.9 copy.9
  46.4 0.0 reduce-scatter.3.cloned.1.call-update
  46.4 0.0 all-reduce.5.cloned.1.call-start
  46.5 22.5 %all-reduce.3.cloned.1.call-done = f32[512,256]{1,0:T(8,128)} async-done(((f32[512,256]{1,0:T(8,128)}), f32[512,256]{1,0:T(8,128)}) %all-reduce.3.cloned.1.call-update) | async-done | bytes 524304 | tf_op jit(solution)/shard_map/psum | solution.py:62
  69.0 0.0 copy-done
  69.0 1.1 fusion.16
  70.1 0.6 gather_fusion.3
  70.7 29.9 %reduce-scatter.3.cloned.1.call-done = f32[32,256]{1,0:T(8,128)} async-done(((f32[512,256]{1,0:T(8,128)}), f32[32,256]{1,0:T(8,128)}) %reduce-scatter.3.cloned.1.call-update) | async-done | bytes 32784 | tf_op jit(solution)/shard_map/reduce_scatter | solution.py:60
  100.6 0.0 copy-done.2
  100.6 0.8 fusion.17
  101.4 20.1 %all_gather.7 = bf16[512,256]{1,0:T(8,128)(2,1)S(1)} all-gather(bf16[32,256]{1,0:T(8,128)(2,1)S(1)} %fusion.17), channel_id=1, replica_groups=mesh['grp'=2,'col'=16] {'col'}, dimensions={0}, use_global_device_ids=true | all-gather | bytes 278528 | tf_op jit(solution)/shard_map/all_gather | solution.py:56
  121.5 0.6 gather_fusion.2
  122.1 1.8 fusion.11
  123.8 0.5 fusion.13
  124.3 2.0 %fusion = f32[4,128,256]{2,0,1:T(4,128)S(1)} fusion(f32[16,128,256]{2,1,0:T(8,128)S(1)} %fusion.13, s32[16]{0:T(128)S(1)} %bitcast.47), kind=kOutput, calls=%fused_computation.4 | convolution fusion | flops 25165888 | bytes 2621504 | tf_op jit(solution)/shard_map/kn,kjr->njr/dot_general | solution.py:32
  126.3 0.9 copy.12
  127.2 0.0 all-reduce.5.cloned.1.call-update
  127.2 0.2 reduce-scatter.5.cloned.1.call-start
  127.5 0.5 fusion.15
  128.0 2.0 %fusion.2 = f32[4,128,256]{2,0,1:T(4,128)S(1)} fusion(f32[16,128,256]{2,1,0:T(8,128)S(1)} %fusion.15, s32[16]{0:T(128)S(1)} %bitcast.49), kind=kOutput, calls=%fused_computation.6 | convolution fusion | flops 25165888 | bytes 2621504 | tf_op jit(solution)/shard_map/kd,kir->dir/dot_general | solution.py:31
  130.0 0.0 copy-start.3
  130.0 0.9 copy.11
  130.9 0.0 reduce-scatter.5.cloned.1.call-update
  130.9 22.3 %all-reduce.5.cloned.1.call-done = f32[512,256]{1,0:T(8,128)} async-done(((f32[512,256]{1,0:T(8,128)}), f32[512,256]{1,0:T(8,128)}) %all-reduce.5.cloned.1.call-update) | async-done | bytes 524304 | tf_op jit(solution)/shard_map/psum | solution.py:62
  153.3 1.9 %multiply_subtract_fusion = f32[512,256]{1,0:T(8,128)} fusion(f32[512,256]{1,0:T(8,128)} %all-reduce.5.cloned.1.call-done, f32[512,256]{1,0:T(8,128)S(1)} %copy-done, f32[512,256]{1,0:T(8,128)S(1)} %copy-done.1), kind=kLoop, calls=%fused_computation.23 | loop fusion | flops 524288 | bytes 2097152 | tf_op jit(solution)/shard_map/sub | solution.py:63
  155.2 29.2 %reduce-scatter.5.cloned.1.call-done = f32[32,256]{1,0:T(8,128)} async-done(((f32[512,256]{1,0:T(8,128)}), f32[32,256]{1,0:T(8,128)}) %reduce-scatter.5.cloned.1.call-update) | async-done | bytes 32784 | tf_op jit(solution)/shard_map/reduce_scatter | solution.py:60
  184.4 0.0 copy-done.3
  184.4 1.4 multiply_subtract_fusion.2
  (8 shorter events, 0.0 us)
Async XLA Ops:
  8.0 61.0 %all-reduce.3.cloned.1.call-start = ((), (), s32[]{:S(2)}) async-start(), calls=%async_computation.3 | async-start | bytes 1048576 | tf_op jit(solution)/shard_map/psum | solution.py:62
  39.3 0.7 copy-start.4
  42.9 0.7 copy-start.5
  42.9 57.7 %reduce-scatter.3.cloned.1.call-start = ((), (), s32[]{:S(2)}) async-start(), calls=%async_computation.2 | async-start | bytes 557056 | tf_op jit(solution)/shard_map/reduce_scatter | solution.py:60
  43.5 25.5 %copy-start = (f32[512,256]{1,0:T(8,128)S(1)}, f32[512,256]{1,0:T(8,128)}, u32[]{:S(2)}) copy-start(f32[512,256]{1,0:T(8,128)} %param.10) | copy-start | bytes 1572868
  46.4 54.2 %copy-start.2 = (f32[32,256]{1,0:T(8,128)S(1)}, f32[32,256]{1,0:T(8,128)}, u32[]{:S(2)}) copy-start(f32[32,256]{1,0:T(8,128)} %param.9) | copy-start | bytes 98308
  46.4 106.9 %all-reduce.5.cloned.1.call-start = ((), (), s32[]{:S(2)}) async-start(), calls=%async_computation.5 | async-start | bytes 1048576 | tf_op jit(solution)/shard_map/psum | solution.py:62
  127.2 57.1 %reduce-scatter.5.cloned.1.call-start = ((), (), s32[]{:S(2)}) async-start(), calls=%async_computation.4 | async-start | bytes 557056 | tf_op jit(solution)/shard_map/reduce_scatter | solution.py:60
  128.0 25.3 %copy-start.1 = (f32[512,256]{1,0:T(8,128)S(1)}, f32[512,256]{1,0:T(8,128)}, u32[]{:S(2)}) copy-start(f32[512,256]{1,0:T(8,128)} %all-reduce.3.cloned.1.call-done) | copy-start | bytes 1572868
  130.0 54.4 %copy-start.3 = (f32[32,256]{1,0:T(8,128)S(1)}, f32[32,256]{1,0:T(8,128)}, u32[]{:S(2)}) copy-start(f32[32,256]{1,0:T(8,128)} %reduce-scatter.3.cloned.1.call-done) | copy-start | bytes 98308
Sparse Core Ops, SparseCore 0:
  43.0 25.9 all-reduce.2
  127.4 25.8 all-reduce.4
Sparse Core Ops, SparseCore 1:
  47.5 53.1 reduce-scatter.2
  131.3 53.1 reduce-scatter.4
where the time goes:
time: 194 us; the launch traced here: 193 us
  waiting for transfers between devices  104 us (54%)
  blocking collectives  43.9 us (23%)
  between operations  16.3 us (8%)
  matrix products  13.4 us (7%)
  other arithmetic  9.04 us (5%)
  local copies, waits for them, and re-layouts  6.25 us (3%)
    reduce_scatter x2, waiting for transfers between devices, shards(): lax.psum_scatter(grad_doc, 'col', scatter_dimension=0, tiled=True)  59.1 us
    psum x2, waiting for transfers between devices, shards(): summed = lax.psum(grad_ngram, 'grp')  44.9 us
    all_gather x2, blocking collectives, shards(): lax.all_gather(doc_now.astype(jnp.bfloat16), 'col', axis=0, tiled=True)  43.9 us
    dot_general x2, matrix products, local_grads(): jnp.einsum('kn,kjr->njr', ngram_onehot, ngram_terms, precision=highest)  3.94 us
    dot_general x2, matrix products, local_grads(): jnp.einsum('kd,kir->dir', doc_onehot, doc_terms, precision=highest)  3.94 us
  transfers between devices with their start and end apart: 4, of which 4 were waited for; matrix products, arithmetic and copies ran while one was open for 5% of the time, Pallas kernels for 0%

commit v1 on v0

v1 whole, which is shorter than its diff:
```python
import functools
import math

import jax
import jax.numpy as jnp
from jax import lax
from jax.experimental import pallas as pl
from jax.experimental.pallas import tpu as pltpu
from jax.sharding import PartitionSpec as P

R = 256
BLK = 128
BF = jnp.bfloat16
F32 = jnp.float32
VMEM = pl.BlockSpec(memory_space=pltpu.VMEM)
SMEM = pl.BlockSpec(memory_space=pltpu.SMEM)


def dot(a, b, dims):
    return lax.dot_general(a, b, (dims, ((), ())), preferred_element_type=F32)


def tile_errors(chunk, place, docs, ngrams, counts, pmi, weights, s, e):
    count = counts[0, 0]
    for k in range(pmi.shape[2]):
        d = docs[0, 0, k]
        lanes = pl.ds(pl.multiple_of(ngrams[0, 0, k] * BLK, BLK), BLK)
        live = (k < count).astype(F32)
        for i in range(BLK // chunk):
            at, row = place(d, i)
            at = pl.ds(pl.multiple_of(at, chunk), chunk)
            row = pl.ds(pl.multiple_of(row, chunk), chunk)
            p = pmi[0, 0, k, row, :].astype(F32)
            w = weights[0, 0, k, row, :].astype(F32)
            e[at, lanes] = (live * w * (s[at, lanes] - p)).astype(BF)


def relative_place(me, chunk):
    low = me & 3
    z = me >> 2

    def place(d, i):
        c, x = i & 1, i >> 1
        return ((c * 2 + x) * 4 + (d ^ z)) * chunk, ((x * 2 + c) ^ low) * chunk

    return place


def first_kernel(docs, ngrams, counts, pmi, weights, quarter, other, half, v, keep, send, gv, s, e, u, v16):
    n = quarter.shape[0]
    u[:n, :] = quarter[...]
    u[n : 2 * n, :] = other[...]
    u[2 * n :, :] = half[...]
    v16[...] = v[...].astype(BF)
    gradients(docs, ngrams, counts, pmi, weights, keep, send, gv, s, e, u, v16)


def second_kernel(
    rate, docs, ngrams, counts, pmi, weights, quarter, other, half, v, gv_own, gv_other,
    keep, send, gv, v_out, s, e, u, v16,
):
    n = quarter.shape[0]
    u[:n, :] = quarter[...]
    u[n : 2 * n, :] = other[...]
    u[2 * n :, :] = half[...]
    now = v[...] - rate * (gv_own[...].astype(F32) + gv_other[...].astype(F32))
    v_out[...] = now
    v16[...] = now.astype(BF)
    gradients(docs, ngrams, counts, pmi, weights, keep, send, gv, s, e, u, v16)


def gradients(docs, ngrams, counts, pmi, weights, keep, send, gv, s, e, u, v16):
    n = keep.shape[0]
    chunk = 2 * n // 16
    s[...] = dot(u[...], v16[...], ((1,), (1,)))
    place = relative_place(lax.axis_index("col"), chunk)
    tile_errors(chunk, place, docs, ngrams, counts, pmi, weights, s, e)
    gu = dot(e[...], v16[...], ((1,), (0,)))
    keep[...] = gu[:n, :]
    send[...] = gu[n:, :].astype(BF)
    gv[...] = dot(e[...], u[...], ((0,), (0,))).astype(BF)


def step_call(kernel, rows, ngram_rows, extra_out, arrays):
    return pl.pallas_call(
        kernel,
        out_shape=[
            jax.ShapeDtypeStruct((rows // 2, R), F32),
            jax.ShapeDtypeStruct((rows // 2, R), BF),
            jax.ShapeDtypeStruct((ngram_rows, R), BF),
        ]
        + extra_out,
        in_specs=[SMEM] * 3 + [VMEM] * (len(arrays) - 3),
        out_specs=[VMEM] * (3 + len(extra_out)),
        scratch_shapes=[
            pltpu.VMEM((rows, ngram_rows), F32),
            pltpu.VMEM((rows, ngram_rows), BF),
            pltpu.VMEM((rows, R), BF),
            pltpu.VMEM((ngram_rows, R), BF),
        ],
        compiler_params=pltpu.CompilerParams(vmem_limit_bytes=24 * 1024 * 1024),
        cost_estimate=pl.CostEstimate(
            flops=6 * rows * ngram_rows * R, bytes_accessed=4 * rows * ngram_rows, transcendentals=0
        ),
    )(*arrays)


def swap(x, bit):
    return lax.ppermute(x, "col", [(i, i ^ bit) for i in range(lax.axis_size("col"))])


def swap_group(x):
    return lax.ppermute(x, "grp", [(0, 1), (1, 0)])


def spread(quarter):
    other = swap(quarter, 2)
    half = swap(jnp.concatenate([quarter, other], 0), 1)
    return other, half


def gather_quarter(own):
    far = {j: swap(own, 4 * j) for j in (3, 2, 1)}
    return jnp.concatenate([own] + [far[j] for j in (1, 2, 3)], 0)


def quarter_sum(keep, send):
    n = keep.shape[0] // 2
    got = swap(send, 1).astype(F32)
    got_x = swap((keep[n:] + got[n:]).astype(BF), 2).astype(F32)
    return keep[:n] + got[:n] + got_x


def small_slice(doc_now, ngram_now, block_docs, block_ngrams, block_counts, pmi, weights, rates):
    doc_rate, ngram_rate = rates
    own = doc_now.shape[0]
    rows = own * 16
    ngram_rows = ngram_now.shape[0]
    slots = (block_docs, block_ngrams, block_counts, pmi, weights)

    quarter = gather_quarter(doc_now.astype(BF))
    other, half = spread(quarter)
    keep, send, gv = step_call(
        first_kernel, rows, ngram_rows, [], (*slots, quarter, other, half, ngram_now)
    )
    gv_other = swap_group(gv)
    part = quarter_sum(keep, send)
    part16 = part.astype(BF)
    far = {j: swap(part16, 4 * j) for j in (3, 2, 1)}
    sums = []
    for z in range(4):
        total = part[z * own : (z + 1) * own]
        for j in (1, 2, 3):
            k = z ^ j
            total = total + far[j][k * own : (k + 1) * own].astype(F32)
        sums.append(total)
    doc_now = doc_now - doc_rate * sums[0]
    quarter = jnp.concatenate(
        [doc_now.astype(BF)]
        + [
            (quarter[z * own : (z + 1) * own].astype(F32) - doc_rate * sums[z]).astype(BF)
            for z in (1, 2, 3)
        ],
        0,
    )
    other, half = spread(quarter)
    keep, send, gv, ngram_now = step_call(
        functools.partial(second_kernel, ngram_rate),
        rows,
        ngram_rows,
        [jax.ShapeDtypeStruct((ngram_rows, R), F32)],
        (*slots, quarter, other, half, ngram_now, gv, gv_other),
    )
    gv_other = swap_group(gv)
    part = quarter_sum(keep, send)
    total = part[:own]
    for j in (3, 2, 1):
        total = total + swap(part[j * own : (j + 1) * own].astype(BF), 4 * j).astype(F32)
    doc_now = doc_now - doc_rate * total
    ngram_now = ngram_now - ngram_rate * (gv.astype(F32) + gv_other.astype(F32))
    return doc_now, ngram_now


def plain_kernel(docs, ngrams, counts, pmi, weights, u, v, gu, gv, s, e):
    v16 = v[...].astype(BF)
    s[...] = dot(u[...], v16, ((1,), (1,)))
    tile_errors(
        BLK, lambda d, i: (d * BLK, 0), docs, ngrams, counts, pmi, weights, s, e
    )
    gu[...] = dot(e[...], v16, ((1,), (0,)))
    gv[...] = dot(e[...], u[...], ((0,), (0,)))


def any_slice(doc_now, ngram_now, block_docs, block_ngrams, block_counts, pmi, weights, rates):
    doc_rate, ngram_rate = rates
    slots = (block_docs, block_ngrams, block_counts, pmi, weights)
    rows = doc_now.shape[0] * lax.axis_size("col")
    ngram_rows = ngram_now.shape[0]
    for step in range(2):
        u = lax.all_gather(doc_now.astype(BF), "col", axis=0, tiled=True)
        gu, gv = pl.pallas_call(
            plain_kernel,
            out_shape=[
                jax.ShapeDtypeStruct((rows, R), F32),
                jax.ShapeDtypeStruct((ngram_rows, R), F32),
            ],
            in_specs=[SMEM] * 3 + [VMEM] * 4,
            out_specs=[VMEM] * 2,
            scratch_shapes=[
                pltpu.VMEM((rows, ngram_rows), F32),
                pltpu.VMEM((rows, ngram_rows), BF),
            ],
            compiler_params=pltpu.CompilerParams(vmem_limit_bytes=24 * 1024 * 1024),
        )(*slots, u, ngram_now)
        doc_now = doc_now - doc_rate * lax.psum_scatter(gu, "col", scatter_dimension=0, tiled=True)
        ngram_now = ngram_now - ngram_rate * lax.psum(gv, "grp")
    return doc_now, ngram_now


def shards(doc_factors, ngram_factors, block_docs, block_ngrams, block_counts, pmi, weights):
    shard_count = lax.axis_size("col")
    group_count = lax.axis_size("grp")
    doc_total = doc_factors.shape[0] * shard_count * group_count
    ngram_total = ngram_factors.shape[0] * shard_count
    width = doc_factors.shape[1]
    doc_base = math.sqrt(ngram_total) + 1.5 * math.sqrt(width)
    ngram_base = math.sqrt(doc_total) + 1.5 * math.sqrt(width)
    rates = (100.0 / (doc_base * doc_base), 100.0 / (ngram_base * ngram_base))
    run = small_slice if (group_count, shard_count) == (2, 16) else any_slice
    return run(
        doc_factors, ngram_factors, block_docs, block_ngrams, block_counts, pmi, weights, rates
    )


def solution(mesh):
    return jax.shard_map(
        shards,
        mesh=mesh,
        in_specs=(
            P(("grp", "col"), None),
            P("col", None),
            P("grp", "col", None),
            P("grp", "col", None),
            P("grp", "col"),
            P("grp", "col", None, None, None),
            P("grp", "col", None, None, None),
        ),
        out_specs=(P(("grp", "col"), None), P("col", None)),
        check_vma=False,
    )
```

time: 194 us -> 60.6 us (0.31)
  waiting for transfers between devices: 104 us -> 26.9 us
  blocking collectives: 43.9 us -> 0 us
  starting transfers between devices: 0.35 us -> 23.2 us
  between operations: 16.3 us -> 1.44 us
  matrix products: 13.4 us -> 0 us
  other arithmetic: 9.04 us -> 2.49 us
  Pallas kernels: 0 us -> 3.13 us
  local copies, waits for them, and re-layouts: 6.25 us -> 3.17 us
    reduce_scatter x2 -> x0, waiting for transfers between devices: 59.1 us -> none  [shards(): lax.psum_scatter(grad_doc, 'col', scatter_dimension=0, tiled=True)]
    psum x2 -> x0, waiting for transfers between devices: 44.9 us -> none  [shards(): summed = lax.psum(grad_ngram, 'grp')]
    all_gather x2 -> x0, blocking collectives: 43.9 us -> none  [shards(): lax.all_gather(doc_now.astype(jnp.bfloat16), 'col', axis=0, tiled=True)]
    ppermute x0 -> x19, waiting for transfers between devices: none -> 26.9 us  [the longest x17 22.6 us: swap(): lax.ppermute(x, 'col', [(i, i ^ bit) for i in range(lax.axis_size('col'))])]
    ppermute x0 -> x19, starting transfers between devices: none -> 23.2 us  [the longest x17 20.1 us: swap(): lax.ppermute(x, 'col', [(i, i ^ bit) for i in range(lax.axis_size('col'))])]
    dot_general x10 -> x0, matrix products: 13.4 us -> none  [the longest x2 3.94 us: local_grads(): jnp.einsum('kn,kjr->njr', ngram_onehot, ngram_terms, precision=highest)]
    convert_element_type x5, other arithmetic: 3.71 us -> 0.1 us  [the longest x2 0.04 us: quarter_sum(): got = swap(send, 1).astype(F32)]
    dot_general x4 -> x0, local copies, waits for them, and re-layouts: 3.57 us -> none  [the longest x2 1.8 us: local_grads(): jnp.einsum('kd,kir->dir', doc_onehot, doc_terms, precision=highest)]
  transfers between devices with their start and end apart: 4 -> 19, of which waited for: 4 -> 15; matrix products, arithmetic and copies ran while one was open for 5% -> 1% of each run, Pallas kernels for 0% -> 0%
where the time goes in v1:
time: 60.6 us; the launch traced here: 60.3 us
  waiting for transfers between devices  26.9 us (44%)
  starting transfers between devices  23.2 us (38%)
  local copies, waits for them, and re-layouts  3.17 us (5%)
  Pallas kernels  3.13 us (5%)
  other arithmetic  2.49 us (4%)
  between operations  1.44 us (2%)
    ppermute x17, waiting for transfers between devices, swap(): lax.ppermute(x, 'col', [(i, i ^ bit) for i in range(lax.axis_size('col'))])  22.6 us
    ppermute x17, starting transfers between devices, swap(): lax.ppermute(x, 'col', [(i, i ^ bit) for i in range(lax.axis_size('col'))])  20.1 us
    ppermute x2, waiting for transfers between devices, swap_group(): return lax.ppermute(x, 'grp', [(0, 1), (1, 0)])  4.27 us
    unnamed x17, local copies, waits for them, and re-layouts  3.15 us
    pallas_call x2, Pallas kernels, step_call(): pl.pallas_call(kernel, out_shape=[jax.ShapeDtypeStruct((rows // 2, R), F3...  3.13 us
    ppermute x2, starting transfers between devices, swap_group(): return lax.ppermute(x, 'grp', [(0, 1), (1, 0)])  3.03 us
  transfers between devices with their start and end apart: 19, of which 15 were waited for; matrix products, arithmetic and copies ran while one was open for 1% of the time, Pallas kernels for 0%

profile of v1, /device:TPU:0, one launch (start us, length us, event | category | flops | bytes accessed | tf_op | source)
XLA Modules:
  0.0 60.3 jit_solution(614504150433801283)
XLA Ops:
  0.6 0.8 %constant_dynamic-update-slice_fusion.4 = (bf16[256,256]{1,0:T(8,128)(2,1)S(1)}, bf16[32,256]{1,0:T(8,128)(2,1)S(1)}) fusion(f32[32,256]{1,0:T(8,128)} %param.7), kind=kLoop, calls=%fused_computation.43 | loop fusion | flops 8191 | bytes 65536
  1.4 5.0 %collective-permute-start.2 = (bf16[32,256]{1,0:T(8,128)(2,1)S(1)}, bf16[32,256]{1,0:T(8,128)(2,1)S(1)}, u32[]{:S(2)}, u32[]{:S(2)}) collective-permute-start(bf16[32,256]{1,0:T(8,128)(2,1)S(1)} %get-tuple-element.30), channel_id=1, source_target_pairs={{0,12},{1,13},{2,14},{3,15},{4,8},{5,9},{6,10},{7,11},{8,4},{9,5},... | collective-permute-start | bytes 49160 | tf_op jit(solution)/shard_map/ppermute | solution.py:109
  6.4 0.0 collective-permute-start.1
  6.4 0.6 collective-permute-start
  7.0 1.1 %collective-permute-done.2 = bf16[32,256]{1,0:T(8,128)(2,1)S(1)} collective-permute-done((bf16[32,256]{1,0:T(8,128)(2,1)S(1)}, bf16[32,256]{1,0:T(8,128)(2,1)S(1)}, u32[]{:S(2)}, u32[]{:S(2)}) %collective-permute-start.2) | collective-permute-done | bytes 16416 | tf_op jit(solution)/shard_map/ppermute | solution.py:109
  8.2 2.9 %collective-permute-done.1 = bf16[32,256]{1,0:T(8,128)(2,1)S(1)} collective-permute-done((bf16[32,256]{1,0:T(8,128)(2,1)S(1)}, bf16[32,256]{1,0:T(8,128)(2,1)S(1)}, u32[]{:S(2)}, u32[]{:S(2)}) %collective-permute-start.1) | collective-permute-done | bytes 16416 | tf_op jit(solution)/shard_map/ppermute | solution.py:109
  11.1 0.0 collective-permute-done
  11.1 1.6 %collective-permute-start.3 = (bf16[128,256]{1,0:T(8,128)(2,1)S(1)}, bf16[128,256]{1,0:T(8,128)(2,1)S(1)}, u32[]{:S(2)}, u32[]{:S(2)}) collective-permute-start(bf16[128,256]{1,0:T(8,128)(2,1)S(1)} %pad_maximum_fusion.quarter), channel_id=1, source_target_pairs={{0,2},{1,3},{2,0},{3,1},{4,6},{5,7},{6,4},{7,5},{8,10},{9,11},{10,... | collective-permute-start | bytes 196616 | tf_op jit(solution)/shard_map/ppermute | solution.py:109
  12.7 2.8 %collective-permute-done.3.other = bf16[128,256]{1,0:T(8,128)(2,1)S(1)} collective-permute-done((bf16[128,256]{1,0:T(8,128)(2,1)S(1)}, bf16[128,256]{1,0:T(8,128)(2,1)S(1)}, u32[]{:S(2)}, u32[]{:S(2)}) %collective-permute-start.3) | collective-permute-done | bytes 65568 | tf_op jit(solution)/shard_map/ppermute | solution.py:109
  15.4 0.0 copy-start.5
  15.4 0.1 collective-permute-start.4
  16.2 0.7 %collective-permute-done.4.half = bf16[256,256]{1,0:T(8,128)(2,1)S(1)} collective-permute-done((bf16[256,256]{1,0:T(8,128)(2,1)S(1)}, bf16[256,256]{1,0:T(8,128)(2,1)S(1)}, u32[]{:S(2)}, u32[]{:S(2)}) %collective-permute-start.4) | collective-permute-done | bytes 131104 | tf_op jit(solution)/shard_map/ppermute | solution.py:109
  16.9 1.0 %copy-done = bf16[1,1,16,128,128]{4,3,2,1,0:T(8,128)(2,1)S(1)} copy-done((bf16[1,1,16,128,128]{4,3,2,1,0:T(8,128)(2,1)S(1)}, bf16[1,1,16,128,128]{4,3,2,1,0:T(8,128)(2,1)}, u32[]{:S(2)}) %copy-start) | copy-done | bytes 524312
  17.9 1.0 %copy-done.1 = bf16[1,1,16,128,128]{4,3,2,1,0:T(8,128)(2,1)S(1)} copy-done((bf16[1,1,16,128,128]{4,3,2,1,0:T(8,128)(2,1)S(1)}, bf16[1,1,16,128,128]{4,3,2,1,0:T(8,128)(2,1)}, u32[]{:S(2)}) %copy-start.1) | copy-done | bytes 524312
  19.0 1.0 %copy-done.2 = f32[512,256]{1,0:T(8,128)S(1)} copy-done((f32[512,256]{1,0:T(8,128)S(1)}, f32[512,256]{1,0:T(8,128)}, u32[]{:S(2)}) %copy-start.2) | copy-done | bytes 524312
  20.0 1.6 %shard_map.86 = (f32[256,256]{1,0:T(8,128)S(1)}, bf16[256,256]{1,0:T(8,128)(2,1)S(1)}, bf16[512,256]{1,0:T(8,128)(2,1)S(1)}) custom-call(s32[1,1,16]{2,1,0:T(1,128)S(1)} %copy-done.4, s32[1,1,16]{2,1,0:T(1,128)S(1)} %copy-done.5, s32[1,1]{1,0:T(1,128)S(6)} %copy.17.counts, bf16[1,1,16,128,128]{4,3,2,1,0:T(8,128)(2,1)S(1)} %copy-done, ...), custom_call_target="tpu_custom_call" | custom-call | flops 402653184 | bytes 1048576 | tf_op jit(solution)/shard_map/pallas_call | solution.py:85
  21.6 0.2 collective-permute-start.5
  21.8 1.2 %collective-permute-done.5 = bf16[256,256]{1,0:T(8,128)(2,1)S(1)} collective-permute-done((bf16[256,256]{1,0:T(8,128)(2,1)S(1)}, bf16[256,256]{1,0:T(8,128)(2,1)S(1)}, u32[]{:S(2)}, u32[]{:S(2)}) %collective-permute-start.5) | collective-permute-done | bytes 131104 | tf_op jit(solution)/shard_map/ppermute | solution.py:109
  23.0 0.0 copy-start.6
  23.0 1.6 %collective-permute-start.6 = (bf16[128,256]{1,0:T(8,128)(2,1)S(1)}, bf16[128,256]{1,0:T(8,128)(2,1)S(1)}, u32[]{:S(2)}, u32[]{:S(2)}) collective-permute-start(bf16[128,256]{1,0:T(8,128)(2,1)S(1)} %fusion.2), channel_id=1, source_target_pairs={{0,2},{1,3},{2,0},{3,1},{4,6},{5,7},{6,4},{7,5},{8,10},{9,11},{10,... | collective-permute-start | bytes 196616 | tf_op jit(solution)/shard_map/ppermute | solution.py:109
  24.6 2.8 %collective-permute-done.6 = bf16[128,256]{1,0:T(8,128)(2,1)S(1)} collective-permute-done((bf16[128,256]{1,0:T(8,128)(2,1)S(1)}, bf16[128,256]{1,0:T(8,128)(2,1)S(1)}, u32[]{:S(2)}, u32[]{:S(2)}) %collective-permute-start.6) | collective-permute-done | bytes 65568 | tf_op jit(solution)/shard_map/ppermute | solution.py:109
  27.4 0.0 copy-start.3
  27.4 1.5 %collective-permute-start.9 = (bf16[128,256]{1,0:T(8,128)(2,1)S(1)}, bf16[128,256]{1,0:T(8,128)(2,1)S(1)}, u32[]{:S(2)}, u32[]{:S(2)}) collective-permute-start(bf16[128,256]{1,0:T(8,128)(2,1)S(1)} %get-tuple-element.27), channel_id=1, source_target_pairs={{0,12},{1,13},{2,14},{3,15},{4,8},{5,9},{6,10},{7,11},{8,4},{9,5},... | collective-permute-start | bytes 196616 | tf_op jit(solution)/shard_map/ppermute | solution.py:109
  28.9 0.6 %collective-permute-start.8 = (bf16[128,256]{1,0:T(8,128)(2,1)S(1)}, bf16[128,256]{1,0:T(8,128)(2,1)S(1)}, u32[]{:S(2)}, u32[]{:S(2)}) collective-permute-start(bf16[128,256]{1,0:T(8,128)(2,1)S(1)} %get-tuple-element.27), channel_id=1, source_target_pairs={{0,8},{1,9},{2,10},{3,11},{4,12},{5,13},{6,14},{7,15},{8,0},{9,1},... | collective-permute-start | bytes 196616 | tf_op jit(solution)/shard_map/ppermute | solution.py:109
  29.5 2.4 %collective-permute-start.7 = (bf16[128,256]{1,0:T(8,128)(2,1)S(1)}, bf16[128,256]{1,0:T(8,128)(2,1)S(1)}, u32[]{:S(2)}, u32[]{:S(2)}) collective-permute-start(bf16[128,256]{1,0:T(8,128)(2,1)S(1)} %get-tuple-element.27), channel_id=1, source_target_pairs={{0,4},{1,5},{2,6},{3,7},{4,0},{5,1},{6,2},{7,3},{8,12},{9,13},{10,... | collective-permute-start | bytes 196616 | tf_op jit(solution)/shard_map/ppermute | solution.py:109
  31.9 2.0 %collective-permute-done.9 = bf16[128,256]{1,0:T(8,128)(2,1)S(1)} collective-permute-done((bf16[128,256]{1,0:T(8,128)(2,1)S(1)}, bf16[128,256]{1,0:T(8,128)(2,1)S(1)}, u32[]{:S(2)}, u32[]{:S(2)}) %collective-permute-start.9) | collective-permute-done | bytes 65568 | tf_op jit(solution)/shard_map/ppermute | solution.py:109
  33.9 1.9 %collective-permute-done.8 = bf16[128,256]{1,0:T(8,128)(2,1)S(1)} collective-permute-done((bf16[128,256]{1,0:T(8,128)(2,1)S(1)}, bf16[128,256]{1,0:T(8,128)(2,1)S(1)}, u32[]{:S(2)}, u32[]{:S(2)}) %collective-permute-start.8) | collective-permute-done | bytes 65568 | tf_op jit(solution)/shard_map/ppermute | solution.py:109
  35.8 0.0 collective-permute-done.7
  35.9 1.6 %collective-permute-start.10 = (bf16[128,256]{1,0:T(8,128)(2,1)S(1)}, bf16[128,256]{1,0:T(8,128)(2,1)S(1)}, u32[]{:S(2)}, u32[]{:S(2)}) collective-permute-start(bf16[128,256]{1,0:T(8,128)(2,1)S(1)} %pad_maximum_fusion.1.quarter), channel_id=1, source_target_pairs={{0,2},{1,3},{2,0},{3,1},{4,6},{5,7},{6,4},{7,5},{8,10},{9,11},{10,... | collective-permute-start | bytes 196616 | tf_op jit(solution)/shard_map/ppermute | solution.py:109
  37.4 1.5 %collective-permute-start.12 = (bf16[512,256]{1,0:T(8,128)(2,1)S(1)}, bf16[512,256]{1,0:T(8,128)(2,1)S(1)}, u32[]{:S(2)}, u32[]{:S(2)}) collective-permute-start(bf16[512,256]{1,0:T(8,128)(2,1)S(1)} %get-tuple-element.11.gv_own), channel_id=1, source_target_pairs={{0,16},{16,0},{1,17},{17,1},{2,18},{18,2},{3,19},{19,3},{4,20},{20... | collective-permute-start | bytes 786440 | tf_op jit(solution)/shard_map/ppermute | solution.py:113
  39.0 1.3 %collective-permute-done.10.other = bf16[128,256]{1,0:T(8,128)(2,1)S(1)} collective-permute-done((bf16[128,256]{1,0:T(8,128)(2,1)S(1)}, bf16[128,256]{1,0:T(8,128)(2,1)S(1)}, u32[]{:S(2)}, u32[]{:S(2)}) %collective-permute-start.10) | collective-permute-done | bytes 65568 | tf_op jit(solution)/shard_map/ppermute | solution.py:109
  40.2 0.0 collective-permute-start.11
  40.2 4.3 %collective-permute-done.12.gv_other = bf16[512,256]{1,0:T(8,128)(2,1)S(1)} collective-permute-done((bf16[512,256]{1,0:T(8,128)(2,1)S(1)}, bf16[512,256]{1,0:T(8,128)(2,1)S(1)}, u32[]{:S(2)}, u32[]{:S(2)}) %collective-permute-start.12) | collective-permute-done | bytes 262176 | tf_op jit(solution)/shard_map/ppermute | solution.py:113
  44.5 0.0 collective-permute-done.11.half
  44.5 1.6 %shard_map.87 = (f32[256,256]{1,0:T(8,128)S(1)}, bf16[256,256]{1,0:T(8,128)(2,1)S(1)}, bf16[512,256]{1,0:T(8,128)(2,1)S(1)}, f32[512,256]{1,0:T(8,128)S(1)}) custom-call(s32[1,1,16]{2,1,0:T(1,128)S(1)} %copy-done.4, s32[1,1,16]{2,1,0:T(1,128)S(1)} %copy-done.5, s32[1,1]{1,0:T(1,128)S(6)} %copy.17.counts, bf16[1,1,16,128,128]{4,3,2,1,0:T(8,128)(2,1)S(1)} %copy-done, ...), custom_call_target="tpu_custom_call" | custom-call | flops 402653184 | bytes 1048576 | tf_op jit(solution)/shard_map/pallas_call | solution.py:85
  46.1 0.1 collective-permute-start.13
  46.2 1.3 %collective-permute-done.13 = bf16[256,256]{1,0:T(8,128)(2,1)S(1)} collective-permute-done((bf16[256,256]{1,0:T(8,128)(2,1)S(1)}, bf16[256,256]{1,0:T(8,128)(2,1)S(1)}, u32[]{:S(2)}, u32[]{:S(2)}) %collective-permute-start.13) | collective-permute-done | bytes 131104 | tf_op jit(solution)/shard_map/ppermute | solution.py:109
  47.5 0.6 collective-permute-start.14
  48.1 1.5 %collective-permute-start.18 = (bf16[512,256]{1,0:T(8,128)(2,1)S(1)}, bf16[512,256]{1,0:T(8,128)(2,1)S(1)}, u32[]{:S(2)}, u32[]{:S(2)}) collective-permute-start(bf16[512,256]{1,0:T(8,128)(2,1)S(1)} %get-tuple-element.15), channel_id=1, source_target_pairs={{0,16},{16,0},{1,17},{17,1},{2,18},{18,2},{3,19},{19,3},{4,20},{20... | collective-permute-start | bytes 786440 | tf_op jit(solution)/shard_map/ppermute | solution.py:113
  49.7 2.2 %collective-permute-done.14 = bf16[128,256]{1,0:T(8,128)(2,1)S(1)} collective-permute-done((bf16[128,256]{1,0:T(8,128)(2,1)S(1)}, bf16[128,256]{1,0:T(8,128)(2,1)S(1)}, u32[]{:S(2)}, u32[]{:S(2)}) %collective-permute-start.14) | collective-permute-done | bytes 65568 | tf_op jit(solution)/shard_map/ppermute | solution.py:109
  51.9 2.2 %collective-permute-start.15 = (bf16[32,256]{1,0:T(8,128)(2,1)S(1)}, bf16[32,256]{1,0:T(8,128)(2,1)S(1)}, u32[]{:S(2)}, u32[]{:S(2)}) collective-permute-start(bf16[32,256]{1,0:T(8,128)(2,1)S(1)} %get-tuple-element.31), channel_id=1, source_target_pairs={{0,12},{1,13},{2,14},{3,15},{4,8},{5,9},{6,10},{7,11},{8,4},{9,5},... | collective-permute-start | bytes 49160 | tf_op jit(solution)/shard_map/ppermute | solution.py:109
  54.1 0.0 collective-permute-start.17
  54.1 2.3 %collective-permute-start.16 = (bf16[32,256]{1,0:T(8,128)(2,1)S(1)}, bf16[32,256]{1,0:T(8,128)(2,1)S(1)}, u32[]{:S(2)}, u32[]{:S(2)}) collective-permute-start(bf16[32,256]{1,0:T(8,128)(2,1)S(1)} %get-tuple-element.33), channel_id=1, source_target_pairs={{0,8},{1,9},{2,10},{3,11},{4,12},{5,13},{6,14},{7,15},{8,0},{9,1},... | collective-permute-start | bytes 49160 | tf_op jit(solution)/shard_map/ppermute | solution.py:109
  56.4 1.2 %collective-permute-done.15 = bf16[32,256]{1,0:T(8,128)(2,1)S(1)} collective-permute-done((bf16[32,256]{1,0:T(8,128)(2,1)S(1)}, bf16[32,256]{1,0:T(8,128)(2,1)S(1)}, u32[]{:S(2)}, u32[]{:S(2)}) %collective-permute-start.15) | collective-permute-done | bytes 16416 | tf_op jit(solution)/shard_map/ppermute | solution.py:109
  57.6 0.3 collective-permute-done.17
  57.8 0.9 %collective-permute-done.16 = bf16[32,256]{1,0:T(8,128)(2,1)S(1)} collective-permute-done((bf16[32,256]{1,0:T(8,128)(2,1)S(1)}, bf16[32,256]{1,0:T(8,128)(2,1)S(1)}, u32[]{:S(2)}, u32[]{:S(2)}) %collective-permute-start.16) | collective-permute-done | bytes 16416 | tf_op jit(solution)/shard_map/ppermute | solution.py:109
  58.7 0.6 %fusion.7 = f32[32,256]{1,0:T(8,128)} fusion(f32[32,256]{1,0:T(8,128)S(1)} %get-tuple-element.26, f32[128,256]{1,0:T(8,128)S(1)} %get-tuple-element.17, bf16[32,256]{1,0:T(8,128)(2,1)S(1)} %collective-permute-done.17, bf16[32,256]{1,0:T(8,128)(2,1)S(1)} %collective-permute-done.16, bf16[32,256]{1,0:T(8,128)(2,1)S(1)} %collective-permute-done.15), kind=kLoop, calls=%fused_computation.15 | loop fusion | flops 65536 | bytes 147456 | tf_op jit(solution)/shard_map/sub | solution.py:179
  59.4 0.9 %multiply_subtract_fusion = f32[512,256]{1,0:T(8,128)} fusion(f32[512,256]{1,0:T(8,128)S(1)} %get-tuple-element.14, bf16[512,256]{1,0:T(8,128)(2,1)S(1)} %collective-permute-done.18, bf16[512,256]{1,0:T(8,128)(2,1)S(1)} %get-tuple-element.15), kind=kLoop, calls=%fused_computation | loop fusion | flops 655360 | bytes 1572864 | tf_op jit(solution)/shard_map/sub | solution.py:180
  (27 shorter events, 0.2 us)
Async XLA Ops:
  1.4 6.8 %collective-permute-start.2 = (bf16[32,256]{1,0:T(8,128)(2,1)S(1)}, bf16[32,256]{1,0:T(8,128)(2,1)S(1)}, u32[]{:S(2)}, u32[]{:S(2)}) collective-permute-start(bf16[32,256]{1,0:T(8,128)(2,1)S(1)} %get-tuple-element.30), channel_id=1, source_target_pairs={{0,12},{1,13},{2,14},{3,15},{4,8},{5,9},{6,10},{7,11},{8,4},{9,5},... | collective-permute-start | bytes 49160 | tf_op jit(solution)/shard_map/ppermute | solution.py:109
  6.4 4.6 %collective-permute-start.1 = (bf16[32,256]{1,0:T(8,128)(2,1)S(1)}, bf16[32,256]{1,0:T(8,128)(2,1)S(1)}, u32[]{:S(2)}, u32[]{:S(2)}) collective-permute-start(bf16[32,256]{1,0:T(8,128)(2,1)S(1)} %get-tuple-element.30), channel_id=1, source_target_pairs={{0,8},{1,9},{2,10},{3,11},{4,12},{5,13},{6,14},{7,15},{8,0},{9,1},... | collective-permute-start | bytes 49160 | tf_op jit(solution)/shard_map/ppermute | solution.py:109
  6.4 4.6 %collective-permute-start = (bf16[32,256]{1,0:T(8,128)(2,1)S(1)}, bf16[32,256]{1,0:T(8,128)(2,1)S(1)}, u32[]{:S(2)}, u32[]{:S(2)}) collective-permute-start(bf16[32,256]{1,0:T(8,128)(2,1)S(1)} %get-tuple-element.30), channel_id=1, source_target_pairs={{0,4},{1,5},{2,6},{3,7},{4,0},{5,1},{6,2},{7,3},{8,12},{9,13},{10,... | collective-permute-start | bytes 49160 | tf_op jit(solution)/shard_map/ppermute | solution.py:109
  11.1 4.3 %collective-permute-start.3 = (bf16[128,256]{1,0:T(8,128)(2,1)S(1)}, bf16[128,256]{1,0:T(8,128)(2,1)S(1)}, u32[]{:S(2)}, u32[]{:S(2)}) collective-permute-start(bf16[128,256]{1,0:T(8,128)(2,1)S(1)} %pad_maximum_fusion.quarter), channel_id=1, source_target_pairs={{0,2},{1,3},{2,0},{3,1},{4,6},{5,7},{6,4},{7,5},{8,10},{9,11},{10,... | collective-permute-start | bytes 196616 | tf_op jit(solution)/shard_map/ppermute | solution.py:109
  15.4 1.4 %copy-start.4 = (s32[1,1,16]{2,1,0:T(1,128)S(1)}, s32[1,1,16]{2,1,0:T(1,128)}, u32[]{:S(2)}) copy-start(s32[1,1,16]{2,1,0:T(1,128)} %docs.3) | copy-start | bytes 196
  15.4 1.4 %copy-start.5 = (s32[1,1,16]{2,1,0:T(1,128)S(1)}, s32[1,1,16]{2,1,0:T(1,128)}, u32[]{:S(2)}) copy-start(s32[1,1,16]{2,1,0:T(1,128)} %ngrams.3) | copy-start | bytes 196
  15.4 1.4 %collective-permute-start.4 = (bf16[256,256]{1,0:T(8,128)(2,1)S(1)}, bf16[256,256]{1,0:T(8,128)(2,1)S(1)}, u32[]{:S(2)}, u32[]{:S(2)}) collective-permute-start(bf16[256,256]{1,0:T(8,128)(2,1)S(1)} %constant_dynamic-update-slice_fusion), channel_id=1, source_target_pairs={{0,1},{1,0},{2,3},{3,2},{4,5},{5,4},{6,7},{7,6},{8,9},{9,8},{10,11... | collective-permute-start | bytes 393224 | tf_op jit(solution)/shard_map/ppermute | solution.py:109
  16.9 1.0 %copy-start = (bf16[1,1,16,128,128]{4,3,2,1,0:T(8,128)(2,1)S(1)}, bf16[1,1,16,128,128]{4,3,2,1,0:T(8,128)(2,1)}, u32[]{:S(2)}) copy-start(bf16[1,1,16,128,128]{4,3,2,1,0:T(8,128)(2,1)} %pmi.3) | copy-start | bytes 1572868
  17.9 1.0 %copy-start.1 = (bf16[1,1,16,128,128]{4,3,2,1,0:T(8,128)(2,1)S(1)}, bf16[1,1,16,128,128]{4,3,2,1,0:T(8,128)(2,1)}, u32[]{:S(2)}) copy-start(bf16[1,1,16,128,128]{4,3,2,1,0:T(8,128)(2,1)} %weights.3) | copy-start | bytes 1572868
  19.0 1.0 %copy-start.2 = (f32[512,256]{1,0:T(8,128)S(1)}, f32[512,256]{1,0:T(8,128)}, u32[]{:S(2)}) copy-start(f32[512,256]{1,0:T(8,128)} %v.3) | copy-start | bytes 1572868
  21.6 1.4 %collective-permute-start.5 = (bf16[256,256]{1,0:T(8,128)(2,1)S(1)}, bf16[256,256]{1,0:T(8,128)(2,1)S(1)}, u32[]{:S(2)}, u32[]{:S(2)}) collective-permute-start(bf16[256,256]{1,0:T(8,128)(2,1)S(1)} %get-tuple-element.10), channel_id=1, source_target_pairs={{0,1},{1,0},{2,3},{3,2},{4,5},{5,4},{6,7},{7,6},{8,9},{9,8},{10,11... | collective-permute-start | bytes 393224 | tf_op jit(solution)/shard_map/ppermute | solution.py:109
  23.0 12.8 %copy-start.6 = (f32[32,256]{1,0:T(8,128)S(1)}, f32[32,256]{1,0:T(8,128)}, u32[]{:S(2)}) copy-start(f32[32,256]{1,0:T(8,128)} %param.7) | copy-start | bytes 98308
  23.0 4.3 %collective-permute-start.6 = (bf16[128,256]{1,0:T(8,128)(2,1)S(1)}, bf16[128,256]{1,0:T(8,128)(2,1)S(1)}, u32[]{:S(2)}, u32[]{:S(2)}) collective-permute-start(bf16[128,256]{1,0:T(8,128)(2,1)S(1)} %fusion.2), channel_id=1, source_target_pairs={{0,2},{1,3},{2,0},{3,1},{4,6},{5,7},{6,4},{7,5},{8,10},{9,11},{10,... | collective-permute-start | bytes 196616 | tf_op jit(solution)/shard_map/ppermute | solution.py:109
  27.4 17.1 %copy-start.3 = (f32[512,256]{1,0:T(8,128)S(1)}, f32[512,256]{1,0:T(8,128)}, u32[]{:S(2)}) copy-start(f32[512,256]{1,0:T(8,128)} %v.3) | copy-start | bytes 1572868
  27.4 6.5 %collective-permute-start.9 = (bf16[128,256]{1,0:T(8,128)(2,1)S(1)}, bf16[128,256]{1,0:T(8,128)(2,1)S(1)}, u32[]{:S(2)}, u32[]{:S(2)}) collective-permute-start(bf16[128,256]{1,0:T(8,128)(2,1)S(1)} %get-tuple-element.27), channel_id=1, source_target_pairs={{0,12},{1,13},{2,14},{3,15},{4,8},{5,9},{6,10},{7,11},{8,4},{9,5},... | collective-permute-start | bytes 196616 | tf_op jit(solution)/shard_map/ppermute | solution.py:109
  28.9 6.9 %collective-permute-start.8 = (bf16[128,256]{1,0:T(8,128)(2,1)S(1)}, bf16[128,256]{1,0:T(8,128)(2,1)S(1)}, u32[]{:S(2)}, u32[]{:S(2)}) collective-permute-start(bf16[128,256]{1,0:T(8,128)(2,1)S(1)} %get-tuple-element.27), channel_id=1, source_target_pairs={{0,8},{1,9},{2,10},{3,11},{4,12},{5,13},{6,14},{7,15},{8,0},{9,1},... | collective-permute-start | bytes 196616 | tf_op jit(solution)/shard_map/ppermute | solution.py:109
  29.5 6.3 %collective-permute-start.7 = (bf16[128,256]{1,0:T(8,128)(2,1)S(1)}, bf16[128,256]{1,0:T(8,128)(2,1)S(1)}, u32[]{:S(2)}, u32[]{:S(2)}) collective-permute-start(bf16[128,256]{1,0:T(8,128)(2,1)S(1)} %get-tuple-element.27), channel_id=1, source_target_pairs={{0,4},{1,5},{2,6},{3,7},{4,0},{5,1},{6,2},{7,3},{8,12},{9,13},{10,... | collective-permute-start | bytes 196616 | tf_op jit(solution)/shard_map/ppermute | solution.py:109
  35.9 4.3 %collective-permute-start.10 = (bf16[128,256]{1,0:T(8,128)(2,1)S(1)}, bf16[128,256]{1,0:T(8,128)(2,1)S(1)}, u32[]{:S(2)}, u32[]{:S(2)}) collective-permute-start(bf16[128,256]{1,0:T(8,128)(2,1)S(1)} %pad_maximum_fusion.1.quarter), channel_id=1, source_target_pairs={{0,2},{1,3},{2,0},{3,1},{4,6},{5,7},{6,4},{7,5},{8,10},{9,11},{10,... | collective-permute-start | bytes 196616 | tf_op jit(solution)/shard_map/ppermute | solution.py:109
  37.4 7.0 %collective-permute-start.12 = (bf16[512,256]{1,0:T(8,128)(2,1)S(1)}, bf16[512,256]{1,0:T(8,128)(2,1)S(1)}, u32[]{:S(2)}, u32[]{:S(2)}) collective-permute-start(bf16[512,256]{1,0:T(8,128)(2,1)S(1)} %get-tuple-element.11.gv_own), channel_id=1, source_target_pairs={{0,16},{16,0},{1,17},{17,1},{2,18},{18,2},{3,19},{19,3},{4,20},{20... | collective-permute-start | bytes 786440 | tf_op jit(solution)/shard_map/ppermute | solution.py:113
  40.2 4.3 %collective-permute-start.11 = (bf16[256,256]{1,0:T(8,128)(2,1)S(1)}, bf16[256,256]{1,0:T(8,128)(2,1)S(1)}, u32[]{:S(2)}, u32[]{:S(2)}) collective-permute-start(bf16[256,256]{1,0:T(8,128)(2,1)S(1)} %constant_dynamic-update-slice_fusion.5), channel_id=1, source_target_pairs={{0,1},{1,0},{2,3},{3,2},{4,5},{5,4},{6,7},{7,6},{8,9},{9,8},{10,11... | collective-permute-start | bytes 393224 | tf_op jit(solution)/shard_map/ppermute | solution.py:109
  46.1 1.4 %collective-permute-start.13 = (bf16[256,256]{1,0:T(8,128)(2,1)S(1)}, bf16[256,256]{1,0:T(8,128)(2,1)S(1)}, u32[]{:S(2)}, u32[]{:S(2)}) collective-permute-start(bf16[256,256]{1,0:T(8,128)(2,1)S(1)} %get-tuple-element.13), channel_id=1, source_target_pairs={{0,1},{1,0},{2,3},{3,2},{4,5},{5,4},{6,7},{7,6},{8,9},{9,8},{10,11... | collective-permute-start | bytes 393224 | tf_op jit(solution)/shard_map/ppermute | solution.py:109
  47.5 4.3 %collective-permute-start.14 = (bf16[128,256]{1,0:T(8,128)(2,1)S(1)}, bf16[128,256]{1,0:T(8,128)(2,1)S(1)}, u32[]{:S(2)}, u32[]{:S(2)}) collective-permute-start(bf16[128,256]{1,0:T(8,128)(2,1)S(1)} %fusion), channel_id=1, source_target_pairs={{0,2},{1,3},{2,0},{3,1},{4,6},{5,7},{6,4},{7,5},{8,10},{9,11},{10,... | collective-permute-start | bytes 196616 | tf_op jit(solution)/shard_map/ppermute | solution.py:109
  48.1 11.2 %collective-permute-start.18 = (bf16[512,256]{1,0:T(8,128)(2,1)S(1)}, bf16[512,256]{1,0:T(8,128)(2,1)S(1)}, u32[]{:S(2)}, u32[]{:S(2)}) collective-permute-start(bf16[512,256]{1,0:T(8,128)(2,1)S(1)} %get-tuple-element.15), channel_id=1, source_target_pairs={{0,16},{16,0},{1,17},{17,1},{2,18},{18,2},{3,19},{19,3},{4,20},{20... | collective-permute-start | bytes 786440 | tf_op jit(solution)/shard_map/ppermute | solution.py:113
  51.9 5.6 %collective-permute-start.15 = (bf16[32,256]{1,0:T(8,128)(2,1)S(1)}, bf16[32,256]{1,0:T(8,128)(2,1)S(1)}, u32[]{:S(2)}, u32[]{:S(2)}) collective-permute-start(bf16[32,256]{1,0:T(8,128)(2,1)S(1)} %get-tuple-element.31), channel_id=1, source_target_pairs={{0,12},{1,13},{2,14},{3,15},{4,8},{5,9},{6,10},{7,11},{8,4},{9,5},... | collective-permute-start | bytes 49160 | tf_op jit(solution)/shard_map/ppermute | solution.py:109
  54.1 3.7 %collective-permute-start.17 = (bf16[32,256]{1,0:T(8,128)(2,1)S(1)}, bf16[32,256]{1,0:T(8,128)(2,1)S(1)}, u32[]{:S(2)}, u32[]{:S(2)}) collective-permute-start(bf16[32,256]{1,0:T(8,128)(2,1)S(1)} %get-tuple-element.32), channel_id=1, source_target_pairs={{0,4},{1,5},{2,6},{3,7},{4,0},{5,1},{6,2},{7,3},{8,12},{9,13},{10,... | collective-permute-start | bytes 49160 | tf_op jit(solution)/shard_map/ppermute | solution.py:109
  54.1 4.6 %collective-permute-start.16 = (bf16[32,256]{1,0:T(8,128)(2,1)S(1)}, bf16[32,256]{1,0:T(8,128)(2,1)S(1)}, u32[]{:S(2)}, u32[]{:S(2)}) collective-permute-start(bf16[32,256]{1,0:T(8,128)(2,1)S(1)} %get-tuple-element.33), channel_id=1, source_target_pairs={{0,8},{1,9},{2,10},{3,11},{4,12},{5,13},{6,14},{7,15},{8,0},{9,1},... | collective-permute-start | bytes 49160 | tf_op jit(solution)/shard_map/ppermute | solution.py:109

commit v2 on v0

v2 whole, which is shorter than its diff:
```python
import functools
import math

import jax
import jax.numpy as jnp
from jax import lax
from jax.experimental import pallas as pl
from jax.experimental.pallas import tpu as pltpu
from jax.sharding import PartitionSpec as P

R = 256
BLK = 128
BF = jnp.bfloat16
F32 = jnp.float32
VMEM = pl.BlockSpec(memory_space=pltpu.VMEM)
SMEM = pl.BlockSpec(memory_space=pltpu.SMEM)
HBM = pl.BlockSpec(memory_space=pltpu.HBM)
ANY = pl.BlockSpec(memory_space=pl.ANY)
MIB = 1024 * 1024
PLACE_VMEM = 53 * MIB
LONG = 10**11


def dot(a, b, dims):
    return lax.dot_general(a, b, (dims, ((), ())), preferred_element_type=F32)


def shape(rows, columns, dtype):
    return jax.ShapeDtypeStruct((rows, columns), dtype)


def call(kernel, outs, in_specs, arrays, scratch=(), flops=0, vmem=16 * MIB):
    read = sum(a.size * a.dtype.itemsize for a in arrays)
    return pl.pallas_call(
        kernel,
        out_shape=outs,
        in_specs=in_specs,
        out_specs=[VMEM] * len(outs),
        scratch_shapes=list(scratch),
        compiler_params=pltpu.CompilerParams(vmem_limit_bytes=vmem),
        cost_estimate=pl.CostEstimate(flops=flops, bytes_accessed=read, transcendentals=0),
    )(*arrays)


ALONG_X = 3
ALONG_Z = (0, 5, 9, 12)
OTHER_CORE = 1


def place_kernel(
    docs, ngrams, counts, pmi_hbm, weights_hbm, v_hbm, mine, theirs, v16, pmi, weights, v, sems, v_sem
):
    slots = pmi.shape[0]
    parts = sems.shape[1]
    v_copy = pltpu.make_async_copy(v_hbm, v, v_sem)
    v_copy.start()
    copies = []
    for a, (src, dst) in enumerate(((weights_hbm, weights), (pmi_hbm, pmi))):
        for i in range(parts):
            some = pl.ds(i * (slots // parts), slots // parts)
            copies.append(pltpu.make_async_copy(src.at[0, 0, some], dst.at[some], sems.at[a, i]))
            copies[-1].start()
    half = mine.shape[0] // 2
    v_half = v.shape[0] // 2
    v_copy.wait()
    now = v[...].astype(BF)
    v16[...] = now
    theirs[2 * half :, :R] = now[:v_half]
    theirs[2 * half :, R:] = now[v_half:]
    me = lax.axis_index("col")
    low, my_z = me & 3, me >> 2
    count = counts[0, 0]
    own = half // 8
    for k in range(slots):
        if k % (slots // parts) == 0:
            for a in range(2):
                copies[a * parts + k // (slots // parts)].wait()
        lanes = pl.ds(pl.multiple_of(ngrams[0, 0, k] * BLK, BLK), BLK)
        z = docs[0, 0, k] ^ my_z
        first = low ^ ((z ^ (z >> 1)) & 1)
        live = k < count
        for x in range(2):
            at = pl.multiple_of((x * 4 + z) * own, own)
            for h, out in enumerate((mine, theirs)):
                rows = pl.ds(pl.multiple_of((first ^ (x * 2) ^ (x ^ h)) * own, own), own)
                tile = weights[k, rows, :]
                out[pl.ds(at, own), lanes] = jnp.where(live, tile, jnp.zeros_like(tile))
                out[pl.ds(at + half, own), lanes] = pmi[k, rows, :]


def errors_and_gu(u, v_blocks, tiles, e):
    half = u.shape[0]
    gu = None
    for i, v in enumerate(v_blocks):
        width = v.shape[0]
        lanes = slice(i * width, (i + 1) * width)
        s = dot(u, v, ((1,), (1,)))
        w = tiles[:half, lanes].astype(F32)
        p = tiles[half : 2 * half, lanes].astype(F32)
        err = (w * (s - p)).astype(BF)
        e[:, lanes] = err
        term = dot(err, v, ((1,), (0,)))
        gu = term if gu is None else gu + term
    return gu


def pair_kernel(near, other, pair):
    own = near.shape[0]
    pair[:own, :] = near[...].astype(BF)
    pair[own:, :] = other[...].astype(BF)


def own_kernel(pair, far1, far2, far3, v16, mine, u, e, gu):
    own = pair.shape[0] // 2
    for x in range(2):
        for z, far in enumerate((pair, far1, far2, far3)):
            at = (x * 4 + z) * own
            u[at : at + own, :] = far[x * own : (x + 1) * own, :]
    n = v16.shape[0] // 2
    gu[...] = errors_and_gu(u[...], [v16[:n], v16[n:]], mine, e)


def theirs_kernel(u, gu_own, theirs, *rest):
    *v16_theirs, keep, send1, send2, send3, e = rest
    half = u.shape[0]
    own = half // 8
    if v16_theirs:
        (v16,) = v16_theirs
        n = v16.shape[0] // 2
        v_blocks = [v16[:n], v16[n:]]
    else:
        v_blocks = [theirs[2 * half :, :R], theirs[2 * half :, R:]]
    gu = gu_own[...] + errors_and_gu(u[...], v_blocks, theirs, e)
    for z, out in enumerate((keep, send1, send2, send3)):
        for x in range(2):
            at = (x * 4 + z) * own
            out[x * own : (x + 1) * own, :] = gu[at : at + own].astype(out.dtype)


def along_z_kernel(keep, got1, got2, got3, total, total16):
    now = keep[...] + got1[...].astype(F32) + got2[...].astype(F32) + got3[...].astype(F32)
    total[...] = now
    total16[...] = now.astype(BF)


def pair_update_kernel(rate, doc, pair, total, got, doc_out, pair_out):
    own = doc.shape[0]
    now = doc[...] - rate * (total[:own, :] + got[own:, :].astype(F32))
    doc_out[...] = now
    pair_out[:own, :] = now.astype(BF)
    now = pair[own:, :].astype(F32) - rate * (total[own:, :] + got[:own, :].astype(F32))
    pair_out[own:, :] = now.astype(BF)


def ngram_update_kernel(rate, ours, got, v, after, v_out, v16):
    now = v[...] - rate * (ours[...].astype(F32) + got[...].astype(F32))
    v_out[...] = now
    v16[...] = now.astype(BF)


def ngram_kernel(e, e_theirs, u, keep, send):
    send[...] = dot(e_theirs[...], u[...], ((0,), (0,))).astype(BF)
    keep[...] = dot(e[...], u[...], ((0,), (0,)))


def swap(x, mask):
    return lax.ppermute(x, "col", [(i, i ^ mask) for i in range(lax.axis_size("col"))])


def along_z(blocks):
    got = [swap(blocks[j - 1], ALONG_Z[j]) for j in (3, 2, 1)]
    return got[::-1]


def swap_group(x):
    return lax.ppermute(x, "grp", [(0, 1), (1, 0)])


def small_slice(doc_now, ngram_now, block_docs, block_ngrams, block_counts, pmi, weights, rates):
    doc_rate, ngram_rate = rates
    own = doc_now.shape[0]
    half = 8 * own
    n = ngram_now.shape[0]
    slots = pmi.shape[2]
    flops = 2 * 2 * half * 2 * n * R
    ngram_grads = [shape(n, R, F32), shape(n, R, BF)]

    other = swap(doc_now, ALONG_X)
    mine, theirs, v16 = call(
        place_kernel,
        [shape(2 * half, n, BF), shape(3 * half, n, BF), shape(n, R, BF)],
        [SMEM] * 3 + [HBM] * 3,
        (block_docs, block_ngrams, block_counts, pmi, weights, ngram_now),
        [
            pltpu.VMEM((slots, BLK, BLK), BF),
            pltpu.VMEM((slots, BLK, BLK), BF),
            pltpu.VMEM((n, R), F32),
            pltpu.SemaphoreType.DMA((2, 4)),
            pltpu.SemaphoreType.DMA,
        ],
        vmem=PLACE_VMEM,
    )
    theirs, other = lax.optimization_barrier((theirs, other))
    (pair,) = call(pair_kernel, [shape(2 * own, R, BF)], [VMEM] * 2, (doc_now, other))
    far = along_z([pair] * 3)
    theirs = swap(theirs, OTHER_CORE)
    def gradients(pair, far, v16, *v16_theirs):
        u, e, gu = call(
            own_kernel,
            [shape(half, R, BF), shape(half, n, BF), shape(half, R, F32)],
            [VMEM] * 6,
            (pair, *far, v16, mine),
            flops=LONG,
        )
        keep, *send, e_theirs = call(
            theirs_kernel,
            [shape(2 * own, R, F32)] + [shape(2 * own, R, BF)] * 3 + [shape(half, n, BF)],
            [VMEM] * (3 + len(v16_theirs)),
            (u, gu, theirs, *v16_theirs),
            flops=flops // 2,
        )
        got = along_z(send)
        gv_keep, gv_send = call(
            ngram_kernel, ngram_grads, [VMEM] * 3, (e, e_theirs, u), flops=flops // 2
        )
        ours = (gv_keep + swap(gv_send, OTHER_CORE).astype(F32)).astype(BF)
        return keep, got, ours, swap_group(ours)

    keep, got, ours, ngram_got = gradients(pair, far, v16)
    total, total16 = call(
        along_z_kernel,
        [shape(2 * own, R, F32), shape(2 * own, R, BF)],
        [VMEM] * 4,
        (keep, *got),
        flops=LONG,
    )
    doc_now, pair = call(
        functools.partial(pair_update_kernel, doc_rate),
        [shape(own, R, F32), shape(2 * own, R, BF)],
        [VMEM] * 4,
        (doc_now, pair, total, swap(total16, ALONG_X)),
        flops=LONG,
    )
    far = along_z([pair] * 3)
    ngram_now, v16 = call(
        functools.partial(ngram_update_kernel, ngram_rate),
        [shape(n, R, F32), shape(n, R, BF)],
        [VMEM] * 3 + [ANY],
        (ours, ngram_got, ngram_now, pair),
    )
    v16_theirs = swap(v16, OTHER_CORE)

    keep, got, ours, ngram_got = gradients(pair, far, v16, v16_theirs)
    for some in got:
        keep = keep + some.astype(F32)
    total = keep[:own] + swap(keep[own:].astype(BF), ALONG_X).astype(F32)
    ngram_now = ngram_now - ngram_rate * (ours.astype(F32) + ngram_got.astype(F32))
    doc_now = doc_now - doc_rate * total
    return doc_now, ngram_now


def plain_kernel(docs, ngrams, counts, pmi, weights, u, v, gu, gv, s, e):
    v16 = v[...].astype(BF)
    s[...] = dot(u[...], v16, ((1,), (1,)))
    count = counts[0, 0]
    for k in range(pmi.shape[2]):
        rows = pl.ds(pl.multiple_of(docs[0, 0, k] * BLK, BLK), BLK)
        lanes = pl.ds(pl.multiple_of(ngrams[0, 0, k] * BLK, BLK), BLK)
        live = (k < count).astype(F32)
        p = pmi[0, 0, k].astype(F32)
        w = weights[0, 0, k].astype(F32)
        e[rows, lanes] = (live * w * (s[rows, lanes] - p)).astype(BF)
    gu[...] = dot(e[...], v16, ((1,), (0,)))
    gv[...] = dot(e[...], u[...], ((0,), (0,)))


def any_slice(doc_now, ngram_now, block_docs, block_ngrams, block_counts, pmi, weights, rates):
    doc_rate, ngram_rate = rates
    slots = (block_docs, block_ngrams, block_counts, pmi, weights)
    rows = doc_now.shape[0] * lax.axis_size("col")
    n = ngram_now.shape[0]
    for step in range(2):
        u = lax.all_gather(doc_now.astype(BF), "col", axis=0, tiled=True)
        gu, gv = call(
            plain_kernel,
            [shape(rows, R, F32), shape(n, R, F32)],
            [SMEM] * 3 + [VMEM] * 4,
            (*slots, u, ngram_now),
            [pltpu.VMEM((rows, n), F32), pltpu.VMEM((rows, n), BF)],
            flops=6 * rows * n * R,
        )
        doc_now = doc_now - doc_rate * lax.psum_scatter(gu, "col", scatter_dimension=0, tiled=True)
        ngram_now = ngram_now - ngram_rate * lax.psum(gv, "grp")
    return doc_now, ngram_now


def shards(doc_factors, ngram_factors, block_docs, block_ngrams, block_counts, pmi, weights):
    shard_count = lax.axis_size("col")
    group_count = lax.axis_size("grp")
    doc_total = doc_factors.shape[0] * shard_count * group_count
    ngram_total = ngram_factors.shape[0] * shard_count
    width = doc_factors.shape[1]
    doc_base = math.sqrt(ngram_total) + 1.5 * math.sqrt(width)
    ngram_base = math.sqrt(doc_total) + 1.5 * math.sqrt(width)
    rates = (100.0 / (doc_base * doc_base), 100.0 / (ngram_base * ngram_base))
    run = small_slice if (group_count, shard_count) == (2, 16) else any_slice
    return run(
        doc_factors, ngram_factors, block_docs, block_ngrams, block_counts, pmi, weights, rates
    )


def solution(mesh):
    return jax.shard_map(
        shards,
        mesh=mesh,
        in_specs=(
            P(("grp", "col"), None),
            P("col", None),
            P("grp", "col", None),
            P("grp", "col", None),
            P("grp", "col"),
            P("grp", "col", None, None, None),
            P("grp", "col", None, None, None),
        ),
        out_specs=(P(("grp", "col"), None), P("col", None)),
        check_vma=False,
    )
```

time: 194 us -> 49.8 us (0.26)
  waiting for transfers between devices: 104 us -> 17 us
  blocking collectives: 43.9 us -> 0 us
  starting transfers between devices: 0.35 us -> 23.3 us
  between operations: 16.3 us -> 1.51 us
  matrix products: 13.4 us -> 0 us
  other arithmetic: 9.04 us -> 1.65 us
  local copies, waits for them, and re-layouts: 6.25 us -> 0.03 us
  Pallas kernels: 0 us -> 6.14 us
    reduce_scatter x2 -> x0, waiting for transfers between devices: 59.1 us -> none  [shards(): lax.psum_scatter(grad_doc, 'col', scatter_dimension=0, tiled=True)]
    psum x2 -> x0, waiting for transfers between devices: 44.9 us -> none  [shards(): summed = lax.psum(grad_ngram, 'grp')]
    all_gather x2 -> x0, blocking collectives: 43.9 us -> none  [shards(): lax.all_gather(doc_now.astype(jnp.bfloat16), 'col', axis=0, tiled=True)]
    ppermute x0 -> x21, starting transfers between devices: none -> 23.3 us  [the longest x19 20.2 us: swap(): lax.ppermute(x, 'col', [(i, i ^ mask) for i in range(lax.axis_size('col'))])]
    ppermute x0 -> x21, waiting for transfers between devices: none -> 17 us  [the longest x19 14.6 us: swap(): lax.ppermute(x, 'col', [(i, i ^ mask) for i in range(lax.axis_size('col'))])]
    dot_general x10 -> x0, matrix products: 13.4 us -> none  [the longest x2 3.94 us: local_grads(): jnp.einsum('kn,kjr->njr', ngram_onehot, ngram_terms, precision=highest)]
    pallas_call x0 -> x11, Pallas kernels: none -> 6.14 us  [call(): pl.pallas_call(kernel, out_shape=outs, in_specs=in_specs, out_specs=[VMEM...]
    convert_element_type x5 -> x2, other arithmetic: 3.71 us -> 0.13 us  [gradients(): ours = (gv_keep + swap(gv_send, OTHER_CORE).astype(F32)).astype(BF)]
  transfers between devices with their start and end apart: 4 -> 21, of which waited for: 4 -> 11; matrix products, arithmetic and copies ran while one was open for 5% -> 2% of each run, Pallas kernels for 0% -> 10%
where the time goes in v2:
time: 49.8 us; the launch traced here: 49.6 us
  starting transfers between devices  23.3 us (47%)
  waiting for transfers between devices  17 us (34%)
  Pallas kernels  6.14 us (12%)
  other arithmetic  1.65 us (3%)
  between operations  1.51 us (3%)
    ppermute x19, starting transfers between devices, swap(): lax.ppermute(x, 'col', [(i, i ^ mask) for i in range(lax.axis_size('col'))])  20.2 us
    ppermute x19, waiting for transfers between devices, swap(): lax.ppermute(x, 'col', [(i, i ^ mask) for i in range(lax.axis_size('col'))])  14.6 us
    pallas_call x11, Pallas kernels, call(): pl.pallas_call(kernel, out_shape=outs, in_specs=in_specs, out_specs=[VMEM...  6.14 us
    ppermute x2, starting transfers between devices, swap_group(): return lax.ppermute(x, 'grp', [(0, 1), (1, 0)])  3.13 us
    ppermute x2, waiting for transfers between devices, swap_group(): return lax.ppermute(x, 'grp', [(0, 1), (1, 0)])  2.39 us
  transfers between devices with their start and end apart: 21, of which 11 were waited for; matrix products, arithmetic and copies ran while one was open for 2% of the time, Pallas kernels for 10%

profile of v2, /device:TPU:0, one launch (start us, length us, event | category | flops | bytes accessed | tf_op | source)
XLA Modules:
  0.0 49.6 jit_solution(3308712156525990240)
XLA Ops:
  0.7 2.4 %collective-permute-start = (f32[32,256]{1,0:T(8,128)}, f32[32,256]{1,0:T(8,128)S(1)}, u32[]{:S(2)}, u32[]{:S(2)}) collective-permute-start(f32[32,256]{1,0:T(8,128)} %doc.1), channel_id=1, source_target_pairs={{0,3},{1,2},{2,1},{3,0},{4,7},{5,6},{6,5},{7,4},{8,11},{9,10},{10,... | collective-permute-start | bytes 98312 | tf_op jit(solution)/shard_map/ppermute | solution.py:167
  3.8 3.3 %shard_map.86 = (bf16[512,512]{1,0:T(8,128)(2,1)S(1)}, bf16[768,512]{1,0:T(8,128)(2,1)}, bf16[512,256]{1,0:T(8,128)(2,1)S(1)}) custom-call(s32[1,1,16]{2,1,0:T(1,128)S(1)} %copy-done.4, s32[1,1,16]{2,1,0:T(1,128)S(1)} %copy-done.5, s32[1,1]{1,0:T(1,128)S(6)} %copy.9.counts, bf16[1,1,16,128,128]{4,3,2,1,0:T(8,128)(2,1)} %pmi_hbm.1, ...), custom_call_target="tpu_custom_call" | custom-call | bytes 1572996 | tf_op jit(solution)/shard_map/pallas_call | solution.py:34
  7.1 3.7 %collective-permute-start.3 = (bf16[64,256]{1,0:T(8,128)(2,1)S(1)}, bf16[64,256]{1,0:T(8,128)(2,1)S(1)}, u32[]{:S(2)}, u32[]{:S(2)}) collective-permute-start(bf16[64,256]{1,0:T(8,128)(2,1)S(1)} %shard_map.87.pair), channel_id=1, source_target_pairs={{0,12},{1,13},{2,14},{3,15},{4,8},{5,9},{6,10},{7,11},{8,4},{9,5},... | collective-permute-start | bytes 98312 | tf_op jit(solution)/shard_map/ppermute | solution.py:167
  10.8 0.0 collective-permute-start.2
  10.8 0.5 %collective-permute-start.1 = (bf16[64,256]{1,0:T(8,128)(2,1)S(1)}, bf16[64,256]{1,0:T(8,128)(2,1)S(1)}, u32[]{:S(2)}, u32[]{:S(2)}) collective-permute-start(bf16[64,256]{1,0:T(8,128)(2,1)S(1)} %shard_map.87.pair), channel_id=1, source_target_pairs={{0,5},{1,4},{2,7},{3,6},{4,1},{5,0},{6,3},{7,2},{8,13},{9,12},{10,... | collective-permute-start | bytes 98312 | tf_op jit(solution)/shard_map/ppermute | solution.py:167
  11.3 0.5 %collective-permute-start.4 = (bf16[768,512]{1,0:T(8,128)(2,1)}, bf16[768,512]{1,0:T(8,128)(2,1)S(1)}, u32[]{:S(2)}, u32[]{:S(2)}) collective-permute-start(bf16[768,512]{1,0:T(8,128)(2,1)} %get-tuple-element.39), channel_id=1, source_target_pairs={{0,1},{1,0},{2,3},{3,2},{4,5},{5,4},{6,7},{7,6},{8,9},{9,8},{10,11... | collective-permute-start | bytes 2359304 | tf_op jit(solution)/shard_map/ppermute | solution.py:167
  11.8 1.2 %collective-permute-done.3.far3 = bf16[64,256]{1,0:T(8,128)(2,1)S(1)} collective-permute-done((bf16[64,256]{1,0:T(8,128)(2,1)S(1)}, bf16[64,256]{1,0:T(8,128)(2,1)S(1)}, u32[]{:S(2)}, u32[]{:S(2)}) %collective-permute-start.3) | collective-permute-done | bytes 32800 | tf_op jit(solution)/shard_map/ppermute | solution.py:167
  13.0 2.1 %collective-permute-done.2.far2 = bf16[64,256]{1,0:T(8,128)(2,1)S(1)} collective-permute-done((bf16[64,256]{1,0:T(8,128)(2,1)S(1)}, bf16[64,256]{1,0:T(8,128)(2,1)S(1)}, u32[]{:S(2)}, u32[]{:S(2)}) %collective-permute-start.2) | collective-permute-done | bytes 32800 | tf_op jit(solution)/shard_map/ppermute | solution.py:167
  15.1 0.0 collective-permute-done.1.far1
  15.1 0.5 %shard_map.88 = (bf16[256,256]{1,0:T(8,128)(2,1)S(1)}, bf16[256,512]{1,0:T(8,128)(2,1)S(1)}, f32[256,256]{1,0:T(8,128)S(1)}) custom-call(bf16[64,256]{1,0:T(8,128)(2,1)S(1)} %shard_map.87.pair, bf16[64,256]{1,0:T(8,128)(2,1)S(1)} %collective-permute-done.1.far1, bf16[64,256]{1,0:T(8,128)(2,1)S(1)} %collective-permute-done.2.far2, ...), custom_call_target="tpu_custom_call" | custom-call | flops 99999997952 | bytes 917504 | tf_op jit(solution)/shard_map/pallas_call | solution.py:34
  15.6 0.5 %shard_map.89 = (f32[64,256]{1,0:T(8,128)S(1)}, bf16[64,256]{1,0:T(8,128)(2,1)S(1)}, bf16[64,256]{1,0:T(8,128)(2,1)S(1)}, bf16[64,256]{1,0:T(8,128)(2,1)S(1)}, bf16[256,512]{1,0:T(8,128)(2,1)S(1)}) custom-call(bf16[256,256]{1,0:T(8,128)(2,1)S(1)} %get-tuple-element.37.u, f32[256,256]{1,0:T(8,128)S(1)} %get-tuple-element.38.gu_own, ...), custom_call_target="tpu_custom_call" | custom-call | flops 134217728 | bytes 1179648 | tf_op jit(solution)/shard_map/pallas_call | solution.py:34
  16.1 0.6 %collective-permute-start.5 = (bf16[64,256]{1,0:T(8,128)(2,1)S(1)}, bf16[64,256]{1,0:T(8,128)(2,1)S(1)}, u32[]{:S(2)}, u32[]{:S(2)}) collective-permute-start(bf16[64,256]{1,0:T(8,128)(2,1)S(1)} %get-tuple-element.41), channel_id=1, source_target_pairs={{0,5},{1,4},{2,7},{3,6},{4,1},{5,0},{6,3},{7,2},{8,13},{9,12},{10,... | collective-permute-start | bytes 98312 | tf_op jit(solution)/shard_map/ppermute | solution.py:167
  16.8 1.8 %collective-permute-start.6 = (bf16[64,256]{1,0:T(8,128)(2,1)S(1)}, bf16[64,256]{1,0:T(8,128)(2,1)S(1)}, u32[]{:S(2)}, u32[]{:S(2)}) collective-permute-start(bf16[64,256]{1,0:T(8,128)(2,1)S(1)} %get-tuple-element.42), channel_id=1, source_target_pairs={{0,9},{1,8},{2,11},{3,10},{4,13},{5,12},{6,15},{7,14},{8,1},{9,0},... | collective-permute-start | bytes 98312 | tf_op jit(solution)/shard_map/ppermute | solution.py:167
  18.6 1.8 %collective-permute-start.7 = (bf16[64,256]{1,0:T(8,128)(2,1)S(1)}, bf16[64,256]{1,0:T(8,128)(2,1)S(1)}, u32[]{:S(2)}, u32[]{:S(2)}) collective-permute-start(bf16[64,256]{1,0:T(8,128)(2,1)S(1)} %get-tuple-element.43), channel_id=1, source_target_pairs={{0,12},{1,13},{2,14},{3,15},{4,8},{5,9},{6,10},{7,11},{8,4},{9,5},... | collective-permute-start | bytes 98312 | tf_op jit(solution)/shard_map/ppermute | solution.py:167
  20.3 0.3 shard_map.92
  20.7 0.1 collective-permute-start.12
  20.8 0.2 collective-permute-done.6.got2
  21.0 3.3 %collective-permute-done.7.got3 = bf16[64,256]{1,0:T(8,128)(2,1)S(1)} collective-permute-done((bf16[64,256]{1,0:T(8,128)(2,1)S(1)}, bf16[64,256]{1,0:T(8,128)(2,1)S(1)}, u32[]{:S(2)}, u32[]{:S(2)}) %collective-permute-start.7) | collective-permute-done | bytes 32800 | tf_op jit(solution)/shard_map/ppermute | solution.py:167
  24.3 0.1 collective-permute-start.8
  24.4 0.1 add_convert_fusion.1.ours
  24.5 1.6 %collective-permute-start.13 = (bf16[512,256]{1,0:T(8,128)(2,1)S(1)}, bf16[512,256]{1,0:T(8,128)(2,1)S(1)}, u32[]{:S(2)}, u32[]{:S(2)}) collective-permute-start(bf16[512,256]{1,0:T(8,128)(2,1)S(1)} %add_convert_fusion.1.ours), channel_id=1, source_target_pairs={{0,16},{16,0},{1,17},{17,1},{2,18},{18,2},{3,19},{19,3},{4,20},{20... | collective-permute-start | bytes 786440 | tf_op jit(solution)/shard_map/ppermute | solution.py:176
  26.1 1.7 %collective-permute-done.8.got = bf16[64,256]{1,0:T(8,128)(2,1)S(1)} collective-permute-done((bf16[64,256]{1,0:T(8,128)(2,1)S(1)}, bf16[64,256]{1,0:T(8,128)(2,1)S(1)}, u32[]{:S(2)}, u32[]{:S(2)}) %collective-permute-start.8) | collective-permute-done | bytes 32800 | tf_op jit(solution)/shard_map/ppermute | solution.py:167
  27.7 1.9 %collective-permute-start.11 = (bf16[64,256]{1,0:T(8,128)(2,1)S(1)}, bf16[64,256]{1,0:T(8,128)(2,1)S(1)}, u32[]{:S(2)}, u32[]{:S(2)}) collective-permute-start(bf16[64,256]{1,0:T(8,128)(2,1)S(1)} %get-tuple-element.47.after.pair), channel_id=1, source_target_pairs={{0,12},{1,13},{2,14},{3,15},{4,8},{5,9},{6,10},{7,11},{8,4},{9,5},... | collective-permute-start | bytes 98312 | tf_op jit(solution)/shard_map/ppermute | solution.py:167
  29.6 0.0 collective-permute-start.10
  29.6 2.3 %collective-permute-start.9 = (bf16[64,256]{1,0:T(8,128)(2,1)S(1)}, bf16[64,256]{1,0:T(8,128)(2,1)S(1)}, u32[]{:S(2)}, u32[]{:S(2)}) collective-permute-start(bf16[64,256]{1,0:T(8,128)(2,1)S(1)} %get-tuple-element.47.after.pair), channel_id=1, source_target_pairs={{0,5},{1,4},{2,7},{3,6},{4,1},{5,0},{6,3},{7,2},{8,13},{9,12},{10,... | collective-permute-start | bytes 98312 | tf_op jit(solution)/shard_map/ppermute | solution.py:167
  31.9 1.5 %collective-permute-done.13.got = bf16[512,256]{1,0:T(8,128)(2,1)S(1)} collective-permute-done((bf16[512,256]{1,0:T(8,128)(2,1)S(1)}, bf16[512,256]{1,0:T(8,128)(2,1)S(1)}, u32[]{:S(2)}, u32[]{:S(2)}) %collective-permute-start.13) | collective-permute-done | bytes 262176 | tf_op jit(solution)/shard_map/ppermute | solution.py:176
  33.4 0.1 shard_map.93
  33.5 0.1 collective-permute-start.14
  33.6 0.8 %collective-permute-done.10.far2 = bf16[64,256]{1,0:T(8,128)(2,1)S(1)} collective-permute-done((bf16[64,256]{1,0:T(8,128)(2,1)S(1)}, bf16[64,256]{1,0:T(8,128)(2,1)S(1)}, u32[]{:S(2)}, u32[]{:S(2)}) %collective-permute-start.10) | collective-permute-done | bytes 32800 | tf_op jit(solution)/shard_map/ppermute | solution.py:167
  34.4 0.5 %shard_map.94 = (bf16[256,256]{1,0:T(8,128)(2,1)S(1)}, bf16[256,512]{1,0:T(8,128)(2,1)S(1)}, f32[256,256]{1,0:T(8,128)S(1)}) custom-call(bf16[64,256]{1,0:T(8,128)(2,1)S(1)} %get-tuple-element.47.after.pair, bf16[64,256]{1,0:T(8,128)(2,1)S(1)} %collective-permute-done.9.far1, bf16[64,256]{1,0:T(8,128)(2,1)S(1)} %collective-permute-done.10.far2, ...), custom_call_target="tpu_custom_call" | custom-call | flops 99999997952 | bytes 917504 | tf_op jit(solution)/shard_map/pallas_call | solution.py:34
  34.9 0.2 collective-permute-done.14.rest_0_
  35.1 0.5 %shard_map.95 = (f32[64,256]{1,0:T(8,128)S(1)}, bf16[64,256]{1,0:T(8,128)(2,1)S(1)}, bf16[64,256]{1,0:T(8,128)(2,1)S(1)}, bf16[64,256]{1,0:T(8,128)(2,1)S(1)}, bf16[256,512]{1,0:T(8,128)(2,1)S(1)}) custom-call(bf16[256,256]{1,0:T(8,128)(2,1)S(1)} %get-tuple-element.53.u, f32[256,256]{1,0:T(8,128)S(1)} %get-tuple-element.54.gu_own, ...), custom_call_target="tpu_custom_call" | custom-call | flops 134217728 | bytes 1441792 | tf_op jit(solution)/shard_map/pallas_call | solution.py:34
  35.6 0.3 shard_map.96
  36.0 0.2 collective-permute-start.19
  36.2 0.6 %collective-permute-start.15 = (bf16[64,256]{1,0:T(8,128)(2,1)S(1)}, bf16[64,256]{1,0:T(8,128)(2,1)S(1)}, u32[]{:S(2)}, u32[]{:S(2)}) collective-permute-start(bf16[64,256]{1,0:T(8,128)(2,1)S(1)} %get-tuple-element.56), channel_id=1, source_target_pairs={{0,5},{1,4},{2,7},{3,6},{4,1},{5,0},{6,3},{7,2},{8,13},{9,12},{10,... | collective-permute-start | bytes 98312 | tf_op jit(solution)/shard_map/ppermute | solution.py:167
  36.8 1.5 %collective-permute-start.16 = (bf16[64,256]{1,0:T(8,128)(2,1)S(1)}, bf16[64,256]{1,0:T(8,128)(2,1)S(1)}, u32[]{:S(2)}, u32[]{:S(2)}) collective-permute-start(bf16[64,256]{1,0:T(8,128)(2,1)S(1)} %get-tuple-element.57), channel_id=1, source_target_pairs={{0,9},{1,8},{2,11},{3,10},{4,13},{5,12},{6,15},{7,14},{8,1},{9,0},... | collective-permute-start | bytes 98312 | tf_op jit(solution)/shard_map/ppermute | solution.py:167
  38.2 2.1 %collective-permute-start.17 = (bf16[64,256]{1,0:T(8,128)(2,1)S(1)}, bf16[64,256]{1,0:T(8,128)(2,1)S(1)}, u32[]{:S(2)}, u32[]{:S(2)}) collective-permute-start(bf16[64,256]{1,0:T(8,128)(2,1)S(1)} %get-tuple-element.58), channel_id=1, source_target_pairs={{0,12},{1,13},{2,14},{3,15},{4,8},{5,9},{6,10},{7,11},{8,4},{9,5},... | collective-permute-start | bytes 98312 | tf_op jit(solution)/shard_map/ppermute | solution.py:167
  40.3 0.0 collective-permute-done.19
  40.3 0.1 add_convert_fusion
  40.4 1.5 %collective-permute-start.20 = (bf16[512,256]{1,0:T(8,128)(2,1)S(1)}, bf16[512,256]{1,0:T(8,128)(2,1)S(1)}, u32[]{:S(2)}, u32[]{:S(2)}) collective-permute-start(bf16[512,256]{1,0:T(8,128)(2,1)S(1)} %add_convert_fusion), channel_id=1, source_target_pairs={{0,16},{16,0},{1,17},{17,1},{2,18},{18,2},{3,19},{19,3},{4,20},{20... | collective-permute-start | bytes 786440 | tf_op jit(solution)/shard_map/ppermute | solution.py:176
  41.9 0.0 collective-permute-done.15
  41.9 0.0 collective-permute-done.16
  41.9 2.0 %collective-permute-done.17 = bf16[64,256]{1,0:T(8,128)(2,1)S(1)} collective-permute-done((bf16[64,256]{1,0:T(8,128)(2,1)S(1)}, bf16[64,256]{1,0:T(8,128)(2,1)S(1)}, u32[]{:S(2)}, u32[]{:S(2)}) %collective-permute-start.17) | collective-permute-done | bytes 32800 | tf_op jit(solution)/shard_map/ppermute | solution.py:167
  44.0 0.1 collective-permute-start.18
  44.1 3.2 %collective-permute-done.18 = bf16[32,256]{1,0:T(8,128)(2,1)S(1)} collective-permute-done((bf16[32,256]{1,0:T(8,128)(2,1)S(1)}, bf16[32,256]{1,0:T(8,128)(2,1)S(1)}, u32[]{:S(2)}, u32[]{:S(2)}) %collective-permute-start.18) | collective-permute-done | bytes 16416 | tf_op jit(solution)/shard_map/ppermute | solution.py:167
  47.2 0.6 %fusion.1 = f32[32,256]{1,0:T(8,128)} fusion(f32[32,256]{1,0:T(8,128)S(1)} %get-tuple-element.46, f32[64,256]{1,0:T(8,128)S(1)} %convert_add_fusion, bf16[32,256]{1,0:T(8,128)(2,1)S(1)} %collective-permute-done.18), kind=kLoop, calls=%fused_computation.7 | loop fusion | flops 32768 | bytes 114688 | tf_op jit(solution)/shard_map/sub | solution.py:258
  47.8 0.9 %collective-permute-done.20 = bf16[512,256]{1,0:T(8,128)(2,1)S(1)} collective-permute-done((bf16[512,256]{1,0:T(8,128)(2,1)S(1)}, bf16[512,256]{1,0:T(8,128)(2,1)S(1)}, u32[]{:S(2)}, u32[]{:S(2)}) %collective-permute-start.20) | collective-permute-done | bytes 262176 | tf_op jit(solution)/shard_map/ppermute | solution.py:176
  48.7 0.9 %multiply_subtract_fusion = f32[512,256]{1,0:T(8,128)} fusion(f32[512,256]{1,0:T(8,128)S(1)} %get-tuple-element.59, bf16[512,256]{1,0:T(8,128)(2,1)S(1)} %collective-permute-done.20, bf16[512,256]{1,0:T(8,128)(2,1)S(1)} %add_convert_fusion), kind=kLoop, calls=%fused_computation | loop fusion | flops 655360 | bytes 1572864 | tf_op jit(solution)/shard_map/sub | solution.py:257
  (23 shorter events, 0.1 us)
Async XLA Ops:
  0.6 3.1 %copy-start.5 = (s32[1,1,16]{2,1,0:T(1,128)S(1)}, s32[1,1,16]{2,1,0:T(1,128)}, u32[]{:S(2)}) copy-start(s32[1,1,16]{2,1,0:T(1,128)} %ngrams.1) | copy-start | bytes 196
  0.6 3.1 %copy-start.4 = (s32[1,1,16]{2,1,0:T(1,128)S(1)}, s32[1,1,16]{2,1,0:T(1,128)}, u32[]{:S(2)}) copy-start(s32[1,1,16]{2,1,0:T(1,128)} %docs.1) | copy-start | bytes 196
  0.7 6.4 %collective-permute-start = (f32[32,256]{1,0:T(8,128)}, f32[32,256]{1,0:T(8,128)S(1)}, u32[]{:S(2)}, u32[]{:S(2)}) collective-permute-start(f32[32,256]{1,0:T(8,128)} %doc.1), channel_id=1, source_target_pairs={{0,3},{1,2},{2,1},{3,0},{4,7},{5,6},{6,5},{7,4},{8,11},{9,10},{10,... | collective-permute-start | bytes 98312 | tf_op jit(solution)/shard_map/ppermute | solution.py:167
  3.8 3.3 %copy-start.3 = (f32[32,256]{1,0:T(8,128)S(1)}, f32[32,256]{1,0:T(8,128)}, u32[]{:S(2)}) copy-start(f32[32,256]{1,0:T(8,128)} %doc.1) | copy-start | bytes 98308
  7.1 5.9 %collective-permute-start.3 = (bf16[64,256]{1,0:T(8,128)(2,1)S(1)}, bf16[64,256]{1,0:T(8,128)(2,1)S(1)}, u32[]{:S(2)}, u32[]{:S(2)}) collective-permute-start(bf16[64,256]{1,0:T(8,128)(2,1)S(1)} %shard_map.87.pair), channel_id=1, source_target_pairs={{0,12},{1,13},{2,14},{3,15},{4,8},{5,9},{6,10},{7,11},{8,4},{9,5},... | collective-permute-start | bytes 98312 | tf_op jit(solution)/shard_map/ppermute | solution.py:167
  10.8 4.3 %collective-permute-start.2 = (bf16[64,256]{1,0:T(8,128)(2,1)S(1)}, bf16[64,256]{1,0:T(8,128)(2,1)S(1)}, u32[]{:S(2)}, u32[]{:S(2)}) collective-permute-start(bf16[64,256]{1,0:T(8,128)(2,1)S(1)} %shard_map.87.pair), channel_id=1, source_target_pairs={{0,9},{1,8},{2,11},{3,10},{4,13},{5,12},{6,15},{7,14},{8,1},{9,0},... | collective-permute-start | bytes 98312 | tf_op jit(solution)/shard_map/ppermute | solution.py:167
  10.8 4.3 %collective-permute-start.1 = (bf16[64,256]{1,0:T(8,128)(2,1)S(1)}, bf16[64,256]{1,0:T(8,128)(2,1)S(1)}, u32[]{:S(2)}, u32[]{:S(2)}) collective-permute-start(bf16[64,256]{1,0:T(8,128)(2,1)S(1)} %shard_map.87.pair), channel_id=1, source_target_pairs={{0,5},{1,4},{2,7},{3,6},{4,1},{5,0},{6,3},{7,2},{8,13},{9,12},{10,... | collective-permute-start | bytes 98312 | tf_op jit(solution)/shard_map/ppermute | solution.py:167
  11.3 4.3 %collective-permute-start.4 = (bf16[768,512]{1,0:T(8,128)(2,1)}, bf16[768,512]{1,0:T(8,128)(2,1)S(1)}, u32[]{:S(2)}, u32[]{:S(2)}) collective-permute-start(bf16[768,512]{1,0:T(8,128)(2,1)} %get-tuple-element.39), channel_id=1, source_target_pairs={{0,1},{1,0},{2,3},{3,2},{4,5},{5,4},{6,7},{7,6},{8,9},{9,8},{10,11... | collective-permute-start | bytes 2359304 | tf_op jit(solution)/shard_map/ppermute | solution.py:167
  15.6 5.0 %copy-start = (bf16[768,512]{1,0:T(8,128)(2,1)}, bf16[768,512]{1,0:T(8,128)(2,1)S(1)}, u32[]{:S(2)}) copy-start(bf16[768,512]{1,0:T(8,128)(2,1)S(1)} %collective-permute-done.4.theirs) | copy-start | bytes 2359300
  16.1 4.7 %collective-permute-start.5 = (bf16[64,256]{1,0:T(8,128)(2,1)S(1)}, bf16[64,256]{1,0:T(8,128)(2,1)S(1)}, u32[]{:S(2)}, u32[]{:S(2)}) collective-permute-start(bf16[64,256]{1,0:T(8,128)(2,1)S(1)} %get-tuple-element.41), channel_id=1, source_target_pairs={{0,5},{1,4},{2,7},{3,6},{4,1},{5,0},{6,3},{7,2},{8,13},{9,12},{10,... | collective-permute-start | bytes 98312 | tf_op jit(solution)/shard_map/ppermute | solution.py:167
  16.8 4.3 %collective-permute-start.6 = (bf16[64,256]{1,0:T(8,128)(2,1)S(1)}, bf16[64,256]{1,0:T(8,128)(2,1)S(1)}, u32[]{:S(2)}, u32[]{:S(2)}) collective-permute-start(bf16[64,256]{1,0:T(8,128)(2,1)S(1)} %get-tuple-element.42), channel_id=1, source_target_pairs={{0,9},{1,8},{2,11},{3,10},{4,13},{5,12},{6,15},{7,14},{8,1},{9,0},... | collective-permute-start | bytes 98312 | tf_op jit(solution)/shard_map/ppermute | solution.py:167
  18.6 5.7 %collective-permute-start.7 = (bf16[64,256]{1,0:T(8,128)(2,1)S(1)}, bf16[64,256]{1,0:T(8,128)(2,1)S(1)}, u32[]{:S(2)}, u32[]{:S(2)}) collective-permute-start(bf16[64,256]{1,0:T(8,128)(2,1)S(1)} %get-tuple-element.43), channel_id=1, source_target_pairs={{0,12},{1,13},{2,14},{3,15},{4,8},{5,9},{6,10},{7,11},{8,4},{9,5},... | collective-permute-start | bytes 98312 | tf_op jit(solution)/shard_map/ppermute | solution.py:167
  20.7 3.7 %collective-permute-start.12 = (bf16[512,256]{1,0:T(8,128)(2,1)S(1)}, bf16[512,256]{1,0:T(8,128)(2,1)S(1)}, u32[]{:S(2)}, u32[]{:S(2)}) collective-permute-start(bf16[512,256]{1,0:T(8,128)(2,1)S(1)} %get-tuple-element.51), channel_id=1, source_target_pairs={{0,1},{1,0},{2,3},{3,2},{4,5},{5,4},{6,7},{7,6},{8,9},{9,8},{10,11... | collective-permute-start | bytes 786440 | tf_op jit(solution)/shard_map/ppermute | solution.py:167
  24.3 3.4 %collective-permute-start.8 = (bf16[64,256]{1,0:T(8,128)(2,1)S(1)}, bf16[64,256]{1,0:T(8,128)(2,1)S(1)}, u32[]{:S(2)}, u32[]{:S(2)}) collective-permute-start(bf16[64,256]{1,0:T(8,128)(2,1)S(1)} %get-tuple-element.45), channel_id=1, source_target_pairs={{0,3},{1,2},{2,1},{3,0},{4,7},{5,6},{6,5},{7,4},{8,11},{9,10},{10,... | collective-permute-start | bytes 98312 | tf_op jit(solution)/shard_map/ppermute | solution.py:167
  24.5 8.9 %collective-permute-start.13 = (bf16[512,256]{1,0:T(8,128)(2,1)S(1)}, bf16[512,256]{1,0:T(8,128)(2,1)S(1)}, u32[]{:S(2)}, u32[]{:S(2)}) collective-permute-start(bf16[512,256]{1,0:T(8,128)(2,1)S(1)} %add_convert_fusion.1.ours), channel_id=1, source_target_pairs={{0,16},{16,0},{1,17},{17,1},{2,18},{18,2},{3,19},{19,3},{4,20},{20... | collective-permute-start | bytes 786440 | tf_op jit(solution)/shard_map/ppermute | solution.py:176
  27.7 5.7 %copy-start.2 = (f32[512,256]{1,0:T(8,128)S(1)}, f32[512,256]{1,0:T(8,128)}, u32[]{:S(2)}) copy-start(f32[512,256]{1,0:T(8,128)} %v.1) | copy-start | bytes 1572868
  27.7 5.9 %collective-permute-start.11 = (bf16[64,256]{1,0:T(8,128)(2,1)S(1)}, bf16[64,256]{1,0:T(8,128)(2,1)S(1)}, u32[]{:S(2)}, u32[]{:S(2)}) collective-permute-start(bf16[64,256]{1,0:T(8,128)(2,1)S(1)} %get-tuple-element.47.after.pair), channel_id=1, source_target_pairs={{0,12},{1,13},{2,14},{3,15},{4,8},{5,9},{6,10},{7,11},{8,4},{9,5},... | collective-permute-start | bytes 98312 | tf_op jit(solution)/shard_map/ppermute | solution.py:167
  29.6 4.8 %collective-permute-start.10 = (bf16[64,256]{1,0:T(8,128)(2,1)S(1)}, bf16[64,256]{1,0:T(8,128)(2,1)S(1)}, u32[]{:S(2)}, u32[]{:S(2)}) collective-permute-start(bf16[64,256]{1,0:T(8,128)(2,1)S(1)} %get-tuple-element.47.after.pair), channel_id=1, source_target_pairs={{0,9},{1,8},{2,11},{3,10},{4,13},{5,12},{6,15},{7,14},{8,1},{9,0},... | collective-permute-start | bytes 98312 | tf_op jit(solution)/shard_map/ppermute | solution.py:167
  29.6 4.8 %collective-permute-start.9 = (bf16[64,256]{1,0:T(8,128)(2,1)S(1)}, bf16[64,256]{1,0:T(8,128)(2,1)S(1)}, u32[]{:S(2)}, u32[]{:S(2)}) collective-permute-start(bf16[64,256]{1,0:T(8,128)(2,1)S(1)} %get-tuple-element.47.after.pair), channel_id=1, source_target_pairs={{0,5},{1,4},{2,7},{3,6},{4,1},{5,0},{6,3},{7,2},{8,13},{9,12},{10,... | collective-permute-start | bytes 98312 | tf_op jit(solution)/shard_map/ppermute | solution.py:167
  33.5 1.6 %copy-start.1 = (bf16[768,512]{1,0:T(8,128)(2,1)S(1)}, bf16[768,512]{1,0:T(8,128)(2,1)}, u32[]{:S(2)}) copy-start(bf16[768,512]{1,0:T(8,128)(2,1)} %copy-done) | copy-start | bytes 2359300
  33.5 1.6 %collective-permute-start.14 = (bf16[512,256]{1,0:T(8,128)(2,1)S(1)}, bf16[512,256]{1,0:T(8,128)(2,1)S(1)}, u32[]{:S(2)}, u32[]{:S(2)}) collective-permute-start(bf16[512,256]{1,0:T(8,128)(2,1)S(1)} %get-tuple-element.52.v16), channel_id=1, source_target_pairs={{0,1},{1,0},{2,3},{3,2},{4,5},{5,4},{6,7},{7,6},{8,9},{9,8},{10,11... | collective-permute-start | bytes 786440 | tf_op jit(solution)/shard_map/ppermute | solution.py:167
  36.0 4.3 %collective-permute-start.19 = (bf16[512,256]{1,0:T(8,128)(2,1)S(1)}, bf16[512,256]{1,0:T(8,128)(2,1)S(1)}, u32[]{:S(2)}, u32[]{:S(2)}) collective-permute-start(bf16[512,256]{1,0:T(8,128)(2,1)S(1)} %get-tuple-element.63), channel_id=1, source_target_pairs={{0,1},{1,0},{2,3},{3,2},{4,5},{5,4},{6,7},{7,6},{8,9},{9,8},{10,11... | collective-permute-start | bytes 786440 | tf_op jit(solution)/shard_map/ppermute | solution.py:167
  36.2 5.8 %collective-permute-start.15 = (bf16[64,256]{1,0:T(8,128)(2,1)S(1)}, bf16[64,256]{1,0:T(8,128)(2,1)S(1)}, u32[]{:S(2)}, u32[]{:S(2)}) collective-permute-start(bf16[64,256]{1,0:T(8,128)(2,1)S(1)} %get-tuple-element.56), channel_id=1, source_target_pairs={{0,5},{1,4},{2,7},{3,6},{4,1},{5,0},{6,3},{7,2},{8,13},{9,12},{10,... | collective-permute-start | bytes 98312 | tf_op jit(solution)/shard_map/ppermute | solution.py:167
  36.8 5.2 %collective-permute-start.16 = (bf16[64,256]{1,0:T(8,128)(2,1)S(1)}, bf16[64,256]{1,0:T(8,128)(2,1)S(1)}, u32[]{:S(2)}, u32[]{:S(2)}) collective-permute-start(bf16[64,256]{1,0:T(8,128)(2,1)S(1)} %get-tuple-element.57), channel_id=1, source_target_pairs={{0,9},{1,8},{2,11},{3,10},{4,13},{5,12},{6,15},{7,14},{8,1},{9,0},... | collective-permute-start | bytes 98312 | tf_op jit(solution)/shard_map/ppermute | solution.py:167
  38.2 5.7 %collective-permute-start.17 = (bf16[64,256]{1,0:T(8,128)(2,1)S(1)}, bf16[64,256]{1,0:T(8,128)(2,1)S(1)}, u32[]{:S(2)}, u32[]{:S(2)}) collective-permute-start(bf16[64,256]{1,0:T(8,128)(2,1)S(1)} %get-tuple-element.58), channel_id=1, source_target_pairs={{0,12},{1,13},{2,14},{3,15},{4,8},{5,9},{6,10},{7,11},{8,4},{9,5},... | collective-permute-start | bytes 98312 | tf_op jit(solution)/shard_map/ppermute | solution.py:167
  40.4 8.3 %collective-permute-start.20 = (bf16[512,256]{1,0:T(8,128)(2,1)S(1)}, bf16[512,256]{1,0:T(8,128)(2,1)S(1)}, u32[]{:S(2)}, u32[]{:S(2)}) collective-permute-start(bf16[512,256]{1,0:T(8,128)(2,1)S(1)} %add_convert_fusion), channel_id=1, source_target_pairs={{0,16},{16,0},{1,17},{17,1},{2,18},{18,2},{3,19},{19,3},{4,20},{20... | collective-permute-start | bytes 786440 | tf_op jit(solution)/shard_map/ppermute | solution.py:176
  44.0 3.2 %collective-permute-start.18 = (bf16[32,256]{1,0:T(8,128)(2,1)S(1)}, bf16[32,256]{1,0:T(8,128)(2,1)S(1)}, u32[]{:S(2)}, u32[]{:S(2)}) collective-permute-start(bf16[32,256]{1,0:T(8,128)(2,1)S(1)} %slice.17), channel_id=1, source_target_pairs={{0,3},{1,2},{2,1},{3,0},{4,7},{5,6},{6,5},{7,4},{8,11},{9,10},{10,... | collective-permute-start | bytes 49160 | tf_op jit(solution)/shard_map/ppermute | solution.py:167

commit v3 on v2

--- a/solution.py
+++ b/solution.py
@@ -17,7 +17,7 @@
 HBM = pl.BlockSpec(memory_space=pltpu.HBM)
 ANY = pl.BlockSpec(memory_space=pl.ANY)
 MIB = 1024 * 1024
-PLACE_VMEM = 53 * MIB
+PLACE_VMEM = int(52.4 * MIB)
 LONG = 10**11
 
 
@@ -29,8 +29,9 @@
     return jax.ShapeDtypeStruct((rows, columns), dtype)
 
 
-def call(kernel, outs, in_specs, arrays, scratch=(), flops=0, vmem=16 * MIB):
-    read = sum(a.size * a.dtype.itemsize for a in arrays)
+def call(kernel, outs, in_specs, arrays, scratch=(), flops=0, read=None, vmem=16 * MIB):
+    if read is None:
+        read = sum(a.size * a.dtype.itemsize for a in arrays)
     return pl.pallas_call(
         kernel,
         out_shape=outs,
@@ -42,8 +43,8 @@
     )(*arrays)
 
 
-ALONG_X = 3
-ALONG_Z = (0, 5, 9, 12)
+FAR = 9
+NEAR = (0, 3, 5, 7)
 OTHER_CORE = 1
 
 
@@ -61,12 +62,6 @@
             copies.append(pltpu.make_async_copy(src.at[0, 0, some], dst.at[some], sems.at[a, i]))
             copies[-1].start()
     half = mine.shape[0] // 2
-    v_half = v.shape[0] // 2
-    v_copy.wait()
-    now = v[...].astype(BF)
-    v16[...] = now
-    theirs[2 * half :, :R] = now[:v_half]
-    theirs[2 * half :, R:] = now[v_half:]
     me = lax.axis_index("col")
     low, my_z = me & 3, me >> 2
     count = counts[0, 0]
@@ -77,15 +72,18 @@
                 copies[a * parts + k // (slots // parts)].wait()
         lanes = pl.ds(pl.multiple_of(ngrams[0, 0, k] * BLK, BLK), BLK)
         z = docs[0, 0, k] ^ my_z
-        first = low ^ ((z ^ (z >> 1)) & 1)
+        near, far = z & 1, z >> 1
         live = k < count
         for x in range(2):
-            at = pl.multiple_of((x * 4 + z) * own, own)
+            at = pl.multiple_of((far * 4 + near * 2 + x) * own, own)
+            core = far ^ (near | x)
             for h, out in enumerate((mine, theirs)):
-                rows = pl.ds(pl.multiple_of((first ^ (x * 2) ^ (x ^ h)) * own, own), own)
+                rows = pl.ds(pl.multiple_of((low ^ (x * 2 + h) ^ core) * own, own), own)
                 tile = weights[k, rows, :]
                 out[pl.ds(at, own), lanes] = jnp.where(live, tile, jnp.zeros_like(tile))
                 out[pl.ds(at + half, own), lanes] = pmi[k, rows, :]
+    v_copy.wait()
+    v16[...] = v[...].astype(BF)
 
 
 def errors_and_gu(u, v_blocks, tiles, e):
@@ -110,37 +108,63 @@
     pair[own:, :] = other[...].astype(BF)
 
 
-def own_kernel(pair, far1, far2, far3, v16, mine, u, e, gu):
+def rows_kernel(pair, far1, far2, far3, u):
     own = pair.shape[0] // 2
     for x in range(2):
         for z, far in enumerate((pair, far1, far2, far3)):
             at = (x * 4 + z) * own
             u[at : at + own, :] = far[x * own : (x + 1) * own, :]
+
+
+def all_gu(u, v16, v16_theirs, mine, theirs, e, e_theirs):
     n = v16.shape[0] // 2
-    gu[...] = errors_and_gu(u[...], [v16[:n], v16[n:]], mine, e)
-
-
-def theirs_kernel(u, gu_own, theirs, *rest):
-    *v16_theirs, keep, send1, send2, send3, e = rest
-    half = u.shape[0]
-    own = half // 8
-    if v16_theirs:
-        (v16,) = v16_theirs
-        n = v16.shape[0] // 2
-        v_blocks = [v16[:n], v16[n:]]
-    else:
-        v_blocks = [theirs[2 * half :, :R], theirs[2 * half :, R:]]
-    gu = gu_own[...] + errors_and_gu(u[...], v_blocks, theirs, e)
+    gu = errors_and_gu(u[...], [v16[:n], v16[n:]], mine, e)
+    return gu + errors_and_gu(u[...], [v16_theirs[:n], v16_theirs[n:]], theirs, e_theirs)
+
+
+def near_first_kernel(u, v16, v16_theirs, mine, theirs, keep, send1, send2, send3, e, e_theirs):
+    own = u.shape[0] // 8
+    gu = all_gu(u, v16, v16_theirs, mine, theirs, e, e_theirs)
     for z, out in enumerate((keep, send1, send2, send3)):
         for x in range(2):
             at = (x * 4 + z) * own
             out[x * own : (x + 1) * own, :] = gu[at : at + own].astype(out.dtype)
 
 
-def along_z_kernel(keep, got1, got2, got3, total, total16):
+def far_first_kernel(u, v16, v16_theirs, mine, theirs, keep, send, e, e_theirs):
+    n = keep.shape[0]
+    gu = all_gu(u, v16, v16_theirs, mine, theirs, e, e_theirs)
+    keep[...] = gu[:n]
+    send[...] = gu[n:].astype(BF)
+
+
+def ngram_send_kernel(e_theirs, u, send):
+    send[...] = dot(e_theirs[...], u[...], ((0,), (0,))).astype(BF)
+
+
+def ngram_keep_kernel(e, u, got, ours):
+    ours[...] = (dot(e[...], u[...], ((0,), (0,))) + got[...].astype(F32)).astype(BF)
+
+
+def near_sum_kernel(keep, got1, got2, got3, total, total16):
     now = keep[...] + got1[...].astype(F32) + got2[...].astype(F32) + got3[...].astype(F32)
     total[...] = now
     total16[...] = now.astype(BF)
+
+
+def far_sum_kernel(keep, got, total, send1, send2, send3):
+    own = total.shape[0]
+    now = keep[...] + got[...].astype(F32)
+    for j, out in enumerate((total, send1, send2, send3)):
+        out[...] = now[j * own : (j + 1) * own].astype(out.dtype)
+
+
+def last_kernel(
+    doc_rate, ngram_rate, doc, total, got1, got2, got3, ours, ngram_got, v, doc_out, v_out
+):
+    v_out[...] = v[...] - ngram_rate * (ours[...].astype(F32) + ngram_got[...].astype(F32))
+    now = total[...] + got1[...].astype(F32) + got2[...].astype(F32) + got3[...].astype(F32)
+    doc_out[...] = doc[...] - doc_rate * now
 
 
 def pair_update_kernel(rate, doc, pair, total, got, doc_out, pair_out):
@@ -158,17 +182,12 @@
     v16[...] = now.astype(BF)
 
 
-def ngram_kernel(e, e_theirs, u, keep, send):
-    send[...] = dot(e_theirs[...], u[...], ((0,), (0,))).astype(BF)
-    keep[...] = dot(e[...], u[...], ((0,), (0,)))
-
-
 def swap(x, mask):
     return lax.ppermute(x, "col", [(i, i ^ mask) for i in range(lax.axis_size("col"))])
 
 
-def along_z(blocks):
-    got = [swap(blocks[j - 1], ALONG_Z[j]) for j in (3, 2, 1)]
+def exchange_near(blocks):
+    got = [swap(blocks[j - 1], NEAR[j]) for j in (3, 2, 1)]
     return got[::-1]
 
 
@@ -183,12 +202,11 @@
     n = ngram_now.shape[0]
     slots = pmi.shape[2]
     flops = 2 * 2 * half * 2 * n * R
-    ngram_grads = [shape(n, R, F32), shape(n, R, BF)]
-
-    other = swap(doc_now, ALONG_X)
+
+    other = swap(doc_now, FAR)
     mine, theirs, v16 = call(
         place_kernel,
-        [shape(2 * half, n, BF), shape(3 * half, n, BF), shape(n, R, BF)],
+        [shape(2 * half, n, BF), shape(2 * half, n, BF), shape(n, R, BF)],
         [SMEM] * 3 + [HBM] * 3,
         (block_docs, block_ngrams, block_counts, pmi, weights, ngram_now),
         [
@@ -202,33 +220,41 @@
     )
     theirs, other = lax.optimization_barrier((theirs, other))
     (pair,) = call(pair_kernel, [shape(2 * own, R, BF)], [VMEM] * 2, (doc_now, other))
-    far = along_z([pair] * 3)
+    far = exchange_near([pair] * 3)
     theirs = swap(theirs, OTHER_CORE)
-    def gradients(pair, far, v16, *v16_theirs):
-        u, e, gu = call(
-            own_kernel,
-            [shape(half, R, BF), shape(half, n, BF), shape(half, R, F32)],
-            [VMEM] * 6,
-            (pair, *far, v16, mine),
-            flops=LONG,
+    v16_theirs = swap(v16, OTHER_CORE)
+    def gradients(kernel, keep_and_send, pair, far, v16, v16_theirs):
+        (u,) = call(rows_kernel, [shape(half, R, BF)], [VMEM] * 4, (pair, *far), flops=LONG)
+        *outs, e, e_theirs = call(
+            kernel,
+            keep_and_send + [shape(half, n, BF)] * 2,
+            [VMEM] * 5,
+            (u, v16, v16_theirs, mine, theirs),
+            flops=flops,
         )
-        keep, *send, e_theirs = call(
-            theirs_kernel,
-            [shape(2 * own, R, F32)] + [shape(2 * own, R, BF)] * 3 + [shape(half, n, BF)],
-            [VMEM] * (3 + len(v16_theirs)),
-            (u, gu, theirs, *v16_theirs),
-            flops=flops // 2,
+        (gv,) = call(
+            ngram_send_kernel, [shape(n, R, BF)], [VMEM] * 2, (e_theirs, u), flops=flops // 4
         )
-        got = along_z(send)
-        gv_keep, gv_send = call(
-            ngram_kernel, ngram_grads, [VMEM] * 3, (e, e_theirs, u), flops=flops // 2
+        (ours,) = call(
+            ngram_keep_kernel,
+            [shape(n, R, BF)],
+            [VMEM] * 3,
+            (e, u, swap(gv, OTHER_CORE)),
+            flops=flops // 4,
         )
-        ours = (gv_keep + swap(gv_send, OTHER_CORE).astype(F32)).astype(BF)
-        return keep, got, ours, swap_group(ours)
-
-    keep, got, ours, ngram_got = gradients(pair, far, v16)
+        return *outs, ours, swap_group(ours)
+
+    keep, *send, ours, ngram_got = gradients(
+        near_first_kernel,
+        [shape(2 * own, R, F32)] + [shape(2 * own, R, BF)] * 3,
+        pair,
+        far,
+        v16,
+        v16_theirs,
+    )
+    got = exchange_near(send)
     total, total16 = call(
-        along_z_kernel,
+        near_sum_kernel,
         [shape(2 * own, R, F32), shape(2 * own, R, BF)],
         [VMEM] * 4,
         (keep, *got),
@@ -238,10 +264,9 @@
         functools.partial(pair_update_kernel, doc_rate),
         [shape(own, R, F32), shape(2 * own, R, BF)],
         [VMEM] * 4,
-        (doc_now, pair, total, swap(total16, ALONG_X)),
-        flops=LONG,
-    )
-    far = along_z([pair] * 3)
+        (doc_now, pair, total, swap(total16, FAR)),
+    )
+    far = exchange_near([pair] * 3)
     ngram_now, v16 = call(
         functools.partial(ngram_update_kernel, ngram_rate),
         [shape(n, R, F32), shape(n, R, BF)],
@@ -250,13 +275,28 @@
     )
     v16_theirs = swap(v16, OTHER_CORE)
 
-    keep, got, ours, ngram_got = gradients(pair, far, v16, v16_theirs)
-    for some in got:
-        keep = keep + some.astype(F32)
-    total = keep[:own] + swap(keep[own:].astype(BF), ALONG_X).astype(F32)
-    ngram_now = ngram_now - ngram_rate * (ours.astype(F32) + ngram_got.astype(F32))
-    doc_now = doc_now - doc_rate * total
-    return doc_now, ngram_now
+    keep, send, ours, ngram_got = gradients(
+        far_first_kernel,
+        [shape(half // 2, R, F32), shape(half // 2, R, BF)],
+        pair,
+        far,
+        v16,
+        v16_theirs,
+    )
+    total, *send = call(
+        far_sum_kernel,
+        [shape(own, R, F32)] + [shape(own, R, BF)] * 3,
+        [VMEM] * 2,
+        (keep, swap(send, FAR)),
+        flops=LONG,
+    )
+    return call(
+        functools.partial(last_kernel, doc_rate, ngram_rate),
+        [shape(own, R, F32), shape(n, R, F32)],
+        [VMEM] * 8,
+        (doc_now, total, *exchange_near(send), ours, ngram_got, ngram_now),
+        read=0,
+    )
 
 
 def plain_kernel(docs, ngrams, counts, pmi, weights, u, v, gu, gv, s, e):

time: 49.8 us -> 45.5 us (0.914)
  waiting for transfers between devices: 17 us -> 12.9 us
  starting transfers between devices: 23.3 us -> 25.2 us
  other arithmetic: 1.65 us -> 0 us
  Pallas kernels: 6.14 us -> 5.58 us
    ppermute x2, waiting for transfers between devices: 2.39 us -> 0.01 us  [swap_group(): return lax.ppermute(x, 'grp', [(0, 1), (1, 0)])]
    ppermute x19 -> x20, starting transfers between devices: 20.2 us -> 22 us  [swap(): lax.ppermute(x, 'col', [(i, i ^ mask) for i in range(lax.axis_size('col'))])]
    ppermute x19 -> x20, waiting for transfers between devices: 14.6 us -> 12.9 us  [swap(): lax.ppermute(x, 'col', [(i, i ^ mask) for i in range(lax.axis_size('col'))])]
    sub x2 -> x0, other arithmetic: 1.5 us -> none  [the longest x1 0.88 us: small_slice(): ngram_now - ngram_rate * (ours.astype(F32) + ngram_got.astype(F32))]
    pallas_call x11 -> x15, Pallas kernels: 6.14 us -> 5.58 us  [call(): pl.pallas_call(kernel, out_shape=outs, in_specs=in_specs, out_specs=[VMEM...]
  transfers between devices with their start and end apart: 21 -> 22, of which waited for: 11 -> 11; matrix products, arithmetic and copies ran while one was open for 2% -> 0% of each run, Pallas kernels for 10% -> 6%
where the time goes in v3:
time: 45.5 us; the launch traced here: 45.4 us
  starting transfers between devices  25.2 us (55%)
  waiting for transfers between devices  12.9 us (28%)
  Pallas kernels  5.58 us (12%)
  between operations  1.49 us (3%)
    ppermute x20, starting transfers between devices, swap(): lax.ppermute(x, 'col', [(i, i ^ mask) for i in range(lax.axis_size('col'))])  22 us
    ppermute x20, waiting for transfers between devices, swap(): lax.ppermute(x, 'col', [(i, i ^ mask) for i in range(lax.axis_size('col'))])  12.9 us
    pallas_call x15, Pallas kernels, call(): pl.pallas_call(kernel, out_shape=outs, in_specs=in_specs, out_specs=[VMEM...  5.58 us
    ppermute x2, starting transfers between devices, swap_group(): return lax.ppermute(x, 'grp', [(0, 1), (1, 0)])  3.17 us
  transfers between devices with their start and end apart: 22, of which 11 were waited for; matrix products, arithmetic and copies ran while one was open for 0% of the time, Pallas kernels for 6%

profile of v3, /device:TPU:0, one launch (start us, length us, event | category | flops | bytes accessed | tf_op | source)
XLA Modules:
  0.0 45.4 jit_solution(2817696993782793949)
XLA Ops:
  0.7 3.5 %collective-permute-start = (f32[32,256]{1,0:T(8,128)}, f32[32,256]{1,0:T(8,128)S(1)}, u32[]{:S(2)}, u32[]{:S(2)}) collective-permute-start(f32[32,256]{1,0:T(8,128)} %doc.1), channel_id=1, source_target_pairs={{0,9},{1,8},{2,11},{3,10},{4,13},{5,12},{6,15},{7,14},{8,1},{9,0},... | collective-permute-start | bytes 98312 | tf_op jit(solution)/shard_map/ppermute | solution.py:186
  4.9 2.2 %shard_map.86 = (bf16[512,512]{1,0:T(8,128)(2,1)S(1)}, bf16[512,512]{1,0:T(8,128)(2,1)S(1)}, bf16[512,256]{1,0:T(8,128)(2,1)S(1)}) custom-call(s32[1,1,16]{2,1,0:T(1,128)S(1)} %copy-done.4, s32[1,1,16]{2,1,0:T(1,128)S(1)} %copy-done.5, s32[1,1]{1,0:T(1,128)S(6)} %copy.9.counts, bf16[1,1,16,128,128]{4,3,2,1,0:T(8,128)(2,1)} %pmi_hbm.1, ...), custom_call_target="tpu_custom_call" | custom-call | bytes 1572996 | tf_op jit(solution)/shard_map/pallas_call | solution.py:35
  7.1 2.8 %collective-permute-start.3 = (bf16[64,256]{1,0:T(8,128)(2,1)S(1)}, bf16[64,256]{1,0:T(8,128)(2,1)S(1)}, u32[]{:S(2)}, u32[]{:S(2)}) collective-permute-start(bf16[64,256]{1,0:T(8,128)(2,1)S(1)} %shard_map.87.pair), channel_id=1, source_target_pairs={{0,7},{1,6},{2,5},{3,4},{4,3},{5,2},{6,1},{7,0},{8,15},{9,14},{10,... | collective-permute-start | bytes 98312 | tf_op jit(solution)/shard_map/ppermute | solution.py:186
  9.9 0.0 collective-permute-start.2
  9.9 0.7 %collective-permute-start.1 = (bf16[64,256]{1,0:T(8,128)(2,1)S(1)}, bf16[64,256]{1,0:T(8,128)(2,1)S(1)}, u32[]{:S(2)}, u32[]{:S(2)}) collective-permute-start(bf16[64,256]{1,0:T(8,128)(2,1)S(1)} %shard_map.87.pair), channel_id=1, source_target_pairs={{0,3},{1,2},{2,1},{3,0},{4,7},{5,6},{6,5},{7,4},{8,11},{9,10},{10,... | collective-permute-start | bytes 98312 | tf_op jit(solution)/shard_map/ppermute | solution.py:186
  10.6 0.1 collective-permute-start.4
  10.7 0.5 %collective-permute-start.5 = (bf16[512,512]{1,0:T(8,128)(2,1)S(1)}, bf16[512,512]{1,0:T(8,128)(2,1)S(1)}, u32[]{:S(2)}, u32[]{:S(2)}) collective-permute-start(bf16[512,512]{1,0:T(8,128)(2,1)S(1)} %get-tuple-element.31), channel_id=1, source_target_pairs={{0,1},{1,0},{2,3},{3,2},{4,5},{5,4},{6,7},{7,6},{8,9},{9,8},{10,11... | collective-permute-start | bytes 1572872 | tf_op jit(solution)/shard_map/ppermute | solution.py:186
  11.1 0.4 collective-permute-done.3.far3
  11.6 2.0 %collective-permute-done.2.far2 = bf16[64,256]{1,0:T(8,128)(2,1)S(1)} collective-permute-done((bf16[64,256]{1,0:T(8,128)(2,1)S(1)}, bf16[64,256]{1,0:T(8,128)(2,1)S(1)}, u32[]{:S(2)}, u32[]{:S(2)}) %collective-permute-start.2) | collective-permute-done | bytes 32800 | tf_op jit(solution)/shard_map/ppermute | solution.py:186
  13.6 0.0 collective-permute-done.4.v16_theirs
  13.6 0.0 copy-start.1
  13.7 0.6 %shard_map.89 = (f32[64,256]{1,0:T(8,128)S(1)}, bf16[64,256]{1,0:T(8,128)(2,1)S(1)}, bf16[64,256]{1,0:T(8,128)(2,1)S(1)}, bf16[64,256]{1,0:T(8,128)(2,1)S(1)}, b...) custom-call(bf16[256,256]{1,0:T(8,128)(2,1)S(1)} %shard_map.88.u, bf16[512,256]{1,0:T(8,128)(2,1)S(1)} %get-tuple-element.29.v16, ...), custom_call_target="tpu_custom_call" | custom-call | flops 268435456 | bytes 1703936 | tf_op jit(solution)/shard_map/pallas_call | solution.py:35
  14.3 0.1 copy-done.1
  14.4 0.3 shard_map.93
  14.7 0.3 collective-permute-start.13
  15.0 0.7 %collective-permute-start.6 = (bf16[64,256]{1,0:T(8,128)(2,1)S(1)}, bf16[64,256]{1,0:T(8,128)(2,1)S(1)}, u32[]{:S(2)}, u32[]{:S(2)}) collective-permute-start(bf16[64,256]{1,0:T(8,128)(2,1)S(1)} %get-tuple-element.33), channel_id=1, source_target_pairs={{0,3},{1,2},{2,1},{3,0},{4,7},{5,6},{6,5},{7,4},{8,11},{9,10},{10,... | collective-permute-start | bytes 98312 | tf_op jit(solution)/shard_map/ppermute | solution.py:186
  15.7 1.3 %collective-permute-start.7 = (bf16[64,256]{1,0:T(8,128)(2,1)S(1)}, bf16[64,256]{1,0:T(8,128)(2,1)S(1)}, u32[]{:S(2)}, u32[]{:S(2)}) collective-permute-start(bf16[64,256]{1,0:T(8,128)(2,1)S(1)} %get-tuple-element.34), channel_id=1, source_target_pairs={{0,5},{1,4},{2,7},{3,6},{4,1},{5,0},{6,3},{7,2},{8,13},{9,12},{10,... | collective-permute-start | bytes 98312 | tf_op jit(solution)/shard_map/ppermute | solution.py:186
  17.0 1.1 %collective-permute-start.8 = (bf16[64,256]{1,0:T(8,128)(2,1)S(1)}, bf16[64,256]{1,0:T(8,128)(2,1)S(1)}, u32[]{:S(2)}, u32[]{:S(2)}) collective-permute-start(bf16[64,256]{1,0:T(8,128)(2,1)S(1)} %get-tuple-element.35), channel_id=1, source_target_pairs={{0,7},{1,6},{2,5},{3,4},{4,3},{5,2},{6,1},{7,0},{8,15},{9,14},{10,... | collective-permute-start | bytes 98312 | tf_op jit(solution)/shard_map/ppermute | solution.py:186
  18.1 0.0 collective-permute-done.13.got
  18.1 0.3 shard_map.94.ours
  18.4 1.6 %collective-permute-start.14 = (bf16[512,256]{1,0:T(8,128)(2,1)S(1)}, bf16[512,256]{1,0:T(8,128)(2,1)S(1)}, u32[]{:S(2)}, u32[]{:S(2)}) collective-permute-start(bf16[512,256]{1,0:T(8,128)(2,1)S(1)} %shard_map.94.ours), channel_id=1, source_target_pairs={{0,16},{16,0},{1,17},{17,1},{2,18},{18,2},{3,19},{19,3},{4,20},{20... | collective-permute-start | bytes 786440 | tf_op jit(solution)/shard_map/ppermute | solution.py:195
  20.0 1.3 %collective-permute-done.8.got3 = bf16[64,256]{1,0:T(8,128)(2,1)S(1)} collective-permute-done((bf16[64,256]{1,0:T(8,128)(2,1)S(1)}, bf16[64,256]{1,0:T(8,128)(2,1)S(1)}, u32[]{:S(2)}, u32[]{:S(2)}) %collective-permute-start.8) | collective-permute-done | bytes 32800 | tf_op jit(solution)/shard_map/ppermute | solution.py:186
  21.3 2.7 %collective-permute-start.9 = (bf16[64,256]{1,0:T(8,128)(2,1)S(1)}, bf16[64,256]{1,0:T(8,128)(2,1)S(1)}, u32[]{:S(2)}, u32[]{:S(2)}) collective-permute-start(bf16[64,256]{1,0:T(8,128)(2,1)S(1)} %get-tuple-element.37), channel_id=1, source_target_pairs={{0,9},{1,8},{2,11},{3,10},{4,13},{5,12},{6,15},{7,14},{8,1},{9,0},... | collective-permute-start | bytes 98312 | tf_op jit(solution)/shard_map/ppermute | solution.py:186
  23.9 2.4 %collective-permute-done.9.got = bf16[64,256]{1,0:T(8,128)(2,1)S(1)} collective-permute-done((bf16[64,256]{1,0:T(8,128)(2,1)S(1)}, bf16[64,256]{1,0:T(8,128)(2,1)S(1)}, u32[]{:S(2)}, u32[]{:S(2)}) %collective-permute-start.9) | collective-permute-done | bytes 32800 | tf_op jit(solution)/shard_map/ppermute | solution.py:186
  26.3 0.4 collective-permute-start.12
  26.8 2.3 %collective-permute-start.11 = (bf16[64,256]{1,0:T(8,128)(2,1)S(1)}, bf16[64,256]{1,0:T(8,128)(2,1)S(1)}, u32[]{:S(2)}, u32[]{:S(2)}) collective-permute-start(bf16[64,256]{1,0:T(8,128)(2,1)S(1)} %get-tuple-element.39.pair.after), channel_id=1, source_target_pairs={{0,5},{1,4},{2,7},{3,6},{4,1},{5,0},{6,3},{7,2},{8,13},{9,12},{10,... | collective-permute-start | bytes 98312 | tf_op jit(solution)/shard_map/ppermute | solution.py:186
  29.0 0.3 collective-permute-start.10
  29.4 0.1 shard_map.95
  29.5 0.0 copy-start.2
  29.5 0.4 collective-permute-start.15
  29.9 0.7 %collective-permute-done.12.far3 = bf16[64,256]{1,0:T(8,128)(2,1)S(1)} collective-permute-done((bf16[64,256]{1,0:T(8,128)(2,1)S(1)}, bf16[64,256]{1,0:T(8,128)(2,1)S(1)}, u32[]{:S(2)}, u32[]{:S(2)}) %collective-permute-start.12) | collective-permute-done | bytes 32800 | tf_op jit(solution)/shard_map/ppermute | solution.py:186
  30.6 0.7 %collective-permute-done.11.far2 = bf16[64,256]{1,0:T(8,128)(2,1)S(1)} collective-permute-done((bf16[64,256]{1,0:T(8,128)(2,1)S(1)}, bf16[64,256]{1,0:T(8,128)(2,1)S(1)}, u32[]{:S(2)}, u32[]{:S(2)}) %collective-permute-start.11) | collective-permute-done | bytes 32800 | tf_op jit(solution)/shard_map/ppermute | solution.py:186
  31.3 1.1 %collective-permute-done.10.far1 = bf16[64,256]{1,0:T(8,128)(2,1)S(1)} collective-permute-done((bf16[64,256]{1,0:T(8,128)(2,1)S(1)}, bf16[64,256]{1,0:T(8,128)(2,1)S(1)}, u32[]{:S(2)}, u32[]{:S(2)}) %collective-permute-start.10) | collective-permute-done | bytes 32800 | tf_op jit(solution)/shard_map/ppermute | solution.py:186
  32.5 0.0 collective-permute-done.15.v16_theirs
  32.5 0.6 %shard_map.96 = (f32[128,256]{1,0:T(8,128)S(1)}, bf16[128,256]{1,0:T(8,128)(2,1)S(1)}, bf16[256,512]{1,0:T(8,128)(2,1)S(1)}, bf16[256,512]{1,0:T(8,128)(2,1)S(1)}) custom-call(bf16[256,256]{1,0:T(8,128)(2,1)S(1)} %shard_map.92.u, bf16[512,256]{1,0:T(8,128)(2,1)S(1)} %get-tuple-element.42.v16, bf16[512,256]{1,0:T(8,128)(2,1)S(1)} %collective-permute-done.15.v16_theirs, ...), custom_call_target="tpu_custom_call" | custom-call | flops 268435456 | bytes 1703936 | tf_op jit(solution)/shard_map/pallas_call | solution.py:35
  33.1 0.3 shard_map.98
  33.4 0.2 collective-permute-start.20
  33.6 1.7 %collective-permute-start.16 = (bf16[128,256]{1,0:T(8,128)(2,1)S(1)}, bf16[128,256]{1,0:T(8,128)(2,1)S(1)}, u32[]{:S(2)}, u32[]{:S(2)}) collective-permute-start(bf16[128,256]{1,0:T(8,128)(2,1)S(1)} %get-tuple-element.44), channel_id=1, source_target_pairs={{0,9},{1,8},{2,11},{3,10},{4,13},{5,12},{6,15},{7,14},{8,1},{9,0},... | collective-permute-start | bytes 196616 | tf_op jit(solution)/shard_map/ppermute | solution.py:186
  35.3 0.3 shard_map.99.ours
  35.6 1.6 %collective-permute-start.21 = (bf16[512,256]{1,0:T(8,128)(2,1)S(1)}, bf16[512,256]{1,0:T(8,128)(2,1)S(1)}, u32[]{:S(2)}, u32[]{:S(2)}) collective-permute-start(bf16[512,256]{1,0:T(8,128)(2,1)S(1)} %shard_map.99.ours), channel_id=1, source_target_pairs={{0,16},{16,0},{1,17},{17,1},{2,18},{18,2},{3,19},{19,3},{4,20},{20... | collective-permute-start | bytes 786440 | tf_op jit(solution)/shard_map/ppermute | solution.py:195
  37.2 2.7 %collective-permute-done.16.got = bf16[128,256]{1,0:T(8,128)(2,1)S(1)} collective-permute-done((bf16[128,256]{1,0:T(8,128)(2,1)S(1)}, bf16[128,256]{1,0:T(8,128)(2,1)S(1)}, u32[]{:S(2)}, u32[]{:S(2)}) %collective-permute-start.16) | collective-permute-done | bytes 65568 | tf_op jit(solution)/shard_map/ppermute | solution.py:186
  39.9 0.4 collective-permute-start.17
  40.3 2.6 %collective-permute-start.19 = (bf16[32,256]{1,0:T(8,128)(2,1)S(1)}, bf16[32,256]{1,0:T(8,128)(2,1)S(1)}, u32[]{:S(2)}, u32[]{:S(2)}) collective-permute-start(bf16[32,256]{1,0:T(8,128)(2,1)S(1)} %get-tuple-element.48), channel_id=1, source_target_pairs={{0,7},{1,6},{2,5},{3,4},{4,3},{5,2},{6,1},{7,0},{8,15},{9,14},{10,... | collective-permute-start | bytes 49160 | tf_op jit(solution)/shard_map/ppermute | solution.py:186
  42.9 0.2 collective-permute-done.17.got1
  43.1 0.3 collective-permute-done.18.got2
  43.4 1.0 %collective-permute-done.19.got3 = bf16[32,256]{1,0:T(8,128)(2,1)S(1)} collective-permute-done((bf16[32,256]{1,0:T(8,128)(2,1)S(1)}, bf16[32,256]{1,0:T(8,128)(2,1)S(1)}, u32[]{:S(2)}, u32[]{:S(2)}) %collective-permute-start.19) | collective-permute-done | bytes 16416 | tf_op jit(solution)/shard_map/ppermute | solution.py:186
  44.5 0.0 collective-permute-done.21.ngram_got
  44.5 0.9 %shard_map.100 = (f32[32,256]{1,0:T(8,128)}, f32[512,256]{1,0:T(8,128)}) custom-call(f32[32,256]{1,0:T(8,128)S(1)} %get-tuple-element.38.doc, f32[32,256]{1,0:T(8,128)S(1)} %get-tuple-element.45.total, bf16[32,256]{1,0:T(8,128)(2,1)S(1)} %collective-permute-done.17.got1, bf16[32,256]{1,0:T(8,128)(2,1)S(1)} %collective-permute-done.18.got2, ...), custom_call_target="tpu_custom_call" | custom-call | tf_op jit(solution)/shard_map/pallas_call | solution.py:35
  (23 shorter events, 0.1 us)
Async XLA Ops:
  0.6 4.2 %copy-start.5 = (s32[1,1,16]{2,1,0:T(1,128)S(1)}, s32[1,1,16]{2,1,0:T(1,128)}, u32[]{:S(2)}) copy-start(s32[1,1,16]{2,1,0:T(1,128)} %ngrams.1) | copy-start | bytes 196
  0.6 4.2 %copy-start.4 = (s32[1,1,16]{2,1,0:T(1,128)S(1)}, s32[1,1,16]{2,1,0:T(1,128)}, u32[]{:S(2)}) copy-start(s32[1,1,16]{2,1,0:T(1,128)} %docs.1) | copy-start | bytes 196
  0.7 6.4 %collective-permute-start = (f32[32,256]{1,0:T(8,128)}, f32[32,256]{1,0:T(8,128)S(1)}, u32[]{:S(2)}, u32[]{:S(2)}) collective-permute-start(f32[32,256]{1,0:T(8,128)} %doc.1), channel_id=1, source_target_pairs={{0,9},{1,8},{2,11},{3,10},{4,13},{5,12},{6,15},{7,14},{8,1},{9,0},... | collective-permute-start | bytes 98312 | tf_op jit(solution)/shard_map/ppermute | solution.py:186
  4.9 2.2 %copy-start.3 = (f32[32,256]{1,0:T(8,128)S(1)}, f32[32,256]{1,0:T(8,128)}, u32[]{:S(2)}) copy-start(f32[32,256]{1,0:T(8,128)} %doc.1) | copy-start | bytes 98308
  7.1 4.5 %collective-permute-start.3 = (bf16[64,256]{1,0:T(8,128)(2,1)S(1)}, bf16[64,256]{1,0:T(8,128)(2,1)S(1)}, u32[]{:S(2)}, u32[]{:S(2)}) collective-permute-start(bf16[64,256]{1,0:T(8,128)(2,1)S(1)} %shard_map.87.pair), channel_id=1, source_target_pairs={{0,7},{1,6},{2,5},{3,4},{4,3},{5,2},{6,1},{7,0},{8,15},{9,14},{10,... | collective-permute-start | bytes 98312 | tf_op jit(solution)/shard_map/ppermute | solution.py:186
  9.9 3.7 %collective-permute-start.2 = (bf16[64,256]{1,0:T(8,128)(2,1)S(1)}, bf16[64,256]{1,0:T(8,128)(2,1)S(1)}, u32[]{:S(2)}, u32[]{:S(2)}) collective-permute-start(bf16[64,256]{1,0:T(8,128)(2,1)S(1)} %shard_map.87.pair), channel_id=1, source_target_pairs={{0,5},{1,4},{2,7},{3,6},{4,1},{5,0},{6,3},{7,2},{8,13},{9,12},{10,... | collective-permute-start | bytes 98312 | tf_op jit(solution)/shard_map/ppermute | solution.py:186
  9.9 3.7 %collective-permute-start.1 = (bf16[64,256]{1,0:T(8,128)(2,1)S(1)}, bf16[64,256]{1,0:T(8,128)(2,1)S(1)}, u32[]{:S(2)}, u32[]{:S(2)}) collective-permute-start(bf16[64,256]{1,0:T(8,128)(2,1)S(1)} %shard_map.87.pair), channel_id=1, source_target_pairs={{0,3},{1,2},{2,1},{3,0},{4,7},{5,6},{6,5},{7,4},{8,11},{9,10},{10,... | collective-permute-start | bytes 98312 | tf_op jit(solution)/shard_map/ppermute | solution.py:186
  10.6 3.0 %collective-permute-start.4 = (bf16[512,256]{1,0:T(8,128)(2,1)S(1)}, bf16[512,256]{1,0:T(8,128)(2,1)S(1)}, u32[]{:S(2)}, u32[]{:S(2)}) collective-permute-start(bf16[512,256]{1,0:T(8,128)(2,1)S(1)} %get-tuple-element.29.v16), channel_id=1, source_target_pairs={{0,1},{1,0},{2,3},{3,2},{4,5},{5,4},{6,7},{7,6},{8,9},{9,8},{10,11... | collective-permute-start | bytes 786440 | tf_op jit(solution)/shard_map/ppermute | solution.py:186
  10.7 2.9 %collective-permute-start.5 = (bf16[512,512]{1,0:T(8,128)(2,1)S(1)}, bf16[512,512]{1,0:T(8,128)(2,1)S(1)}, u32[]{:S(2)}, u32[]{:S(2)}) collective-permute-start(bf16[512,512]{1,0:T(8,128)(2,1)S(1)} %get-tuple-element.31), channel_id=1, source_target_pairs={{0,1},{1,0},{2,3},{3,2},{4,5},{5,4},{6,7},{7,6},{8,9},{9,8},{10,11... | collective-permute-start | bytes 1572872 | tf_op jit(solution)/shard_map/ppermute | solution.py:186
  13.6 0.8 %copy-start.1 = (bf16[512,512]{1,0:T(8,128)(2,1)}, bf16[512,512]{1,0:T(8,128)(2,1)S(1)}, u32[]{:S(2)}) copy-start(bf16[512,512]{1,0:T(8,128)(2,1)S(1)} %collective-permute-done.5.theirs) | copy-start | bytes 1572868
  14.7 3.4 %collective-permute-start.13 = (bf16[512,256]{1,0:T(8,128)(2,1)S(1)}, bf16[512,256]{1,0:T(8,128)(2,1)S(1)}, u32[]{:S(2)}, u32[]{:S(2)}) collective-permute-start(bf16[512,256]{1,0:T(8,128)(2,1)S(1)} %shard_map.93), channel_id=1, source_target_pairs={{0,1},{1,0},{2,3},{3,2},{4,5},{5,4},{6,7},{7,6},{8,9},{9,8},{10,11... | collective-permute-start | bytes 786440 | tf_op jit(solution)/shard_map/ppermute | solution.py:186
  15.0 5.0 %collective-permute-start.6 = (bf16[64,256]{1,0:T(8,128)(2,1)S(1)}, bf16[64,256]{1,0:T(8,128)(2,1)S(1)}, u32[]{:S(2)}, u32[]{:S(2)}) collective-permute-start(bf16[64,256]{1,0:T(8,128)(2,1)S(1)} %get-tuple-element.33), channel_id=1, source_target_pairs={{0,3},{1,2},{2,1},{3,0},{4,7},{5,6},{6,5},{7,4},{8,11},{9,10},{10,... | collective-permute-start | bytes 98312 | tf_op jit(solution)/shard_map/ppermute | solution.py:186
  15.7 4.3 %collective-permute-start.7 = (bf16[64,256]{1,0:T(8,128)(2,1)S(1)}, bf16[64,256]{1,0:T(8,128)(2,1)S(1)}, u32[]{:S(2)}, u32[]{:S(2)}) collective-permute-start(bf16[64,256]{1,0:T(8,128)(2,1)S(1)} %get-tuple-element.34), channel_id=1, source_target_pairs={{0,5},{1,4},{2,7},{3,6},{4,1},{5,0},{6,3},{7,2},{8,13},{9,12},{10,... | collective-permute-start | bytes 98312 | tf_op jit(solution)/shard_map/ppermute | solution.py:186
  17.0 4.3 %collective-permute-start.8 = (bf16[64,256]{1,0:T(8,128)(2,1)S(1)}, bf16[64,256]{1,0:T(8,128)(2,1)S(1)}, u32[]{:S(2)}, u32[]{:S(2)}) collective-permute-start(bf16[64,256]{1,0:T(8,128)(2,1)S(1)} %get-tuple-element.35), channel_id=1, source_target_pairs={{0,7},{1,6},{2,5},{3,4},{4,3},{5,2},{6,1},{7,0},{8,15},{9,14},{10,... | collective-permute-start | bytes 98312 | tf_op jit(solution)/shard_map/ppermute | solution.py:186
  18.4 11.0 %collective-permute-start.14 = (bf16[512,256]{1,0:T(8,128)(2,1)S(1)}, bf16[512,256]{1,0:T(8,128)(2,1)S(1)}, u32[]{:S(2)}, u32[]{:S(2)}) collective-permute-start(bf16[512,256]{1,0:T(8,128)(2,1)S(1)} %shard_map.94.ours), channel_id=1, source_target_pairs={{0,16},{16,0},{1,17},{17,1},{2,18},{18,2},{3,19},{19,3},{4,20},{20... | collective-permute-start | bytes 786440 | tf_op jit(solution)/shard_map/ppermute | solution.py:195
  21.2 8.1 %copy-start = (f32[512,256]{1,0:T(8,128)S(1)}, f32[512,256]{1,0:T(8,128)}, u32[]{:S(2)}) copy-start(f32[512,256]{1,0:T(8,128)} %v.1) | copy-start | bytes 1572868
  21.3 5.0 %collective-permute-start.9 = (bf16[64,256]{1,0:T(8,128)(2,1)S(1)}, bf16[64,256]{1,0:T(8,128)(2,1)S(1)}, u32[]{:S(2)}, u32[]{:S(2)}) collective-permute-start(bf16[64,256]{1,0:T(8,128)(2,1)S(1)} %get-tuple-element.37), channel_id=1, source_target_pairs={{0,9},{1,8},{2,11},{3,10},{4,13},{5,12},{6,15},{7,14},{8,1},{9,0},... | collective-permute-start | bytes 98312 | tf_op jit(solution)/shard_map/ppermute | solution.py:186
  26.3 4.3 %collective-permute-start.12 = (bf16[64,256]{1,0:T(8,128)(2,1)S(1)}, bf16[64,256]{1,0:T(8,128)(2,1)S(1)}, u32[]{:S(2)}, u32[]{:S(2)}) collective-permute-start(bf16[64,256]{1,0:T(8,128)(2,1)S(1)} %get-tuple-element.39.pair.after), channel_id=1, source_target_pairs={{0,7},{1,6},{2,5},{3,4},{4,3},{5,2},{6,1},{7,0},{8,15},{9,14},{10,... | collective-permute-start | bytes 98312 | tf_op jit(solution)/shard_map/ppermute | solution.py:186
  26.8 4.6 %collective-permute-start.11 = (bf16[64,256]{1,0:T(8,128)(2,1)S(1)}, bf16[64,256]{1,0:T(8,128)(2,1)S(1)}, u32[]{:S(2)}, u32[]{:S(2)}) collective-permute-start(bf16[64,256]{1,0:T(8,128)(2,1)S(1)} %get-tuple-element.39.pair.after), channel_id=1, source_target_pairs={{0,5},{1,4},{2,7},{3,6},{4,1},{5,0},{6,3},{7,2},{8,13},{9,12},{10,... | collective-permute-start | bytes 98312 | tf_op jit(solution)/shard_map/ppermute | solution.py:186
  29.0 3.4 %collective-permute-start.10 = (bf16[64,256]{1,0:T(8,128)(2,1)S(1)}, bf16[64,256]{1,0:T(8,128)(2,1)S(1)}, u32[]{:S(2)}, u32[]{:S(2)}) collective-permute-start(bf16[64,256]{1,0:T(8,128)(2,1)S(1)} %get-tuple-element.39.pair.after), channel_id=1, source_target_pairs={{0,3},{1,2},{2,1},{3,0},{4,7},{5,6},{6,5},{7,4},{8,11},{9,10},{10,... | collective-permute-start | bytes 98312 | tf_op jit(solution)/shard_map/ppermute | solution.py:186
  29.5 3.0 %copy-start.2 = (bf16[512,512]{1,0:T(8,128)(2,1)S(1)}, bf16[512,512]{1,0:T(8,128)(2,1)}, u32[]{:S(2)}) copy-start(bf16[512,512]{1,0:T(8,128)(2,1)} %copy-done.1) | copy-start | bytes 1572868
  29.5 3.0 %collective-permute-start.15 = (bf16[512,256]{1,0:T(8,128)(2,1)S(1)}, bf16[512,256]{1,0:T(8,128)(2,1)S(1)}, u32[]{:S(2)}, u32[]{:S(2)}) collective-permute-start(bf16[512,256]{1,0:T(8,128)(2,1)S(1)} %get-tuple-element.42.v16), channel_id=1, source_target_pairs={{0,1},{1,0},{2,3},{3,2},{4,5},{5,4},{6,7},{7,6},{8,9},{9,8},{10,11... | collective-permute-start | bytes 786440 | tf_op jit(solution)/shard_map/ppermute | solution.py:186
  33.4 1.9 %collective-permute-start.20 = (bf16[512,256]{1,0:T(8,128)(2,1)S(1)}, bf16[512,256]{1,0:T(8,128)(2,1)S(1)}, u32[]{:S(2)}, u32[]{:S(2)}) collective-permute-start(bf16[512,256]{1,0:T(8,128)(2,1)S(1)} %shard_map.98), channel_id=1, source_target_pairs={{0,1},{1,0},{2,3},{3,2},{4,5},{5,4},{6,7},{7,6},{8,9},{9,8},{10,11... | collective-permute-start | bytes 786440 | tf_op jit(solution)/shard_map/ppermute | solution.py:186
  33.6 6.3 %collective-permute-start.16 = (bf16[128,256]{1,0:T(8,128)(2,1)S(1)}, bf16[128,256]{1,0:T(8,128)(2,1)S(1)}, u32[]{:S(2)}, u32[]{:S(2)}) collective-permute-start(bf16[128,256]{1,0:T(8,128)(2,1)S(1)} %get-tuple-element.44), channel_id=1, source_target_pairs={{0,9},{1,8},{2,11},{3,10},{4,13},{5,12},{6,15},{7,14},{8,1},{9,0},... | collective-permute-start | bytes 196616 | tf_op jit(solution)/shard_map/ppermute | solution.py:186
  35.6 8.9 %collective-permute-start.21 = (bf16[512,256]{1,0:T(8,128)(2,1)S(1)}, bf16[512,256]{1,0:T(8,128)(2,1)S(1)}, u32[]{:S(2)}, u32[]{:S(2)}) collective-permute-start(bf16[512,256]{1,0:T(8,128)(2,1)S(1)} %shard_map.99.ours), channel_id=1, source_target_pairs={{0,16},{16,0},{1,17},{17,1},{2,18},{18,2},{3,19},{19,3},{4,20},{20... | collective-permute-start | bytes 786440 | tf_op jit(solution)/shard_map/ppermute | solution.py:195
  39.9 3.2 %collective-permute-start.17 = (bf16[32,256]{1,0:T(8,128)(2,1)S(1)}, bf16[32,256]{1,0:T(8,128)(2,1)S(1)}, u32[]{:S(2)}, u32[]{:S(2)}) collective-permute-start(bf16[32,256]{1,0:T(8,128)(2,1)S(1)} %get-tuple-element.46), channel_id=1, source_target_pairs={{0,3},{1,2},{2,1},{3,0},{4,7},{5,6},{6,5},{7,4},{8,11},{9,10},{10,... | collective-permute-start | bytes 49160 | tf_op jit(solution)/shard_map/ppermute | solution.py:186
  40.3 3.2 %collective-permute-start.18 = (bf16[32,256]{1,0:T(8,128)(2,1)S(1)}, bf16[32,256]{1,0:T(8,128)(2,1)S(1)}, u32[]{:S(2)}, u32[]{:S(2)}) collective-permute-start(bf16[32,256]{1,0:T(8,128)(2,1)S(1)} %get-tuple-element.47), channel_id=1, source_target_pairs={{0,5},{1,4},{2,7},{3,6},{4,1},{5,0},{6,3},{7,2},{8,13},{9,12},{10,... | collective-permute-start | bytes 49160 | tf_op jit(solution)/shard_map/ppermute | solution.py:186
  40.3 4.2 %collective-permute-start.19 = (bf16[32,256]{1,0:T(8,128)(2,1)S(1)}, bf16[32,256]{1,0:T(8,128)(2,1)S(1)}, u32[]{:S(2)}, u32[]{:S(2)}) collective-permute-start(bf16[32,256]{1,0:T(8,128)(2,1)S(1)} %get-tuple-element.48), channel_id=1, source_target_pairs={{0,7},{1,6},{2,5},{3,4},{4,3},{5,2},{6,1},{7,0},{8,15},{9,14},{10,... | collective-permute-start | bytes 49160 | tf_op jit(solution)/shard_map/ppermute | solution.py:186

commit v4 on v3

--- a/solution.py
+++ b/solution.py
@@ -116,30 +116,30 @@
             u[at : at + own, :] = far[x * own : (x + 1) * own, :]
 
 
-def all_gu(u, v16, v16_theirs, mine, theirs, e, e_theirs):
+def all_gu(u, v16, v16_theirs, mine, theirs, e, gv_send, e_theirs):
     n = v16.shape[0] // 2
     gu = errors_and_gu(u[...], [v16[:n], v16[n:]], mine, e)
-    return gu + errors_and_gu(u[...], [v16_theirs[:n], v16_theirs[n:]], theirs, e_theirs)
-
-
-def near_first_kernel(u, v16, v16_theirs, mine, theirs, keep, send1, send2, send3, e, e_theirs):
+    gu = gu + errors_and_gu(u[...], [v16_theirs[:n], v16_theirs[n:]], theirs, e_theirs)
+    gv_send[...] = dot(e_theirs[...], u[...], ((0,), (0,))).astype(BF)
+    return gu
+
+
+def near_first_kernel(u, *refs):
+    *tiles, keep, send1, send2, send3, e, gv_send, e_theirs = refs
     own = u.shape[0] // 8
-    gu = all_gu(u, v16, v16_theirs, mine, theirs, e, e_theirs)
+    gu = all_gu(u, *tiles, e, gv_send, e_theirs)
     for z, out in enumerate((keep, send1, send2, send3)):
         for x in range(2):
             at = (x * 4 + z) * own
             out[x * own : (x + 1) * own, :] = gu[at : at + own].astype(out.dtype)
 
 
-def far_first_kernel(u, v16, v16_theirs, mine, theirs, keep, send, e, e_theirs):
+def far_first_kernel(u, *refs):
+    *tiles, keep, send, e, gv_send, e_theirs = refs
     n = keep.shape[0]
-    gu = all_gu(u, v16, v16_theirs, mine, theirs, e, e_theirs)
+    gu = all_gu(u, *tiles, e, gv_send, e_theirs)
     keep[...] = gu[:n]
     send[...] = gu[n:].astype(BF)
-
-
-def ngram_send_kernel(e_theirs, u, send):
-    send[...] = dot(e_theirs[...], u[...], ((0,), (0,))).astype(BF)
 
 
 def ngram_keep_kernel(e, u, got, ours):
@@ -225,15 +225,13 @@
     v16_theirs = swap(v16, OTHER_CORE)
     def gradients(kernel, keep_and_send, pair, far, v16, v16_theirs):
         (u,) = call(rows_kernel, [shape(half, R, BF)], [VMEM] * 4, (pair, *far), flops=LONG)
-        *outs, e, e_theirs = call(
+        *outs, e, gv = call(
             kernel,
-            keep_and_send + [shape(half, n, BF)] * 2,
+            keep_and_send + [shape(half, n, BF), shape(n, R, BF)],
             [VMEM] * 5,
             (u, v16, v16_theirs, mine, theirs),
+            [pltpu.VMEM((half, n), BF)],
             flops=flops,
-        )
-        (gv,) = call(
-            ngram_send_kernel, [shape(n, R, BF)], [VMEM] * 2, (e_theirs, u), flops=flops // 4
         )
         (ours,) = call(
             ngram_keep_kernel,
@@ -257,7 +255,7 @@
         near_sum_kernel,
         [shape(2 * own, R, F32), shape(2 * own, R, BF)],
         [VMEM] * 4,
-        (keep, *got),
+        (keep, *got[::-1]),
         flops=LONG,
     )
     doc_now, pair = call(
@@ -294,7 +292,7 @@
         functools.partial(last_kernel, doc_rate, ngram_rate),
         [shape(own, R, F32), shape(n, R, F32)],
         [VMEM] * 8,
-        (doc_now, total, *exchange_near(send), ours, ngram_got, ngram_now),
+        (doc_now, total, *exchange_near(send)[::-1], ours, ngram_got, ngram_now),
         read=0,
     )
 

time: 45.5 us -> 43.9 us (0.965)
  waiting for transfers between devices: 12.9 us -> 9.96 us
  starting transfers between devices: 25.2 us -> 27.1 us
  Pallas kernels: 5.58 us -> 5.06 us
    ppermute x20, waiting for transfers between devices: 12.9 us -> 9.17 us  [swap(): lax.ppermute(x, 'col', [(i, i ^ mask) for i in range(lax.axis_size('col'))])]
    ppermute x20, starting transfers between devices: 22 us -> 23.9 us  [swap(): lax.ppermute(x, 'col', [(i, i ^ mask) for i in range(lax.axis_size('col'))])]
    ppermute x2, waiting for transfers between devices: 0.01 us -> 0.79 us  [swap_group(): return lax.ppermute(x, 'grp', [(0, 1), (1, 0)])]
    pallas_call x15 -> x13, Pallas kernels: 5.58 us -> 5.06 us  [call(): pl.pallas_call(kernel, out_shape=outs, in_specs=in_specs, out_specs=[VMEM...]
  transfers between devices with their start and end apart: 22 -> 22, of which waited for: 11 -> 12; matrix products, arithmetic and copies ran while one was open for 0% -> 0% of each run, Pallas kernels for 6% -> 7%
where the time goes in v4:
time: 43.9 us; the launch traced here: 43.7 us
  starting transfers between devices  27.1 us (62%)
  waiting for transfers between devices  9.96 us (23%)
  Pallas kernels  5.06 us (12%)
  between operations  1.47 us (3%)
    ppermute x20, starting transfers between devices, swap(): lax.ppermute(x, 'col', [(i, i ^ mask) for i in range(lax.axis_size('col'))])  23.9 us
    ppermute x20, waiting for transfers between devices, swap(): lax.ppermute(x, 'col', [(i, i ^ mask) for i in range(lax.axis_size('col'))])  9.17 us
    pallas_call x13, Pallas kernels, call(): pl.pallas_call(kernel, out_shape=outs, in_specs=in_specs, out_specs=[VMEM...  5.06 us
    ppermute x2, starting transfers between devices, swap_group(): return lax.ppermute(x, 'grp', [(0, 1), (1, 0)])  3.17 us
  transfers between devices with their start and end apart: 22, of which 12 were waited for; matrix products, arithmetic and copies ran while one was open for 0% of the time, Pallas kernels for 7%

profile of v4, /device:TPU:0, one launch (start us, length us, event | category | flops | bytes accessed | tf_op | source)
XLA Modules:
  0.0 43.7 jit_solution(1178522376451827724)
XLA Ops:
  0.7 3.5 %collective-permute-start = (f32[32,256]{1,0:T(8,128)}, f32[32,256]{1,0:T(8,128)S(1)}, u32[]{:S(2)}, u32[]{:S(2)}) collective-permute-start(f32[32,256]{1,0:T(8,128)} %doc.1), channel_id=1, source_target_pairs={{0,9},{1,8},{2,11},{3,10},{4,13},{5,12},{6,15},{7,14},{8,1},{9,0},... | collective-permute-start | bytes 98312 | tf_op jit(solution)/shard_map/ppermute | solution.py:186
  4.9 2.2 %shard_map.86 = (bf16[512,512]{1,0:T(8,128)(2,1)S(1)}, bf16[512,512]{1,0:T(8,128)(2,1)S(1)}, bf16[512,256]{1,0:T(8,128)(2,1)S(1)}) custom-call(s32[1,1,16]{2,1,0:T(1,128)S(1)} %copy-done.4, s32[1,1,16]{2,1,0:T(1,128)S(1)} %copy-done.5, s32[1,1]{1,0:T(1,128)S(6)} %copy.9.counts, bf16[1,1,16,128,128]{4,3,2,1,0:T(8,128)(2,1)} %pmi_hbm.1, ...), custom_call_target="tpu_custom_call" | custom-call | bytes 1572996 | tf_op jit(solution)/shard_map/pallas_call | solution.py:35
  7.0 0.0 collective-permute-done.other
  7.1 2.8 %collective-permute-start.3 = (bf16[64,256]{1,0:T(8,128)(2,1)S(1)}, bf16[64,256]{1,0:T(8,128)(2,1)S(1)}, u32[]{:S(2)}, u32[]{:S(2)}) collective-permute-start(bf16[64,256]{1,0:T(8,128)(2,1)S(1)} %shard_map.87.pair), channel_id=1, source_target_pairs={{0,7},{1,6},{2,5},{3,4},{4,3},{5,2},{6,1},{7,0},{8,15},{9,14},{10,... | collective-permute-start | bytes 98312 | tf_op jit(solution)/shard_map/ppermute | solution.py:186
  9.9 0.0 collective-permute-start.2
  9.9 0.7 %collective-permute-start.1 = (bf16[64,256]{1,0:T(8,128)(2,1)S(1)}, bf16[64,256]{1,0:T(8,128)(2,1)S(1)}, u32[]{:S(2)}, u32[]{:S(2)}) collective-permute-start(bf16[64,256]{1,0:T(8,128)(2,1)S(1)} %shard_map.87.pair), channel_id=1, source_target_pairs={{0,3},{1,2},{2,1},{3,0},{4,7},{5,6},{6,5},{7,4},{8,11},{9,10},{10,... | collective-permute-start | bytes 98312 | tf_op jit(solution)/shard_map/ppermute | solution.py:186
  10.6 0.1 collective-permute-start.4
  10.7 0.5 %collective-permute-start.5 = (bf16[512,512]{1,0:T(8,128)(2,1)S(1)}, bf16[512,512]{1,0:T(8,128)(2,1)S(1)}, u32[]{:S(2)}, u32[]{:S(2)}) collective-permute-start(bf16[512,512]{1,0:T(8,128)(2,1)S(1)} %get-tuple-element.31), channel_id=1, source_target_pairs={{0,1},{1,0},{2,3},{3,2},{4,5},{5,4},{6,7},{7,6},{8,9},{9,8},{10,11... | collective-permute-start | bytes 1572872 | tf_op jit(solution)/shard_map/ppermute | solution.py:186
  11.1 0.4 %collective-permute-done.3.far3 = bf16[64,256]{1,0:T(8,128)(2,1)S(1)} collective-permute-done((bf16[64,256]{1,0:T(8,128)(2,1)S(1)}, bf16[64,256]{1,0:T(8,128)(2,1)S(1)}, u32[]{:S(2)}, u32[]{:S(2)}) %collective-permute-start.3) | collective-permute-done | bytes 32800 | tf_op jit(solution)/shard_map/ppermute | solution.py:186
  11.6 2.0 %collective-permute-done.2.far2 = bf16[64,256]{1,0:T(8,128)(2,1)S(1)} collective-permute-done((bf16[64,256]{1,0:T(8,128)(2,1)S(1)}, bf16[64,256]{1,0:T(8,128)(2,1)S(1)}, u32[]{:S(2)}, u32[]{:S(2)}) %collective-permute-start.2) | collective-permute-done | bytes 32800 | tf_op jit(solution)/shard_map/ppermute | solution.py:186
  13.6 0.0 collective-permute-done.1.far1
  13.6 0.0 collective-permute-done.4.refs_1_
  13.6 0.0 copy-start.1
  13.7 0.7 %shard_map.89 = (f32[64,256]{1,0:T(8,128)S(1)}, bf16[64,256]{1,0:T(8,128)(2,1)S(1)}, bf16[64,256]{1,0:T(8,128)(2,1)S(1)}, bf16[64,256]{1,0:T(8,128)(2,1)S(1)}, b...) custom-call(bf16[256,256]{1,0:T(8,128)(2,1)S(1)} %shard_map.88.u, ...), custom_call_target="tpu_custom_call" | custom-call | flops 268435456 | bytes 1703936 | tf_op jit(solution)/shard_map/pallas_call | solution.py:35
  14.3 0.1 copy-done.1
  14.4 0.2 collective-permute-start.13
  14.7 1.7 %collective-permute-start.6 = (bf16[64,256]{1,0:T(8,128)(2,1)S(1)}, bf16[64,256]{1,0:T(8,128)(2,1)S(1)}, u32[]{:S(2)}, u32[]{:S(2)}) collective-permute-start(bf16[64,256]{1,0:T(8,128)(2,1)S(1)} %get-tuple-element.33), channel_id=1, source_target_pairs={{0,7},{1,6},{2,5},{3,4},{4,3},{5,2},{6,1},{7,0},{8,15},{9,14},{10,... | collective-permute-start | bytes 98312 | tf_op jit(solution)/shard_map/ppermute | solution.py:186
  16.3 0.2 collective-permute-start.7
  16.5 1.2 %collective-permute-start.8 = (bf16[64,256]{1,0:T(8,128)(2,1)S(1)}, bf16[64,256]{1,0:T(8,128)(2,1)S(1)}, u32[]{:S(2)}, u32[]{:S(2)}) collective-permute-start(bf16[64,256]{1,0:T(8,128)(2,1)S(1)} %get-tuple-element.35), channel_id=1, source_target_pairs={{0,3},{1,2},{2,1},{3,0},{4,7},{5,6},{6,5},{7,4},{8,11},{9,10},{10,... | collective-permute-start | bytes 98312 | tf_op jit(solution)/shard_map/ppermute | solution.py:186
  17.8 0.0 collective-permute-done.13.got
  17.8 0.3 shard_map.93.ours
  18.0 1.6 %collective-permute-start.14 = (bf16[512,256]{1,0:T(8,128)(2,1)S(1)}, bf16[512,256]{1,0:T(8,128)(2,1)S(1)}, u32[]{:S(2)}, u32[]{:S(2)}) collective-permute-start(bf16[512,256]{1,0:T(8,128)(2,1)S(1)} %shard_map.93.ours), channel_id=1, source_target_pairs={{0,16},{16,0},{1,17},{17,1},{2,18},{18,2},{3,19},{19,3},{4,20},{20... | collective-permute-start | bytes 786440 | tf_op jit(solution)/shard_map/ppermute | solution.py:195
  19.6 0.1 collective-permute-done.7.got2
  19.7 0.2 collective-permute-done.8.got3
  19.9 2.4 %collective-permute-start.9 = (bf16[64,256]{1,0:T(8,128)(2,1)S(1)}, bf16[64,256]{1,0:T(8,128)(2,1)S(1)}, u32[]{:S(2)}, u32[]{:S(2)}) collective-permute-start(bf16[64,256]{1,0:T(8,128)(2,1)S(1)} %get-tuple-element.37), channel_id=1, source_target_pairs={{0,9},{1,8},{2,11},{3,10},{4,13},{5,12},{6,15},{7,14},{8,1},{9,0},... | collective-permute-start | bytes 98312 | tf_op jit(solution)/shard_map/ppermute | solution.py:186
  22.3 1.9 %collective-permute-done.9.got = bf16[64,256]{1,0:T(8,128)(2,1)S(1)} collective-permute-done((bf16[64,256]{1,0:T(8,128)(2,1)S(1)}, bf16[64,256]{1,0:T(8,128)(2,1)S(1)}, u32[]{:S(2)}, u32[]{:S(2)}) %collective-permute-start.9) | collective-permute-done | bytes 32800 | tf_op jit(solution)/shard_map/ppermute | solution.py:186
  24.2 2.3 %collective-permute-start.12 = (bf16[64,256]{1,0:T(8,128)(2,1)S(1)}, bf16[64,256]{1,0:T(8,128)(2,1)S(1)}, u32[]{:S(2)}, u32[]{:S(2)}) collective-permute-start(bf16[64,256]{1,0:T(8,128)(2,1)S(1)} %get-tuple-element.39.pair.after), channel_id=1, source_target_pairs={{0,7},{1,6},{2,5},{3,4},{4,3},{5,2},{6,1},{7,0},{8,15},{9,14},{10,... | collective-permute-start | bytes 98312 | tf_op jit(solution)/shard_map/ppermute | solution.py:186
  26.6 0.2 collective-permute-start.11
  26.8 0.7 %collective-permute-start.10 = (bf16[64,256]{1,0:T(8,128)(2,1)S(1)}, bf16[64,256]{1,0:T(8,128)(2,1)S(1)}, u32[]{:S(2)}, u32[]{:S(2)}) collective-permute-start(bf16[64,256]{1,0:T(8,128)(2,1)S(1)} %get-tuple-element.39.pair.after), channel_id=1, source_target_pairs={{0,3},{1,2},{2,1},{3,0},{4,7},{5,6},{6,5},{7,4},{8,11},{9,10},{10,... | collective-permute-start | bytes 98312 | tf_op jit(solution)/shard_map/ppermute | solution.py:186
  27.5 0.1 shard_map.94
  27.6 0.0 copy-start.2
  27.6 0.2 collective-permute-start.15
  27.8 0.7 %collective-permute-done.12.far3 = bf16[64,256]{1,0:T(8,128)(2,1)S(1)} collective-permute-done((bf16[64,256]{1,0:T(8,128)(2,1)S(1)}, bf16[64,256]{1,0:T(8,128)(2,1)S(1)}, u32[]{:S(2)}, u32[]{:S(2)}) %collective-permute-start.12) | collective-permute-done | bytes 32800 | tf_op jit(solution)/shard_map/ppermute | solution.py:186
  28.5 1.4 %collective-permute-done.11.far2 = bf16[64,256]{1,0:T(8,128)(2,1)S(1)} collective-permute-done((bf16[64,256]{1,0:T(8,128)(2,1)S(1)}, bf16[64,256]{1,0:T(8,128)(2,1)S(1)}, u32[]{:S(2)}, u32[]{:S(2)}) %collective-permute-start.11) | collective-permute-done | bytes 32800 | tf_op jit(solution)/shard_map/ppermute | solution.py:186
  29.9 0.2 collective-permute-done.10.far1
  30.2 0.7 %shard_map.95 = (f32[128,256]{1,0:T(8,128)S(1)}, bf16[128,256]{1,0:T(8,128)(2,1)S(1)}, bf16[256,512]{1,0:T(8,128)(2,1)S(1)}, bf16[512,256]{1,0:T(8,128)(2,1)S(1)}) custom-call(bf16[256,256]{1,0:T(8,128)(2,1)S(1)} %shard_map.92.u, bf16[512,256]{1,0:T(8,128)(2,1)S(1)} %get-tuple-element.42.refs_0_, bf16[512,256]{1,0:T(8,128)(2,1)S(1)} %collective-permute-done.15.refs_1_, ...), custom_call_target="tpu_custom_call" | custom-call | flops 268435456 | bytes 1703936 | tf_op jit(solution)/shard_map/pallas_call | solution.py:35
  30.8 0.3 collective-permute-start.20
  31.2 2.7 %collective-permute-start.16 = (bf16[128,256]{1,0:T(8,128)(2,1)S(1)}, bf16[128,256]{1,0:T(8,128)(2,1)S(1)}, u32[]{:S(2)}, u32[]{:S(2)}) collective-permute-start(bf16[128,256]{1,0:T(8,128)(2,1)S(1)} %get-tuple-element.44), channel_id=1, source_target_pairs={{0,9},{1,8},{2,11},{3,10},{4,13},{5,12},{6,15},{7,14},{8,1},{9,0},... | collective-permute-start | bytes 196616 | tf_op jit(solution)/shard_map/ppermute | solution.py:186
  33.9 0.3 shard_map.97.ours
  34.1 1.6 %collective-permute-start.21 = (bf16[512,256]{1,0:T(8,128)(2,1)S(1)}, bf16[512,256]{1,0:T(8,128)(2,1)S(1)}, u32[]{:S(2)}, u32[]{:S(2)}) collective-permute-start(bf16[512,256]{1,0:T(8,128)(2,1)S(1)} %shard_map.97.ours), channel_id=1, source_target_pairs={{0,16},{16,0},{1,17},{17,1},{2,18},{18,2},{3,19},{19,3},{4,20},{20... | collective-permute-start | bytes 786440 | tf_op jit(solution)/shard_map/ppermute | solution.py:195
  35.7 0.4 collective-permute-done.16.got
  36.1 2.8 %collective-permute-start.17 = (bf16[32,256]{1,0:T(8,128)(2,1)S(1)}, bf16[32,256]{1,0:T(8,128)(2,1)S(1)}, u32[]{:S(2)}, u32[]{:S(2)}) collective-permute-start(bf16[32,256]{1,0:T(8,128)(2,1)S(1)} %get-tuple-element.46), channel_id=1, source_target_pairs={{0,7},{1,6},{2,5},{3,4},{4,3},{5,2},{6,1},{7,0},{8,15},{9,14},{10,... | collective-permute-start | bytes 49160 | tf_op jit(solution)/shard_map/ppermute | solution.py:186
  38.9 0.0 collective-permute-start.18
  38.9 1.3 %collective-permute-start.19 = (bf16[32,256]{1,0:T(8,128)(2,1)S(1)}, bf16[32,256]{1,0:T(8,128)(2,1)S(1)}, u32[]{:S(2)}, u32[]{:S(2)}) collective-permute-start(bf16[32,256]{1,0:T(8,128)(2,1)S(1)} %get-tuple-element.48), channel_id=1, source_target_pairs={{0,3},{1,2},{2,1},{3,0},{4,7},{5,6},{6,5},{7,4},{8,11},{9,10},{10,... | collective-permute-start | bytes 49160 | tf_op jit(solution)/shard_map/ppermute | solution.py:186
  40.3 0.1 collective-permute-done.17.got1
  40.4 1.7 %collective-permute-done.18.got2 = bf16[32,256]{1,0:T(8,128)(2,1)S(1)} collective-permute-done((bf16[32,256]{1,0:T(8,128)(2,1)S(1)}, bf16[32,256]{1,0:T(8,128)(2,1)S(1)}, u32[]{:S(2)}, u32[]{:S(2)}) %collective-permute-start.18) | collective-permute-done | bytes 16416 | tf_op jit(solution)/shard_map/ppermute | solution.py:186
  42.1 0.8 %collective-permute-done.21.ngram_got = bf16[512,256]{1,0:T(8,128)(2,1)S(1)} collective-permute-done((bf16[512,256]{1,0:T(8,128)(2,1)S(1)}, bf16[512,256]{1,0:T(8,128)(2,1)S(1)}, u32[]{:S(2)}, u32[]{:S(2)}) %collective-permute-start.21) | collective-permute-done | bytes 262176 | tf_op jit(solution)/shard_map/ppermute | solution.py:195
  42.9 0.9 %shard_map.98 = (f32[32,256]{1,0:T(8,128)}, f32[512,256]{1,0:T(8,128)}) custom-call(f32[32,256]{1,0:T(8,128)S(1)} %get-tuple-element.38.doc, f32[32,256]{1,0:T(8,128)S(1)} %get-tuple-element.45.total, bf16[32,256]{1,0:T(8,128)(2,1)S(1)} %collective-permute-done.17.got1, bf16[32,256]{1,0:T(8,128)(2,1)S(1)} %collective-permute-done.18.got2, ...), custom_call_target="tpu_custom_call" | custom-call | tf_op jit(solution)/shard_map/pallas_call | solution.py:35
  (21 shorter events, 0.1 us)
Async XLA Ops:
  0.6 4.2 %copy-start.5 = (s32[1,1,16]{2,1,0:T(1,128)S(1)}, s32[1,1,16]{2,1,0:T(1,128)}, u32[]{:S(2)}) copy-start(s32[1,1,16]{2,1,0:T(1,128)} %ngrams.1) | copy-start | bytes 196
  0.6 4.2 %copy-start.4 = (s32[1,1,16]{2,1,0:T(1,128)S(1)}, s32[1,1,16]{2,1,0:T(1,128)}, u32[]{:S(2)}) copy-start(s32[1,1,16]{2,1,0:T(1,128)} %docs.1) | copy-start | bytes 196
  0.7 6.4 %collective-permute-start = (f32[32,256]{1,0:T(8,128)}, f32[32,256]{1,0:T(8,128)S(1)}, u32[]{:S(2)}, u32[]{:S(2)}) collective-permute-start(f32[32,256]{1,0:T(8,128)} %doc.1), channel_id=1, source_target_pairs={{0,9},{1,8},{2,11},{3,10},{4,13},{5,12},{6,15},{7,14},{8,1},{9,0},... | collective-permute-start | bytes 98312 | tf_op jit(solution)/shard_map/ppermute | solution.py:186
  4.9 2.2 %copy-start.3 = (f32[32,256]{1,0:T(8,128)S(1)}, f32[32,256]{1,0:T(8,128)}, u32[]{:S(2)}) copy-start(f32[32,256]{1,0:T(8,128)} %doc.1) | copy-start | bytes 98308
  7.1 4.5 %collective-permute-start.3 = (bf16[64,256]{1,0:T(8,128)(2,1)S(1)}, bf16[64,256]{1,0:T(8,128)(2,1)S(1)}, u32[]{:S(2)}, u32[]{:S(2)}) collective-permute-start(bf16[64,256]{1,0:T(8,128)(2,1)S(1)} %shard_map.87.pair), channel_id=1, source_target_pairs={{0,7},{1,6},{2,5},{3,4},{4,3},{5,2},{6,1},{7,0},{8,15},{9,14},{10,... | collective-permute-start | bytes 98312 | tf_op jit(solution)/shard_map/ppermute | solution.py:186
  9.9 3.7 %collective-permute-start.2 = (bf16[64,256]{1,0:T(8,128)(2,1)S(1)}, bf16[64,256]{1,0:T(8,128)(2,1)S(1)}, u32[]{:S(2)}, u32[]{:S(2)}) collective-permute-start(bf16[64,256]{1,0:T(8,128)(2,1)S(1)} %shard_map.87.pair), channel_id=1, source_target_pairs={{0,5},{1,4},{2,7},{3,6},{4,1},{5,0},{6,3},{7,2},{8,13},{9,12},{10,... | collective-permute-start | bytes 98312 | tf_op jit(solution)/shard_map/ppermute | solution.py:186
  9.9 3.7 %collective-permute-start.1 = (bf16[64,256]{1,0:T(8,128)(2,1)S(1)}, bf16[64,256]{1,0:T(8,128)(2,1)S(1)}, u32[]{:S(2)}, u32[]{:S(2)}) collective-permute-start(bf16[64,256]{1,0:T(8,128)(2,1)S(1)} %shard_map.87.pair), channel_id=1, source_target_pairs={{0,3},{1,2},{2,1},{3,0},{4,7},{5,6},{6,5},{7,4},{8,11},{9,10},{10,... | collective-permute-start | bytes 98312 | tf_op jit(solution)/shard_map/ppermute | solution.py:186
  10.6 3.0 %collective-permute-start.4 = (bf16[512,256]{1,0:T(8,128)(2,1)S(1)}, bf16[512,256]{1,0:T(8,128)(2,1)S(1)}, u32[]{:S(2)}, u32[]{:S(2)}) collective-permute-start(bf16[512,256]{1,0:T(8,128)(2,1)S(1)} %get-tuple-element.29.refs_0_), channel_id=1, source_target_pairs={{0,1},{1,0},{2,3},{3,2},{4,5},{5,4},{6,7},{7,6},{8,9},{9,8},{10,11... | collective-permute-start | bytes 786440 | tf_op jit(solution)/shard_map/ppermute | solution.py:186
  10.7 2.9 %collective-permute-start.5 = (bf16[512,512]{1,0:T(8,128)(2,1)S(1)}, bf16[512,512]{1,0:T(8,128)(2,1)S(1)}, u32[]{:S(2)}, u32[]{:S(2)}) collective-permute-start(bf16[512,512]{1,0:T(8,128)(2,1)S(1)} %get-tuple-element.31), channel_id=1, source_target_pairs={{0,1},{1,0},{2,3},{3,2},{4,5},{5,4},{6,7},{7,6},{8,9},{9,8},{10,11... | collective-permute-start | bytes 1572872 | tf_op jit(solution)/shard_map/ppermute | solution.py:186
  13.6 0.8 %copy-start.1 = (bf16[512,512]{1,0:T(8,128)(2,1)}, bf16[512,512]{1,0:T(8,128)(2,1)S(1)}, u32[]{:S(2)}) copy-start(bf16[512,512]{1,0:T(8,128)(2,1)S(1)} %collective-permute-done.5.refs_3_) | copy-start | bytes 1572868
  14.4 3.3 %collective-permute-start.13 = (bf16[512,256]{1,0:T(8,128)(2,1)S(1)}, bf16[512,256]{1,0:T(8,128)(2,1)S(1)}, u32[]{:S(2)}, u32[]{:S(2)}) collective-permute-start(bf16[512,256]{1,0:T(8,128)(2,1)S(1)} %get-tuple-element.41), channel_id=1, source_target_pairs={{0,1},{1,0},{2,3},{3,2},{4,5},{5,4},{6,7},{7,6},{8,9},{9,8},{10,11... | collective-permute-start | bytes 786440 | tf_op jit(solution)/shard_map/ppermute | solution.py:186
  14.7 5.0 %collective-permute-start.6 = (bf16[64,256]{1,0:T(8,128)(2,1)S(1)}, bf16[64,256]{1,0:T(8,128)(2,1)S(1)}, u32[]{:S(2)}, u32[]{:S(2)}) collective-permute-start(bf16[64,256]{1,0:T(8,128)(2,1)S(1)} %get-tuple-element.33), channel_id=1, source_target_pairs={{0,7},{1,6},{2,5},{3,4},{4,3},{5,2},{6,1},{7,0},{8,15},{9,14},{10,... | collective-permute-start | bytes 98312 | tf_op jit(solution)/shard_map/ppermute | solution.py:186
  16.3 3.4 %collective-permute-start.7 = (bf16[64,256]{1,0:T(8,128)(2,1)S(1)}, bf16[64,256]{1,0:T(8,128)(2,1)S(1)}, u32[]{:S(2)}, u32[]{:S(2)}) collective-permute-start(bf16[64,256]{1,0:T(8,128)(2,1)S(1)} %get-tuple-element.34), channel_id=1, source_target_pairs={{0,5},{1,4},{2,7},{3,6},{4,1},{5,0},{6,3},{7,2},{8,13},{9,12},{10,... | collective-permute-start | bytes 98312 | tf_op jit(solution)/shard_map/ppermute | solution.py:186
  16.5 3.4 %collective-permute-start.8 = (bf16[64,256]{1,0:T(8,128)(2,1)S(1)}, bf16[64,256]{1,0:T(8,128)(2,1)S(1)}, u32[]{:S(2)}, u32[]{:S(2)}) collective-permute-start(bf16[64,256]{1,0:T(8,128)(2,1)S(1)} %get-tuple-element.35), channel_id=1, source_target_pairs={{0,3},{1,2},{2,1},{3,0},{4,7},{5,6},{6,5},{7,4},{8,11},{9,10},{10,... | collective-permute-start | bytes 98312 | tf_op jit(solution)/shard_map/ppermute | solution.py:186
  18.0 9.4 %collective-permute-start.14 = (bf16[512,256]{1,0:T(8,128)(2,1)S(1)}, bf16[512,256]{1,0:T(8,128)(2,1)S(1)}, u32[]{:S(2)}, u32[]{:S(2)}) collective-permute-start(bf16[512,256]{1,0:T(8,128)(2,1)S(1)} %shard_map.93.ours), channel_id=1, source_target_pairs={{0,16},{16,0},{1,17},{17,1},{2,18},{18,2},{3,19},{19,3},{4,20},{20... | collective-permute-start | bytes 786440 | tf_op jit(solution)/shard_map/ppermute | solution.py:195
  19.9 7.6 %copy-start = (f32[512,256]{1,0:T(8,128)S(1)}, f32[512,256]{1,0:T(8,128)}, u32[]{:S(2)}) copy-start(f32[512,256]{1,0:T(8,128)} %v.1) | copy-start | bytes 1572868
  19.9 4.3 %collective-permute-start.9 = (bf16[64,256]{1,0:T(8,128)(2,1)S(1)}, bf16[64,256]{1,0:T(8,128)(2,1)S(1)}, u32[]{:S(2)}, u32[]{:S(2)}) collective-permute-start(bf16[64,256]{1,0:T(8,128)(2,1)S(1)} %get-tuple-element.37), channel_id=1, source_target_pairs={{0,9},{1,8},{2,11},{3,10},{4,13},{5,12},{6,15},{7,14},{8,1},{9,0},... | collective-permute-start | bytes 98312 | tf_op jit(solution)/shard_map/ppermute | solution.py:186
  24.2 4.3 %collective-permute-start.12 = (bf16[64,256]{1,0:T(8,128)(2,1)S(1)}, bf16[64,256]{1,0:T(8,128)(2,1)S(1)}, u32[]{:S(2)}, u32[]{:S(2)}) collective-permute-start(bf16[64,256]{1,0:T(8,128)(2,1)S(1)} %get-tuple-element.39.pair.after), channel_id=1, source_target_pairs={{0,7},{1,6},{2,5},{3,4},{4,3},{5,2},{6,1},{7,0},{8,15},{9,14},{10,... | collective-permute-start | bytes 98312 | tf_op jit(solution)/shard_map/ppermute | solution.py:186
  26.6 3.4 %collective-permute-start.11 = (bf16[64,256]{1,0:T(8,128)(2,1)S(1)}, bf16[64,256]{1,0:T(8,128)(2,1)S(1)}, u32[]{:S(2)}, u32[]{:S(2)}) collective-permute-start(bf16[64,256]{1,0:T(8,128)(2,1)S(1)} %get-tuple-element.39.pair.after), channel_id=1, source_target_pairs={{0,5},{1,4},{2,7},{3,6},{4,1},{5,0},{6,3},{7,2},{8,13},{9,12},{10,... | collective-permute-start | bytes 98312 | tf_op jit(solution)/shard_map/ppermute | solution.py:186
  26.8 3.3 %collective-permute-start.10 = (bf16[64,256]{1,0:T(8,128)(2,1)S(1)}, bf16[64,256]{1,0:T(8,128)(2,1)S(1)}, u32[]{:S(2)}, u32[]{:S(2)}) collective-permute-start(bf16[64,256]{1,0:T(8,128)(2,1)S(1)} %get-tuple-element.39.pair.after), channel_id=1, source_target_pairs={{0,3},{1,2},{2,1},{3,0},{4,7},{5,6},{6,5},{7,4},{8,11},{9,10},{10,... | collective-permute-start | bytes 98312 | tf_op jit(solution)/shard_map/ppermute | solution.py:186
  27.6 2.6 %copy-start.2 = (bf16[512,512]{1,0:T(8,128)(2,1)S(1)}, bf16[512,512]{1,0:T(8,128)(2,1)}, u32[]{:S(2)}) copy-start(bf16[512,512]{1,0:T(8,128)(2,1)} %copy-done.1) | copy-start | bytes 1572868
  27.6 2.6 %collective-permute-start.15 = (bf16[512,256]{1,0:T(8,128)(2,1)S(1)}, bf16[512,256]{1,0:T(8,128)(2,1)S(1)}, u32[]{:S(2)}, u32[]{:S(2)}) collective-permute-start(bf16[512,256]{1,0:T(8,128)(2,1)S(1)} %get-tuple-element.42.refs_0_), channel_id=1, source_target_pairs={{0,1},{1,0},{2,3},{3,2},{4,5},{5,4},{6,7},{7,6},{8,9},{9,8},{10,11... | collective-permute-start | bytes 786440 | tf_op jit(solution)/shard_map/ppermute | solution.py:186
  30.8 3.0 %collective-permute-start.20 = (bf16[512,256]{1,0:T(8,128)(2,1)S(1)}, bf16[512,256]{1,0:T(8,128)(2,1)S(1)}, u32[]{:S(2)}, u32[]{:S(2)}) collective-permute-start(bf16[512,256]{1,0:T(8,128)(2,1)S(1)} %get-tuple-element.50), channel_id=1, source_target_pairs={{0,1},{1,0},{2,3},{3,2},{4,5},{5,4},{6,7},{7,6},{8,9},{9,8},{10,11... | collective-permute-start | bytes 786440 | tf_op jit(solution)/shard_map/ppermute | solution.py:186
  31.2 4.9 %collective-permute-start.16 = (bf16[128,256]{1,0:T(8,128)(2,1)S(1)}, bf16[128,256]{1,0:T(8,128)(2,1)S(1)}, u32[]{:S(2)}, u32[]{:S(2)}) collective-permute-start(bf16[128,256]{1,0:T(8,128)(2,1)S(1)} %get-tuple-element.44), channel_id=1, source_target_pairs={{0,9},{1,8},{2,11},{3,10},{4,13},{5,12},{6,15},{7,14},{8,1},{9,0},... | collective-permute-start | bytes 196616 | tf_op jit(solution)/shard_map/ppermute | solution.py:186
  34.1 8.7 %collective-permute-start.21 = (bf16[512,256]{1,0:T(8,128)(2,1)S(1)}, bf16[512,256]{1,0:T(8,128)(2,1)S(1)}, u32[]{:S(2)}, u32[]{:S(2)}) collective-permute-start(bf16[512,256]{1,0:T(8,128)(2,1)S(1)} %shard_map.97.ours), channel_id=1, source_target_pairs={{0,16},{16,0},{1,17},{17,1},{2,18},{18,2},{3,19},{19,3},{4,20},{20... | collective-permute-start | bytes 786440 | tf_op jit(solution)/shard_map/ppermute | solution.py:195
  36.1 4.2 %collective-permute-start.17 = (bf16[32,256]{1,0:T(8,128)(2,1)S(1)}, bf16[32,256]{1,0:T(8,128)(2,1)S(1)}, u32[]{:S(2)}, u32[]{:S(2)}) collective-permute-start(bf16[32,256]{1,0:T(8,128)(2,1)S(1)} %get-tuple-element.46), channel_id=1, source_target_pairs={{0,7},{1,6},{2,5},{3,4},{4,3},{5,2},{6,1},{7,0},{8,15},{9,14},{10,... | collective-permute-start | bytes 49160 | tf_op jit(solution)/shard_map/ppermute | solution.py:186
  38.9 3.2 %collective-permute-start.18 = (bf16[32,256]{1,0:T(8,128)(2,1)S(1)}, bf16[32,256]{1,0:T(8,128)(2,1)S(1)}, u32[]{:S(2)}, u32[]{:S(2)}) collective-permute-start(bf16[32,256]{1,0:T(8,128)(2,1)S(1)} %get-tuple-element.47), channel_id=1, source_target_pairs={{0,5},{1,4},{2,7},{3,6},{4,1},{5,0},{6,3},{7,2},{8,13},{9,12},{10,... | collective-permute-start | bytes 49160 | tf_op jit(solution)/shard_map/ppermute | solution.py:186
  38.9 3.2 %collective-permute-start.19 = (bf16[32,256]{1,0:T(8,128)(2,1)S(1)}, bf16[32,256]{1,0:T(8,128)(2,1)S(1)}, u32[]{:S(2)}, u32[]{:S(2)}) collective-permute-start(bf16[32,256]{1,0:T(8,128)(2,1)S(1)} %get-tuple-element.48), channel_id=1, source_target_pairs={{0,3},{1,2},{2,1},{3,0},{4,7},{5,6},{6,5},{7,4},{8,11},{9,10},{10,... | collective-permute-start | bytes 49160 | tf_op jit(solution)/shard_map/ppermute | solution.py:186

commit v5 on v4

--- a/solution.py
+++ b/solution.py
@@ -146,7 +146,7 @@
     ours[...] = (dot(e[...], u[...], ((0,), (0,))) + got[...].astype(F32)).astype(BF)
 
 
-def near_sum_kernel(keep, got1, got2, got3, total, total16):
+def near_sum_kernel(keep, got1, got2, got3, held, total, total16):
     now = keep[...] + got1[...].astype(F32) + got2[...].astype(F32) + got3[...].astype(F32)
     total[...] = now
     total16[...] = now.astype(BF)
@@ -167,12 +167,12 @@
     doc_out[...] = doc[...] - doc_rate * now
 
 
-def pair_update_kernel(rate, doc, pair, total, got, doc_out, pair_out):
+def pair_update_kernel(rate, doc, other, total, got, doc_out, pair_out):
     own = doc.shape[0]
     now = doc[...] - rate * (total[:own, :] + got[own:, :].astype(F32))
     doc_out[...] = now
     pair_out[:own, :] = now.astype(BF)
-    now = pair[own:, :].astype(F32) - rate * (total[own:, :] + got[:own, :].astype(F32))
+    now = other[...] - rate * (total[own:, :] + got[:own, :].astype(F32))
     pair_out[own:, :] = now.astype(BF)
 
 
@@ -254,15 +254,15 @@
     total, total16 = call(
         near_sum_kernel,
         [shape(2 * own, R, F32), shape(2 * own, R, BF)],
-        [VMEM] * 4,
-        (keep, *got[::-1]),
+        [VMEM] * 4 + [ANY],
+        (keep, *got[::-1], theirs),
         flops=LONG,
     )
     doc_now, pair = call(
         functools.partial(pair_update_kernel, doc_rate),
         [shape(own, R, F32), shape(2 * own, R, BF)],
         [VMEM] * 4,
-        (doc_now, pair, total, swap(total16, FAR)),
+        (doc_now, other, total, swap(total16, FAR)),
     )
     far = exchange_near([pair] * 3)
     ngram_now, v16 = call(

time: 43.9 us -> 44 us (level)
  transfers between devices with their start and end apart: 22 -> 22, of which waited for: 12 -> 11; matrix products, arithmetic and copies ran while one was open for 0% -> 0% of each run, Pallas kernels for 7% -> 7%
where the time goes in v5:
time: 44 us; the launch traced here: 43.8 us
  starting transfers between devices  27.3 us (62%)
  waiting for transfers between devices  9.98 us (23%)
  Pallas kernels  5.06 us (11%)
  between operations  1.44 us (3%)
    ppermute x20, starting transfers between devices, swap(): lax.ppermute(x, 'col', [(i, i ^ mask) for i in range(lax.axis_size('col'))])  24.1 us
    ppermute x20, waiting for transfers between devices, swap(): lax.ppermute(x, 'col', [(i, i ^ mask) for i in range(lax.axis_size('col'))])  9.07 us
    pallas_call x13, Pallas kernels, call(): pl.pallas_call(kernel, out_shape=outs, in_specs=in_specs, out_specs=[VMEM...  5.06 us
    ppermute x2, starting transfers between devices, swap_group(): return lax.ppermute(x, 'grp', [(0, 1), (1, 0)])  3.17 us
    ppermute x2, waiting for transfers between devices, swap_group(): return lax.ppermute(x, 'grp', [(0, 1), (1, 0)])  0.91 us
  transfers between devices with their start and end apart: 22, of which 11 were waited for; matrix products, arithmetic and copies ran while one was open for 0% of the time, Pallas kernels for 7%

profile of v5, /device:TPU:0, one launch (start us, length us, event | category | flops | bytes accessed | tf_op | source)
XLA Modules:
  0.0 43.8 jit_solution(15996677723097370355)
XLA Ops:
  0.7 3.5 %collective-permute-start = (f32[32,256]{1,0:T(8,128)}, f32[32,256]{1,0:T(8,128)S(1)}, u32[]{:S(2)}, u32[]{:S(2)}) collective-permute-start(f32[32,256]{1,0:T(8,128)} %doc.1), channel_id=1, source_target_pairs={{0,9},{1,8},{2,11},{3,10},{4,13},{5,12},{6,15},{7,14},{8,1},{9,0},... | collective-permute-start | bytes 98312 | tf_op jit(solution)/shard_map/ppermute | solution.py:186
  4.9 2.2 %shard_map.86 = (bf16[512,512]{1,0:T(8,128)(2,1)S(1)}, bf16[512,512]{1,0:T(8,128)(2,1)S(1)}, bf16[512,256]{1,0:T(8,128)(2,1)S(1)}) custom-call(s32[1,1,16]{2,1,0:T(1,128)S(1)} %copy-done.2, s32[1,1,16]{2,1,0:T(1,128)S(1)} %copy-done.3, s32[1,1]{1,0:T(1,128)S(6)} %copy.9.counts, bf16[1,1,16,128,128]{4,3,2,1,0:T(8,128)(2,1)} %pmi_hbm.1, ...), custom_call_target="tpu_custom_call" | custom-call | bytes 1572996 | tf_op jit(solution)/shard_map/pallas_call | solution.py:35
  7.0 0.0 collective-permute-done.other
  7.1 2.8 %collective-permute-start.3 = (bf16[64,256]{1,0:T(8,128)(2,1)S(1)}, bf16[64,256]{1,0:T(8,128)(2,1)S(1)}, u32[]{:S(2)}, u32[]{:S(2)}) collective-permute-start(bf16[64,256]{1,0:T(8,128)(2,1)S(1)} %shard_map.87.pair), channel_id=1, source_target_pairs={{0,7},{1,6},{2,5},{3,4},{4,3},{5,2},{6,1},{7,0},{8,15},{9,14},{10,... | collective-permute-start | bytes 98312 | tf_op jit(solution)/shard_map/ppermute | solution.py:186
  9.9 0.0 collective-permute-start.2
  9.9 0.7 %collective-permute-start.1 = (bf16[64,256]{1,0:T(8,128)(2,1)S(1)}, bf16[64,256]{1,0:T(8,128)(2,1)S(1)}, u32[]{:S(2)}, u32[]{:S(2)}) collective-permute-start(bf16[64,256]{1,0:T(8,128)(2,1)S(1)} %shard_map.87.pair), channel_id=1, source_target_pairs={{0,3},{1,2},{2,1},{3,0},{4,7},{5,6},{6,5},{7,4},{8,11},{9,10},{10,... | collective-permute-start | bytes 98312 | tf_op jit(solution)/shard_map/ppermute | solution.py:186
  10.6 0.1 collective-permute-start.4
  10.7 0.5 %collective-permute-start.5 = (bf16[512,512]{1,0:T(8,128)(2,1)S(1)}, bf16[512,512]{1,0:T(8,128)(2,1)S(1)}, u32[]{:S(2)}, u32[]{:S(2)}) collective-permute-start(bf16[512,512]{1,0:T(8,128)(2,1)S(1)} %get-tuple-element.31), channel_id=1, source_target_pairs={{0,1},{1,0},{2,3},{3,2},{4,5},{5,4},{6,7},{7,6},{8,9},{9,8},{10,11... | collective-permute-start | bytes 1572872 | tf_op jit(solution)/shard_map/ppermute | solution.py:186
  11.1 0.4 %collective-permute-done.3.far3 = bf16[64,256]{1,0:T(8,128)(2,1)S(1)} collective-permute-done((bf16[64,256]{1,0:T(8,128)(2,1)S(1)}, bf16[64,256]{1,0:T(8,128)(2,1)S(1)}, u32[]{:S(2)}, u32[]{:S(2)}) %collective-permute-start.3) | collective-permute-done | bytes 32800 | tf_op jit(solution)/shard_map/ppermute | solution.py:186
  11.6 2.0 %collective-permute-done.2.far2 = bf16[64,256]{1,0:T(8,128)(2,1)S(1)} collective-permute-done((bf16[64,256]{1,0:T(8,128)(2,1)S(1)}, bf16[64,256]{1,0:T(8,128)(2,1)S(1)}, u32[]{:S(2)}, u32[]{:S(2)}) %collective-permute-start.2) | collective-permute-done | bytes 32800 | tf_op jit(solution)/shard_map/ppermute | solution.py:186
  13.6 0.0 collective-permute-done.1.far1
  13.6 0.0 collective-permute-done.4.refs_1_
  13.6 0.0 collective-permute-done.5.refs_3_.held
  13.6 0.6 %shard_map.89 = (f32[64,256]{1,0:T(8,128)S(1)}, bf16[64,256]{1,0:T(8,128)(2,1)S(1)}, bf16[64,256]{1,0:T(8,128)(2,1)S(1)}, bf16[64,256]{1,0:T(8,128)(2,1)S(1)}, b...) custom-call(bf16[256,256]{1,0:T(8,128)(2,1)S(1)} %shard_map.88.u, ...), custom_call_target="tpu_custom_call" | custom-call | flops 268435456 | bytes 1703936 | tf_op jit(solution)/shard_map/pallas_call | solution.py:35
  14.3 0.3 collective-permute-start.13
  14.6 1.7 %collective-permute-start.6 = (bf16[64,256]{1,0:T(8,128)(2,1)S(1)}, bf16[64,256]{1,0:T(8,128)(2,1)S(1)}, u32[]{:S(2)}, u32[]{:S(2)}) collective-permute-start(bf16[64,256]{1,0:T(8,128)(2,1)S(1)} %get-tuple-element.33), channel_id=1, source_target_pairs={{0,7},{1,6},{2,5},{3,4},{4,3},{5,2},{6,1},{7,0},{8,15},{9,14},{10,... | collective-permute-start | bytes 98312 | tf_op jit(solution)/shard_map/ppermute | solution.py:186
  16.3 0.2 collective-permute-start.7
  16.5 1.2 %collective-permute-start.8 = (bf16[64,256]{1,0:T(8,128)(2,1)S(1)}, bf16[64,256]{1,0:T(8,128)(2,1)S(1)}, u32[]{:S(2)}, u32[]{:S(2)}) collective-permute-start(bf16[64,256]{1,0:T(8,128)(2,1)S(1)} %get-tuple-element.35), channel_id=1, source_target_pairs={{0,3},{1,2},{2,1},{3,0},{4,7},{5,6},{6,5},{7,4},{8,11},{9,10},{10,... | collective-permute-start | bytes 98312 | tf_op jit(solution)/shard_map/ppermute | solution.py:186
  17.7 0.0 collective-permute-done.13.got
  17.7 0.3 shard_map.93.ours
  18.0 1.6 %collective-permute-start.14 = (bf16[512,256]{1,0:T(8,128)(2,1)S(1)}, bf16[512,256]{1,0:T(8,128)(2,1)S(1)}, u32[]{:S(2)}, u32[]{:S(2)}) collective-permute-start(bf16[512,256]{1,0:T(8,128)(2,1)S(1)} %shard_map.93.ours), channel_id=1, source_target_pairs={{0,16},{16,0},{1,17},{17,1},{2,18},{18,2},{3,19},{19,3},{4,20},{20... | collective-permute-start | bytes 786440 | tf_op jit(solution)/shard_map/ppermute | solution.py:195
  19.5 0.0 collective-permute-done.6.got1
  19.6 0.1 collective-permute-done.7.got2
  19.6 0.2 collective-permute-done.8.got3
  19.8 2.4 %collective-permute-start.9 = (bf16[64,256]{1,0:T(8,128)(2,1)S(1)}, bf16[64,256]{1,0:T(8,128)(2,1)S(1)}, u32[]{:S(2)}, u32[]{:S(2)}) collective-permute-start(bf16[64,256]{1,0:T(8,128)(2,1)S(1)} %get-tuple-element.37), channel_id=1, source_target_pairs={{0,9},{1,8},{2,11},{3,10},{4,13},{5,12},{6,15},{7,14},{8,1},{9,0},... | collective-permute-start | bytes 98312 | tf_op jit(solution)/shard_map/ppermute | solution.py:186
  22.2 1.9 %collective-permute-done.9.got = bf16[64,256]{1,0:T(8,128)(2,1)S(1)} collective-permute-done((bf16[64,256]{1,0:T(8,128)(2,1)S(1)}, bf16[64,256]{1,0:T(8,128)(2,1)S(1)}, u32[]{:S(2)}, u32[]{:S(2)}) %collective-permute-start.9) | collective-permute-done | bytes 32800 | tf_op jit(solution)/shard_map/ppermute | solution.py:186
  24.2 2.3 %collective-permute-start.12 = (bf16[64,256]{1,0:T(8,128)(2,1)S(1)}, bf16[64,256]{1,0:T(8,128)(2,1)S(1)}, u32[]{:S(2)}, u32[]{:S(2)}) collective-permute-start(bf16[64,256]{1,0:T(8,128)(2,1)S(1)} %get-tuple-element.39.pair.after), channel_id=1, source_target_pairs={{0,7},{1,6},{2,5},{3,4},{4,3},{5,2},{6,1},{7,0},{8,15},{9,14},{10,... | collective-permute-start | bytes 98312 | tf_op jit(solution)/shard_map/ppermute | solution.py:186
  26.5 0.3 collective-permute-start.11
  26.7 0.7 %collective-permute-start.10 = (bf16[64,256]{1,0:T(8,128)(2,1)S(1)}, bf16[64,256]{1,0:T(8,128)(2,1)S(1)}, u32[]{:S(2)}, u32[]{:S(2)}) collective-permute-start(bf16[64,256]{1,0:T(8,128)(2,1)S(1)} %get-tuple-element.39.pair.after), channel_id=1, source_target_pairs={{0,3},{1,2},{2,1},{3,0},{4,7},{5,6},{6,5},{7,4},{8,11},{9,10},{10,... | collective-permute-start | bytes 98312 | tf_op jit(solution)/shard_map/ppermute | solution.py:186
  27.4 0.0 collective-permute-done.14.got
  27.4 0.1 shard_map.94
  27.5 0.2 collective-permute-start.15
  27.7 0.7 %collective-permute-done.12.far3 = bf16[64,256]{1,0:T(8,128)(2,1)S(1)} collective-permute-done((bf16[64,256]{1,0:T(8,128)(2,1)S(1)}, bf16[64,256]{1,0:T(8,128)(2,1)S(1)}, u32[]{:S(2)}, u32[]{:S(2)}) %collective-permute-start.12) | collective-permute-done | bytes 32800 | tf_op jit(solution)/shard_map/ppermute | solution.py:186
  28.5 1.4 %collective-permute-done.11.far2 = bf16[64,256]{1,0:T(8,128)(2,1)S(1)} collective-permute-done((bf16[64,256]{1,0:T(8,128)(2,1)S(1)}, bf16[64,256]{1,0:T(8,128)(2,1)S(1)}, u32[]{:S(2)}, u32[]{:S(2)}) %collective-permute-start.11) | collective-permute-done | bytes 32800 | tf_op jit(solution)/shard_map/ppermute | solution.py:186
  29.8 0.2 collective-permute-done.10.far1
  30.1 0.7 %shard_map.95 = (f32[128,256]{1,0:T(8,128)S(1)}, bf16[128,256]{1,0:T(8,128)(2,1)S(1)}, bf16[256,512]{1,0:T(8,128)(2,1)S(1)}, bf16[512,256]{1,0:T(8,128)(2,1)S(1)}) custom-call(bf16[256,256]{1,0:T(8,128)(2,1)S(1)} %shard_map.92.u, bf16[512,256]{1,0:T(8,128)(2,1)S(1)} %get-tuple-element.42.refs_0_, bf16[512,256]{1,0:T(8,128)(2,1)S(1)} %collective-permute-done.15.refs_1_, ...), custom_call_target="tpu_custom_call" | custom-call | flops 268435456 | bytes 1703936 | tf_op jit(solution)/shard_map/pallas_call | solution.py:35
  30.8 0.3 collective-permute-start.20
  31.1 2.8 %collective-permute-start.16 = (bf16[128,256]{1,0:T(8,128)(2,1)S(1)}, bf16[128,256]{1,0:T(8,128)(2,1)S(1)}, u32[]{:S(2)}, u32[]{:S(2)}) collective-permute-start(bf16[128,256]{1,0:T(8,128)(2,1)S(1)} %get-tuple-element.44), channel_id=1, source_target_pairs={{0,9},{1,8},{2,11},{3,10},{4,13},{5,12},{6,15},{7,14},{8,1},{9,0},... | collective-permute-start | bytes 196616 | tf_op jit(solution)/shard_map/ppermute | solution.py:186
  33.9 0.3 shard_map.97.ours
  34.2 1.6 %collective-permute-start.21 = (bf16[512,256]{1,0:T(8,128)(2,1)S(1)}, bf16[512,256]{1,0:T(8,128)(2,1)S(1)}, u32[]{:S(2)}, u32[]{:S(2)}) collective-permute-start(bf16[512,256]{1,0:T(8,128)(2,1)S(1)} %shard_map.97.ours), channel_id=1, source_target_pairs={{0,16},{16,0},{1,17},{17,1},{2,18},{18,2},{3,19},{19,3},{4,20},{20... | collective-permute-start | bytes 786440 | tf_op jit(solution)/shard_map/ppermute | solution.py:195
  35.8 0.4 collective-permute-done.16.got
  36.2 2.7 %collective-permute-start.17 = (bf16[32,256]{1,0:T(8,128)(2,1)S(1)}, bf16[32,256]{1,0:T(8,128)(2,1)S(1)}, u32[]{:S(2)}, u32[]{:S(2)}) collective-permute-start(bf16[32,256]{1,0:T(8,128)(2,1)S(1)} %get-tuple-element.46), channel_id=1, source_target_pairs={{0,7},{1,6},{2,5},{3,4},{4,3},{5,2},{6,1},{7,0},{8,15},{9,14},{10,... | collective-permute-start | bytes 49160 | tf_op jit(solution)/shard_map/ppermute | solution.py:186
  38.8 0.0 collective-permute-start.18
  38.9 1.5 %collective-permute-start.19 = (bf16[32,256]{1,0:T(8,128)(2,1)S(1)}, bf16[32,256]{1,0:T(8,128)(2,1)S(1)}, u32[]{:S(2)}, u32[]{:S(2)}) collective-permute-start(bf16[32,256]{1,0:T(8,128)(2,1)S(1)} %get-tuple-element.48), channel_id=1, source_target_pairs={{0,3},{1,2},{2,1},{3,0},{4,7},{5,6},{6,5},{7,4},{8,11},{9,10},{10,... | collective-permute-start | bytes 49160 | tf_op jit(solution)/shard_map/ppermute | solution.py:186
  40.3 1.7 %collective-permute-done.18.got2 = bf16[32,256]{1,0:T(8,128)(2,1)S(1)} collective-permute-done((bf16[32,256]{1,0:T(8,128)(2,1)S(1)}, bf16[32,256]{1,0:T(8,128)(2,1)S(1)}, u32[]{:S(2)}, u32[]{:S(2)}) %collective-permute-start.18) | collective-permute-done | bytes 16416 | tf_op jit(solution)/shard_map/ppermute | solution.py:186
  42.0 0.0 collective-permute-done.19.got3
  42.0 0.9 %collective-permute-done.21.ngram_got = bf16[512,256]{1,0:T(8,128)(2,1)S(1)} collective-permute-done((bf16[512,256]{1,0:T(8,128)(2,1)S(1)}, bf16[512,256]{1,0:T(8,128)(2,1)S(1)}, u32[]{:S(2)}, u32[]{:S(2)}) %collective-permute-start.21) | collective-permute-done | bytes 262176 | tf_op jit(solution)/shard_map/ppermute | solution.py:195
  42.9 0.9 %shard_map.98 = (f32[32,256]{1,0:T(8,128)}, f32[512,256]{1,0:T(8,128)}) custom-call(f32[32,256]{1,0:T(8,128)S(1)} %get-tuple-element.38.doc, f32[32,256]{1,0:T(8,128)S(1)} %get-tuple-element.45.total, bf16[32,256]{1,0:T(8,128)(2,1)S(1)} %collective-permute-done.17.got1, bf16[32,256]{1,0:T(8,128)(2,1)S(1)} %collective-permute-done.18.got2, ...), custom_call_target="tpu_custom_call" | custom-call | tf_op jit(solution)/shard_map/pallas_call | solution.py:35
  (17 shorter events, 0.1 us)
Async XLA Ops:
  0.6 4.2 %copy-start.3 = (s32[1,1,16]{2,1,0:T(1,128)S(1)}, s32[1,1,16]{2,1,0:T(1,128)}, u32[]{:S(2)}) copy-start(s32[1,1,16]{2,1,0:T(1,128)} %ngrams.1) | copy-start | bytes 196
  0.6 4.2 %copy-start.2 = (s32[1,1,16]{2,1,0:T(1,128)S(1)}, s32[1,1,16]{2,1,0:T(1,128)}, u32[]{:S(2)}) copy-start(s32[1,1,16]{2,1,0:T(1,128)} %docs.1) | copy-start | bytes 196
  0.7 6.4 %collective-permute-start = (f32[32,256]{1,0:T(8,128)}, f32[32,256]{1,0:T(8,128)S(1)}, u32[]{:S(2)}, u32[]{:S(2)}) collective-permute-start(f32[32,256]{1,0:T(8,128)} %doc.1), channel_id=1, source_target_pairs={{0,9},{1,8},{2,11},{3,10},{4,13},{5,12},{6,15},{7,14},{8,1},{9,0},... | collective-permute-start | bytes 98312 | tf_op jit(solution)/shard_map/ppermute | solution.py:186
  4.9 2.2 %copy-start.1 = (f32[32,256]{1,0:T(8,128)S(1)}, f32[32,256]{1,0:T(8,128)}, u32[]{:S(2)}) copy-start(f32[32,256]{1,0:T(8,128)} %doc.1) | copy-start | bytes 98308
  7.1 4.5 %collective-permute-start.3 = (bf16[64,256]{1,0:T(8,128)(2,1)S(1)}, bf16[64,256]{1,0:T(8,128)(2,1)S(1)}, u32[]{:S(2)}, u32[]{:S(2)}) collective-permute-start(bf16[64,256]{1,0:T(8,128)(2,1)S(1)} %shard_map.87.pair), channel_id=1, source_target_pairs={{0,7},{1,6},{2,5},{3,4},{4,3},{5,2},{6,1},{7,0},{8,15},{9,14},{10,... | collective-permute-start | bytes 98312 | tf_op jit(solution)/shard_map/ppermute | solution.py:186
  9.9 3.7 %collective-permute-start.2 = (bf16[64,256]{1,0:T(8,128)(2,1)S(1)}, bf16[64,256]{1,0:T(8,128)(2,1)S(1)}, u32[]{:S(2)}, u32[]{:S(2)}) collective-permute-start(bf16[64,256]{1,0:T(8,128)(2,1)S(1)} %shard_map.87.pair), channel_id=1, source_target_pairs={{0,5},{1,4},{2,7},{3,6},{4,1},{5,0},{6,3},{7,2},{8,13},{9,12},{10,... | collective-permute-start | bytes 98312 | tf_op jit(solution)/shard_map/ppermute | solution.py:186
  9.9 3.7 %collective-permute-start.1 = (bf16[64,256]{1,0:T(8,128)(2,1)S(1)}, bf16[64,256]{1,0:T(8,128)(2,1)S(1)}, u32[]{:S(2)}, u32[]{:S(2)}) collective-permute-start(bf16[64,256]{1,0:T(8,128)(2,1)S(1)} %shard_map.87.pair), channel_id=1, source_target_pairs={{0,3},{1,2},{2,1},{3,0},{4,7},{5,6},{6,5},{7,4},{8,11},{9,10},{10,... | collective-permute-start | bytes 98312 | tf_op jit(solution)/shard_map/ppermute | solution.py:186
  10.6 3.0 %collective-permute-start.4 = (bf16[512,256]{1,0:T(8,128)(2,1)S(1)}, bf16[512,256]{1,0:T(8,128)(2,1)S(1)}, u32[]{:S(2)}, u32[]{:S(2)}) collective-permute-start(bf16[512,256]{1,0:T(8,128)(2,1)S(1)} %get-tuple-element.29.refs_0_), channel_id=1, source_target_pairs={{0,1},{1,0},{2,3},{3,2},{4,5},{5,4},{6,7},{7,6},{8,9},{9,8},{10,11... | collective-permute-start | bytes 786440 | tf_op jit(solution)/shard_map/ppermute | solution.py:186
  10.7 2.9 %collective-permute-start.5 = (bf16[512,512]{1,0:T(8,128)(2,1)S(1)}, bf16[512,512]{1,0:T(8,128)(2,1)S(1)}, u32[]{:S(2)}, u32[]{:S(2)}) collective-permute-start(bf16[512,512]{1,0:T(8,128)(2,1)S(1)} %get-tuple-element.31), channel_id=1, source_target_pairs={{0,1},{1,0},{2,3},{3,2},{4,5},{5,4},{6,7},{7,6},{8,9},{9,8},{10,11... | collective-permute-start | bytes 1572872 | tf_op jit(solution)/shard_map/ppermute | solution.py:186
  14.3 3.4 %collective-permute-start.13 = (bf16[512,256]{1,0:T(8,128)(2,1)S(1)}, bf16[512,256]{1,0:T(8,128)(2,1)S(1)}, u32[]{:S(2)}, u32[]{:S(2)}) collective-permute-start(bf16[512,256]{1,0:T(8,128)(2,1)S(1)} %get-tuple-element.41), channel_id=1, source_target_pairs={{0,1},{1,0},{2,3},{3,2},{4,5},{5,4},{6,7},{7,6},{8,9},{9,8},{10,11... | collective-permute-start | bytes 786440 | tf_op jit(solution)/shard_map/ppermute | solution.py:186
  14.6 5.0 %collective-permute-start.6 = (bf16[64,256]{1,0:T(8,128)(2,1)S(1)}, bf16[64,256]{1,0:T(8,128)(2,1)S(1)}, u32[]{:S(2)}, u32[]{:S(2)}) collective-permute-start(bf16[64,256]{1,0:T(8,128)(2,1)S(1)} %get-tuple-element.33), channel_id=1, source_target_pairs={{0,7},{1,6},{2,5},{3,4},{4,3},{5,2},{6,1},{7,0},{8,15},{9,14},{10,... | collective-permute-start | bytes 98312 | tf_op jit(solution)/shard_map/ppermute | solution.py:186
  16.3 3.4 %collective-permute-start.7 = (bf16[64,256]{1,0:T(8,128)(2,1)S(1)}, bf16[64,256]{1,0:T(8,128)(2,1)S(1)}, u32[]{:S(2)}, u32[]{:S(2)}) collective-permute-start(bf16[64,256]{1,0:T(8,128)(2,1)S(1)} %get-tuple-element.34), channel_id=1, source_target_pairs={{0,5},{1,4},{2,7},{3,6},{4,1},{5,0},{6,3},{7,2},{8,13},{9,12},{10,... | collective-permute-start | bytes 98312 | tf_op jit(solution)/shard_map/ppermute | solution.py:186
  16.5 3.4 %collective-permute-start.8 = (bf16[64,256]{1,0:T(8,128)(2,1)S(1)}, bf16[64,256]{1,0:T(8,128)(2,1)S(1)}, u32[]{:S(2)}, u32[]{:S(2)}) collective-permute-start(bf16[64,256]{1,0:T(8,128)(2,1)S(1)} %get-tuple-element.35), channel_id=1, source_target_pairs={{0,3},{1,2},{2,1},{3,0},{4,7},{5,6},{6,5},{7,4},{8,11},{9,10},{10,... | collective-permute-start | bytes 98312 | tf_op jit(solution)/shard_map/ppermute | solution.py:186
  18.0 9.4 %collective-permute-start.14 = (bf16[512,256]{1,0:T(8,128)(2,1)S(1)}, bf16[512,256]{1,0:T(8,128)(2,1)S(1)}, u32[]{:S(2)}, u32[]{:S(2)}) collective-permute-start(bf16[512,256]{1,0:T(8,128)(2,1)S(1)} %shard_map.93.ours), channel_id=1, source_target_pairs={{0,16},{16,0},{1,17},{17,1},{2,18},{18,2},{3,19},{19,3},{4,20},{20... | collective-permute-start | bytes 786440 | tf_op jit(solution)/shard_map/ppermute | solution.py:195
  19.8 7.6 %copy-start = (f32[512,256]{1,0:T(8,128)S(1)}, f32[512,256]{1,0:T(8,128)}, u32[]{:S(2)}) copy-start(f32[512,256]{1,0:T(8,128)} %v.1) | copy-start | bytes 1572868
  19.8 4.3 %collective-permute-start.9 = (bf16[64,256]{1,0:T(8,128)(2,1)S(1)}, bf16[64,256]{1,0:T(8,128)(2,1)S(1)}, u32[]{:S(2)}, u32[]{:S(2)}) collective-permute-start(bf16[64,256]{1,0:T(8,128)(2,1)S(1)} %get-tuple-element.37), channel_id=1, source_target_pairs={{0,9},{1,8},{2,11},{3,10},{4,13},{5,12},{6,15},{7,14},{8,1},{9,0},... | collective-permute-start | bytes 98312 | tf_op jit(solution)/shard_map/ppermute | solution.py:186
  24.2 4.3 %collective-permute-start.12 = (bf16[64,256]{1,0:T(8,128)(2,1)S(1)}, bf16[64,256]{1,0:T(8,128)(2,1)S(1)}, u32[]{:S(2)}, u32[]{:S(2)}) collective-permute-start(bf16[64,256]{1,0:T(8,128)(2,1)S(1)} %get-tuple-element.39.pair.after), channel_id=1, source_target_pairs={{0,7},{1,6},{2,5},{3,4},{4,3},{5,2},{6,1},{7,0},{8,15},{9,14},{10,... | collective-permute-start | bytes 98312 | tf_op jit(solution)/shard_map/ppermute | solution.py:186
  26.5 3.4 %collective-permute-start.11 = (bf16[64,256]{1,0:T(8,128)(2,1)S(1)}, bf16[64,256]{1,0:T(8,128)(2,1)S(1)}, u32[]{:S(2)}, u32[]{:S(2)}) collective-permute-start(bf16[64,256]{1,0:T(8,128)(2,1)S(1)} %get-tuple-element.39.pair.after), channel_id=1, source_target_pairs={{0,5},{1,4},{2,7},{3,6},{4,1},{5,0},{6,3},{7,2},{8,13},{9,12},{10,... | collective-permute-start | bytes 98312 | tf_op jit(solution)/shard_map/ppermute | solution.py:186
  26.7 3.3 %collective-permute-start.10 = (bf16[64,256]{1,0:T(8,128)(2,1)S(1)}, bf16[64,256]{1,0:T(8,128)(2,1)S(1)}, u32[]{:S(2)}, u32[]{:S(2)}) collective-permute-start(bf16[64,256]{1,0:T(8,128)(2,1)S(1)} %get-tuple-element.39.pair.after), channel_id=1, source_target_pairs={{0,3},{1,2},{2,1},{3,0},{4,7},{5,6},{6,5},{7,4},{8,11},{9,10},{10,... | collective-permute-start | bytes 98312 | tf_op jit(solution)/shard_map/ppermute | solution.py:186
  27.5 2.6 %collective-permute-start.15 = (bf16[512,256]{1,0:T(8,128)(2,1)S(1)}, bf16[512,256]{1,0:T(8,128)(2,1)S(1)}, u32[]{:S(2)}, u32[]{:S(2)}) collective-permute-start(bf16[512,256]{1,0:T(8,128)(2,1)S(1)} %get-tuple-element.42.refs_0_), channel_id=1, source_target_pairs={{0,1},{1,0},{2,3},{3,2},{4,5},{5,4},{6,7},{7,6},{8,9},{9,8},{10,11... | collective-permute-start | bytes 786440 | tf_op jit(solution)/shard_map/ppermute | solution.py:186
  30.8 3.2 %collective-permute-start.20 = (bf16[512,256]{1,0:T(8,128)(2,1)S(1)}, bf16[512,256]{1,0:T(8,128)(2,1)S(1)}, u32[]{:S(2)}, u32[]{:S(2)}) collective-permute-start(bf16[512,256]{1,0:T(8,128)(2,1)S(1)} %get-tuple-element.50), channel_id=1, source_target_pairs={{0,1},{1,0},{2,3},{3,2},{4,5},{5,4},{6,7},{7,6},{8,9},{9,8},{10,11... | collective-permute-start | bytes 786440 | tf_op jit(solution)/shard_map/ppermute | solution.py:186
  31.1 5.1 %collective-permute-start.16 = (bf16[128,256]{1,0:T(8,128)(2,1)S(1)}, bf16[128,256]{1,0:T(8,128)(2,1)S(1)}, u32[]{:S(2)}, u32[]{:S(2)}) collective-permute-start(bf16[128,256]{1,0:T(8,128)(2,1)S(1)} %get-tuple-element.44), channel_id=1, source_target_pairs={{0,9},{1,8},{2,11},{3,10},{4,13},{5,12},{6,15},{7,14},{8,1},{9,0},... | collective-permute-start | bytes 196616 | tf_op jit(solution)/shard_map/ppermute | solution.py:186
  34.2 8.7 %collective-permute-start.21 = (bf16[512,256]{1,0:T(8,128)(2,1)S(1)}, bf16[512,256]{1,0:T(8,128)(2,1)S(1)}, u32[]{:S(2)}, u32[]{:S(2)}) collective-permute-start(bf16[512,256]{1,0:T(8,128)(2,1)S(1)} %shard_map.97.ours), channel_id=1, source_target_pairs={{0,16},{16,0},{1,17},{17,1},{2,18},{18,2},{3,19},{19,3},{4,20},{20... | collective-permute-start | bytes 786440 | tf_op jit(solution)/shard_map/ppermute | solution.py:195
  36.2 4.1 %collective-permute-start.17 = (bf16[32,256]{1,0:T(8,128)(2,1)S(1)}, bf16[32,256]{1,0:T(8,128)(2,1)S(1)}, u32[]{:S(2)}, u32[]{:S(2)}) collective-permute-start(bf16[32,256]{1,0:T(8,128)(2,1)S(1)} %get-tuple-element.46), channel_id=1, source_target_pairs={{0,7},{1,6},{2,5},{3,4},{4,3},{5,2},{6,1},{7,0},{8,15},{9,14},{10,... | collective-permute-start | bytes 49160 | tf_op jit(solution)/shard_map/ppermute | solution.py:186
  38.8 3.2 %collective-permute-start.18 = (bf16[32,256]{1,0:T(8,128)(2,1)S(1)}, bf16[32,256]{1,0:T(8,128)(2,1)S(1)}, u32[]{:S(2)}, u32[]{:S(2)}) collective-permute-start(bf16[32,256]{1,0:T(8,128)(2,1)S(1)} %get-tuple-element.47), channel_id=1, source_target_pairs={{0,5},{1,4},{2,7},{3,6},{4,1},{5,0},{6,3},{7,2},{8,13},{9,12},{10,... | collective-permute-start | bytes 49160 | tf_op jit(solution)/shard_map/ppermute | solution.py:186
  38.9 3.2 %collective-permute-start.19 = (bf16[32,256]{1,0:T(8,128)(2,1)S(1)}, bf16[32,256]{1,0:T(8,128)(2,1)S(1)}, u32[]{:S(2)}, u32[]{:S(2)}) collective-permute-start(bf16[32,256]{1,0:T(8,128)(2,1)S(1)} %get-tuple-element.48), channel_id=1, source_target_pairs={{0,3},{1,2},{2,1},{3,0},{4,7},{5,6},{6,5},{7,4},{8,11},{9,10},{10,... | collective-permute-start | bytes 49160 | tf_op jit(solution)/shard_map/ppermute | solution.py:186

commit v6 on v5

--- a/solution.py
+++ b/solution.py
@@ -146,6 +146,24 @@
     ours[...] = (dot(e[...], u[...], ((0,), (0,))) + got[...].astype(F32)).astype(BF)
 
 
+def ngram_part_kernel(e, u, part):
+    @pl.when(lax.axis_index("col") < 8)
+    def _():
+        part[...] = dot(e[...], u[...], ((0,), (0,)))
+
+
+def ngram_rest_kernel(e, u, part, got, ours):
+    ahead = lax.axis_index("col") < 8
+
+    @pl.when(ahead)
+    def _():
+        ours[...] = (part[...] + got[...].astype(F32)).astype(BF)
+
+    @pl.when(jnp.logical_not(ahead))
+    def _():
+        ngram_keep_kernel(e, u, got, ours)
+
+
 def near_sum_kernel(keep, got1, got2, got3, held, total, total16):
     now = keep[...] + got1[...].astype(F32) + got2[...].astype(F32) + got3[...].astype(F32)
     total[...] = now
@@ -223,6 +241,7 @@
     far = exchange_near([pair] * 3)
     theirs = swap(theirs, OTHER_CORE)
     v16_theirs = swap(v16, OTHER_CORE)
+
     def gradients(kernel, keep_and_send, pair, far, v16, v16_theirs):
         (u,) = call(rows_kernel, [shape(half, R, BF)], [VMEM] * 4, (pair, *far), flops=LONG)
         *outs, e, gv = call(
@@ -233,13 +252,19 @@
             [pltpu.VMEM((half, n), BF)],
             flops=flops,
         )
-        (ours,) = call(
-            ngram_keep_kernel,
-            [shape(n, R, BF)],
-            [VMEM] * 3,
-            (e, u, swap(gv, OTHER_CORE)),
-            flops=flops // 4,
-        )
+        got = swap(gv, OTHER_CORE)
+        if kernel is near_first_kernel:
+            (ours,) = call(
+                ngram_keep_kernel, [shape(n, R, BF)], [VMEM] * 3, (e, u, got), flops=flops // 4
+            )
+        else:
+            (part,) = call(
+                ngram_part_kernel, [shape(n, R, F32)], [VMEM] * 2, (e, u), flops=flops // 4
+            )
+            outs[1], part = lax.optimization_barrier((outs[1], part))
+            (ours,) = call(
+                ngram_rest_kernel, [shape(n, R, BF)], [VMEM] * 4, (e, u, part, got), flops=flops // 4
+            )
         return *outs, ours, swap_group(ours)
 
     keep, *send, ours, ngram_got = gradients(

time: 44 us -> 43.8 us (level)
    pallas_call x13 -> x14, Pallas kernels: 5.06 us -> 5.1 us  [call(): pl.pallas_call(kernel, out_shape=outs, in_specs=in_specs, out_specs=[VMEM...]
  transfers between devices with their start and end apart: 22 -> 22, of which waited for: 11 -> 12; matrix products, arithmetic and copies ran while one was open for 0% -> 0% of each run, Pallas kernels for 7% -> 7%
where the time goes in v6:
time: 43.8 us; the launch traced here: 43.6 us
  starting transfers between devices  26.9 us (61%)
  waiting for transfers between devices  10.1 us (23%)
  Pallas kernels  5.1 us (12%)
  between operations  1.45 us (3%)
    ppermute x20, starting transfers between devices, swap(): lax.ppermute(x, 'col', [(i, i ^ mask) for i in range(lax.axis_size('col'))])  23.7 us
    ppermute x20, waiting for transfers between devices, swap(): lax.ppermute(x, 'col', [(i, i ^ mask) for i in range(lax.axis_size('col'))])  9.45 us
    pallas_call x14, Pallas kernels, call(): pl.pallas_call(kernel, out_shape=outs, in_specs=in_specs, out_specs=[VMEM...  5.1 us
    ppermute x2, starting transfers between devices, swap_group(): return lax.ppermute(x, 'grp', [(0, 1), (1, 0)])  3.17 us
  transfers between devices with their start and end apart: 22, of which 12 were waited for; matrix products, arithmetic and copies ran while one was open for 0% of the time, Pallas kernels for 7%

profile of v6, /device:TPU:0, one launch (start us, length us, event | category | flops | bytes accessed | tf_op | source)
XLA Modules:
  0.0 43.6 jit_solution(1058741518961239253)
XLA Ops:
  0.7 3.5 %collective-permute-start = (f32[32,256]{1,0:T(8,128)}, f32[32,256]{1,0:T(8,128)S(1)}, u32[]{:S(2)}, u32[]{:S(2)}) collective-permute-start(f32[32,256]{1,0:T(8,128)} %doc.1), channel_id=1, source_target_pairs={{0,9},{1,8},{2,11},{3,10},{4,13},{5,12},{6,15},{7,14},{8,1},{9,0},... | collective-permute-start | bytes 98312 | tf_op jit(solution)/shard_map/ppermute | solution.py:204
  4.9 2.2 %shard_map.86 = (bf16[512,512]{1,0:T(8,128)(2,1)S(1)}, bf16[512,512]{1,0:T(8,128)(2,1)S(1)}, bf16[512,256]{1,0:T(8,128)(2,1)S(1)}) custom-call(s32[1,1,16]{2,1,0:T(1,128)S(1)} %copy-done.2, s32[1,1,16]{2,1,0:T(1,128)S(1)} %copy-done.3, s32[1,1]{1,0:T(1,128)S(6)} %copy.9.counts, bf16[1,1,16,128,128]{4,3,2,1,0:T(8,128)(2,1)} %pmi_hbm.1, ...), custom_call_target="tpu_custom_call" | custom-call | bytes 1572996 | tf_op jit(solution)/shard_map/pallas_call | solution.py:35
  7.0 0.0 collective-permute-done.other
  7.1 2.8 %collective-permute-start.3 = (bf16[64,256]{1,0:T(8,128)(2,1)S(1)}, bf16[64,256]{1,0:T(8,128)(2,1)S(1)}, u32[]{:S(2)}, u32[]{:S(2)}) collective-permute-start(bf16[64,256]{1,0:T(8,128)(2,1)S(1)} %shard_map.87.pair), channel_id=1, source_target_pairs={{0,7},{1,6},{2,5},{3,4},{4,3},{5,2},{6,1},{7,0},{8,15},{9,14},{10,... | collective-permute-start | bytes 98312 | tf_op jit(solution)/shard_map/ppermute | solution.py:204
  9.9 0.0 collective-permute-start.2
  9.9 0.7 %collective-permute-start.1 = (bf16[64,256]{1,0:T(8,128)(2,1)S(1)}, bf16[64,256]{1,0:T(8,128)(2,1)S(1)}, u32[]{:S(2)}, u32[]{:S(2)}) collective-permute-start(bf16[64,256]{1,0:T(8,128)(2,1)S(1)} %shard_map.87.pair), channel_id=1, source_target_pairs={{0,3},{1,2},{2,1},{3,0},{4,7},{5,6},{6,5},{7,4},{8,11},{9,10},{10,... | collective-permute-start | bytes 98312 | tf_op jit(solution)/shard_map/ppermute | solution.py:204
  10.6 0.1 collective-permute-start.4
  10.7 0.5 %collective-permute-start.5 = (bf16[512,512]{1,0:T(8,128)(2,1)S(1)}, bf16[512,512]{1,0:T(8,128)(2,1)S(1)}, u32[]{:S(2)}, u32[]{:S(2)}) collective-permute-start(bf16[512,512]{1,0:T(8,128)(2,1)S(1)} %get-tuple-element.33), channel_id=1, source_target_pairs={{0,1},{1,0},{2,3},{3,2},{4,5},{5,4},{6,7},{7,6},{8,9},{9,8},{10,11... | collective-permute-start | bytes 1572872 | tf_op jit(solution)/shard_map/ppermute | solution.py:204
  11.1 0.4 %collective-permute-done.3.far3 = bf16[64,256]{1,0:T(8,128)(2,1)S(1)} collective-permute-done((bf16[64,256]{1,0:T(8,128)(2,1)S(1)}, bf16[64,256]{1,0:T(8,128)(2,1)S(1)}, u32[]{:S(2)}, u32[]{:S(2)}) %collective-permute-start.3) | collective-permute-done | bytes 32800 | tf_op jit(solution)/shard_map/ppermute | solution.py:204
  11.6 2.0 %collective-permute-done.2.far2 = bf16[64,256]{1,0:T(8,128)(2,1)S(1)} collective-permute-done((bf16[64,256]{1,0:T(8,128)(2,1)S(1)}, bf16[64,256]{1,0:T(8,128)(2,1)S(1)}, u32[]{:S(2)}, u32[]{:S(2)}) %collective-permute-start.2) | collective-permute-done | bytes 32800 | tf_op jit(solution)/shard_map/ppermute | solution.py:204
  13.6 0.0 collective-permute-done.1.far1
  13.6 0.0 collective-permute-done.4.refs_1_
  13.6 0.0 collective-permute-done.5.refs_3_.held
  13.6 0.6 %shard_map.89 = (f32[64,256]{1,0:T(8,128)S(1)}, bf16[64,256]{1,0:T(8,128)(2,1)S(1)}, bf16[64,256]{1,0:T(8,128)(2,1)S(1)}, bf16[64,256]{1,0:T(8,128)(2,1)S(1)}, b...) custom-call(bf16[256,256]{1,0:T(8,128)(2,1)S(1)} %shard_map.88.u, ...), custom_call_target="tpu_custom_call" | custom-call | flops 268435456 | bytes 1703936 | tf_op jit(solution)/shard_map/pallas_call | solution.py:35
  14.3 0.3 collective-permute-start.13
  14.6 1.7 %collective-permute-start.6 = (bf16[64,256]{1,0:T(8,128)(2,1)S(1)}, bf16[64,256]{1,0:T(8,128)(2,1)S(1)}, u32[]{:S(2)}, u32[]{:S(2)}) collective-permute-start(bf16[64,256]{1,0:T(8,128)(2,1)S(1)} %get-tuple-element.35), channel_id=1, source_target_pairs={{0,7},{1,6},{2,5},{3,4},{4,3},{5,2},{6,1},{7,0},{8,15},{9,14},{10,... | collective-permute-start | bytes 98312 | tf_op jit(solution)/shard_map/ppermute | solution.py:204
  16.3 0.2 collective-permute-start.7
  16.5 1.2 %collective-permute-start.8 = (bf16[64,256]{1,0:T(8,128)(2,1)S(1)}, bf16[64,256]{1,0:T(8,128)(2,1)S(1)}, u32[]{:S(2)}, u32[]{:S(2)}) collective-permute-start(bf16[64,256]{1,0:T(8,128)(2,1)S(1)} %get-tuple-element.37), channel_id=1, source_target_pairs={{0,3},{1,2},{2,1},{3,0},{4,7},{5,6},{6,5},{7,4},{8,11},{9,10},{10,... | collective-permute-start | bytes 98312 | tf_op jit(solution)/shard_map/ppermute | solution.py:204
  17.7 0.3 shard_map.93.ours
  18.0 1.6 %collective-permute-start.14 = (bf16[512,256]{1,0:T(8,128)(2,1)S(1)}, bf16[512,256]{1,0:T(8,128)(2,1)S(1)}, u32[]{:S(2)}, u32[]{:S(2)}) collective-permute-start(bf16[512,256]{1,0:T(8,128)(2,1)S(1)} %shard_map.93.ours), channel_id=1, source_target_pairs={{0,16},{16,0},{1,17},{17,1},{2,18},{18,2},{3,19},{19,3},{4,20},{20... | collective-permute-start | bytes 786440 | tf_op jit(solution)/shard_map/ppermute | solution.py:213
  19.6 0.1 collective-permute-done.7.got2
  19.6 0.2 collective-permute-done.8.got3
  19.8 2.4 %collective-permute-start.9 = (bf16[64,256]{1,0:T(8,128)(2,1)S(1)}, bf16[64,256]{1,0:T(8,128)(2,1)S(1)}, u32[]{:S(2)}, u32[]{:S(2)}) collective-permute-start(bf16[64,256]{1,0:T(8,128)(2,1)S(1)} %get-tuple-element.39), channel_id=1, source_target_pairs={{0,9},{1,8},{2,11},{3,10},{4,13},{5,12},{6,15},{7,14},{8,1},{9,0},... | collective-permute-start | bytes 98312 | tf_op jit(solution)/shard_map/ppermute | solution.py:204
  22.2 1.9 %collective-permute-done.9.got = bf16[64,256]{1,0:T(8,128)(2,1)S(1)} collective-permute-done((bf16[64,256]{1,0:T(8,128)(2,1)S(1)}, bf16[64,256]{1,0:T(8,128)(2,1)S(1)}, u32[]{:S(2)}, u32[]{:S(2)}) %collective-permute-start.9) | collective-permute-done | bytes 32800 | tf_op jit(solution)/shard_map/ppermute | solution.py:204
  24.2 2.3 %collective-permute-start.12 = (bf16[64,256]{1,0:T(8,128)(2,1)S(1)}, bf16[64,256]{1,0:T(8,128)(2,1)S(1)}, u32[]{:S(2)}, u32[]{:S(2)}) collective-permute-start(bf16[64,256]{1,0:T(8,128)(2,1)S(1)} %get-tuple-element.41.pair.after), channel_id=1, source_target_pairs={{0,7},{1,6},{2,5},{3,4},{4,3},{5,2},{6,1},{7,0},{8,15},{9,14},{10,... | collective-permute-start | bytes 98312 | tf_op jit(solution)/shard_map/ppermute | solution.py:204
  26.5 0.3 collective-permute-start.11
  26.7 0.7 %collective-permute-start.10 = (bf16[64,256]{1,0:T(8,128)(2,1)S(1)}, bf16[64,256]{1,0:T(8,128)(2,1)S(1)}, u32[]{:S(2)}, u32[]{:S(2)}) collective-permute-start(bf16[64,256]{1,0:T(8,128)(2,1)S(1)} %get-tuple-element.41.pair.after), channel_id=1, source_target_pairs={{0,3},{1,2},{2,1},{3,0},{4,7},{5,6},{6,5},{7,4},{8,11},{9,10},{10,... | collective-permute-start | bytes 98312 | tf_op jit(solution)/shard_map/ppermute | solution.py:204
  27.4 0.0 collective-permute-done.14.got
  27.4 0.1 shard_map.94
  27.5 0.2 collective-permute-start.15
  27.7 0.7 %collective-permute-done.12.far3 = bf16[64,256]{1,0:T(8,128)(2,1)S(1)} collective-permute-done((bf16[64,256]{1,0:T(8,128)(2,1)S(1)}, bf16[64,256]{1,0:T(8,128)(2,1)S(1)}, u32[]{:S(2)}, u32[]{:S(2)}) %collective-permute-start.12) | collective-permute-done | bytes 32800 | tf_op jit(solution)/shard_map/ppermute | solution.py:204
  28.5 1.4 %collective-permute-done.11.far2 = bf16[64,256]{1,0:T(8,128)(2,1)S(1)} collective-permute-done((bf16[64,256]{1,0:T(8,128)(2,1)S(1)}, bf16[64,256]{1,0:T(8,128)(2,1)S(1)}, u32[]{:S(2)}, u32[]{:S(2)}) %collective-permute-start.11) | collective-permute-done | bytes 32800 | tf_op jit(solution)/shard_map/ppermute | solution.py:204
  29.8 0.2 collective-permute-done.10.far1
  30.1 0.0 collective-permute-done.15.refs_1_
  30.1 0.7 %shard_map.95 = (f32[128,256]{1,0:T(8,128)S(1)}, bf16[128,256]{1,0:T(8,128)(2,1)S(1)}, bf16[256,512]{1,0:T(8,128)(2,1)S(1)}, bf16[512,256]{1,0:T(8,128)(2,1)S(1)}) custom-call(bf16[256,256]{1,0:T(8,128)(2,1)S(1)} %shard_map.92.u, bf16[512,256]{1,0:T(8,128)(2,1)S(1)} %get-tuple-element.44.refs_0_, bf16[512,256]{1,0:T(8,128)(2,1)S(1)} %collective-permute-done.15.refs_1_, ...), custom_call_target="tpu_custom_call" | custom-call | flops 268435456 | bytes 1703936 | tf_op jit(solution)/shard_map/pallas_call | solution.py:35
  30.8 0.3 collective-permute-start.20
  31.1 0.3 shard_map.96.part
  31.4 2.6 %collective-permute-start.16 = (bf16[128,256]{1,0:T(8,128)(2,1)S(1)}, bf16[128,256]{1,0:T(8,128)(2,1)S(1)}, u32[]{:S(2)}, u32[]{:S(2)}) collective-permute-start(bf16[128,256]{1,0:T(8,128)(2,1)S(1)} %get-tuple-element.48), channel_id=1, source_target_pairs={{0,9},{1,8},{2,11},{3,10},{4,13},{5,12},{6,15},{7,14},{8,1},{9,0},... | collective-permute-start | bytes 196616 | tf_op jit(solution)/shard_map/ppermute | solution.py:204
  34.0 1.6 %collective-permute-start.21 = (bf16[512,256]{1,0:T(8,128)(2,1)S(1)}, bf16[512,256]{1,0:T(8,128)(2,1)S(1)}, u32[]{:S(2)}, u32[]{:S(2)}) collective-permute-start(bf16[512,256]{1,0:T(8,128)(2,1)S(1)} %shard_map.98.ours), channel_id=1, source_target_pairs={{0,16},{16,0},{1,17},{17,1},{2,18},{18,2},{3,19},{19,3},{4,20},{20... | collective-permute-start | bytes 786440 | tf_op jit(solution)/shard_map/ppermute | solution.py:213
  35.6 0.7 %collective-permute-done.16.got = bf16[128,256]{1,0:T(8,128)(2,1)S(1)} collective-permute-done((bf16[128,256]{1,0:T(8,128)(2,1)S(1)}, bf16[128,256]{1,0:T(8,128)(2,1)S(1)}, u32[]{:S(2)}, u32[]{:S(2)}) %collective-permute-start.16) | collective-permute-done | bytes 65568 | tf_op jit(solution)/shard_map/ppermute | solution.py:204
  36.4 2.5 %collective-permute-start.17 = (bf16[32,256]{1,0:T(8,128)(2,1)S(1)}, bf16[32,256]{1,0:T(8,128)(2,1)S(1)}, u32[]{:S(2)}, u32[]{:S(2)}) collective-permute-start(bf16[32,256]{1,0:T(8,128)(2,1)S(1)} %get-tuple-element.50), channel_id=1, source_target_pairs={{0,7},{1,6},{2,5},{3,4},{4,3},{5,2},{6,1},{7,0},{8,15},{9,14},{10,... | collective-permute-start | bytes 49160 | tf_op jit(solution)/shard_map/ppermute | solution.py:204
  38.8 0.0 collective-permute-start.18
  38.9 1.5 %collective-permute-start.19 = (bf16[32,256]{1,0:T(8,128)(2,1)S(1)}, bf16[32,256]{1,0:T(8,128)(2,1)S(1)}, u32[]{:S(2)}, u32[]{:S(2)}) collective-permute-start(bf16[32,256]{1,0:T(8,128)(2,1)S(1)} %get-tuple-element.52), channel_id=1, source_target_pairs={{0,3},{1,2},{2,1},{3,0},{4,7},{5,6},{6,5},{7,4},{8,11},{9,10},{10,... | collective-permute-start | bytes 49160 | tf_op jit(solution)/shard_map/ppermute | solution.py:204
  40.3 0.2 collective-permute-done.17.got1
  40.5 1.5 %collective-permute-done.18.got2 = bf16[32,256]{1,0:T(8,128)(2,1)S(1)} collective-permute-done((bf16[32,256]{1,0:T(8,128)(2,1)S(1)}, bf16[32,256]{1,0:T(8,128)(2,1)S(1)}, u32[]{:S(2)}, u32[]{:S(2)}) %collective-permute-start.18) | collective-permute-done | bytes 16416 | tf_op jit(solution)/shard_map/ppermute | solution.py:204
  42.0 0.0 collective-permute-done.19.got3
  42.0 0.7 %collective-permute-done.21.ngram_got = bf16[512,256]{1,0:T(8,128)(2,1)S(1)} collective-permute-done((bf16[512,256]{1,0:T(8,128)(2,1)S(1)}, bf16[512,256]{1,0:T(8,128)(2,1)S(1)}, u32[]{:S(2)}, u32[]{:S(2)}) %collective-permute-start.21) | collective-permute-done | bytes 262176 | tf_op jit(solution)/shard_map/ppermute | solution.py:213
  42.7 0.9 %shard_map.99 = (f32[32,256]{1,0:T(8,128)}, f32[512,256]{1,0:T(8,128)}) custom-call(f32[32,256]{1,0:T(8,128)S(1)} %get-tuple-element.40.doc, f32[32,256]{1,0:T(8,128)S(1)} %get-tuple-element.49.total, bf16[32,256]{1,0:T(8,128)(2,1)S(1)} %collective-permute-done.17.got1, bf16[32,256]{1,0:T(8,128)(2,1)S(1)} %collective-permute-done.18.got2, ...), custom_call_target="tpu_custom_call" | custom-call | tf_op jit(solution)/shard_map/pallas_call | solution.py:35
  (18 shorter events, 0.1 us)
Async XLA Ops:
  0.6 4.2 %copy-start.3 = (s32[1,1,16]{2,1,0:T(1,128)S(1)}, s32[1,1,16]{2,1,0:T(1,128)}, u32[]{:S(2)}) copy-start(s32[1,1,16]{2,1,0:T(1,128)} %ngrams.1) | copy-start | bytes 196
  0.6 4.2 %copy-start.2 = (s32[1,1,16]{2,1,0:T(1,128)S(1)}, s32[1,1,16]{2,1,0:T(1,128)}, u32[]{:S(2)}) copy-start(s32[1,1,16]{2,1,0:T(1,128)} %docs.1) | copy-start | bytes 196
  0.7 6.4 %collective-permute-start = (f32[32,256]{1,0:T(8,128)}, f32[32,256]{1,0:T(8,128)S(1)}, u32[]{:S(2)}, u32[]{:S(2)}) collective-permute-start(f32[32,256]{1,0:T(8,128)} %doc.1), channel_id=1, source_target_pairs={{0,9},{1,8},{2,11},{3,10},{4,13},{5,12},{6,15},{7,14},{8,1},{9,0},... | collective-permute-start | bytes 98312 | tf_op jit(solution)/shard_map/ppermute | solution.py:204
  4.9 2.2 %copy-start.1 = (f32[32,256]{1,0:T(8,128)S(1)}, f32[32,256]{1,0:T(8,128)}, u32[]{:S(2)}) copy-start(f32[32,256]{1,0:T(8,128)} %doc.1) | copy-start | bytes 98308
  7.1 4.5 %collective-permute-start.3 = (bf16[64,256]{1,0:T(8,128)(2,1)S(1)}, bf16[64,256]{1,0:T(8,128)(2,1)S(1)}, u32[]{:S(2)}, u32[]{:S(2)}) collective-permute-start(bf16[64,256]{1,0:T(8,128)(2,1)S(1)} %shard_map.87.pair), channel_id=1, source_target_pairs={{0,7},{1,6},{2,5},{3,4},{4,3},{5,2},{6,1},{7,0},{8,15},{9,14},{10,... | collective-permute-start | bytes 98312 | tf_op jit(solution)/shard_map/ppermute | solution.py:204
  9.9 3.7 %collective-permute-start.2 = (bf16[64,256]{1,0:T(8,128)(2,1)S(1)}, bf16[64,256]{1,0:T(8,128)(2,1)S(1)}, u32[]{:S(2)}, u32[]{:S(2)}) collective-permute-start(bf16[64,256]{1,0:T(8,128)(2,1)S(1)} %shard_map.87.pair), channel_id=1, source_target_pairs={{0,5},{1,4},{2,7},{3,6},{4,1},{5,0},{6,3},{7,2},{8,13},{9,12},{10,... | collective-permute-start | bytes 98312 | tf_op jit(solution)/shard_map/ppermute | solution.py:204
  9.9 3.7 %collective-permute-start.1 = (bf16[64,256]{1,0:T(8,128)(2,1)S(1)}, bf16[64,256]{1,0:T(8,128)(2,1)S(1)}, u32[]{:S(2)}, u32[]{:S(2)}) collective-permute-start(bf16[64,256]{1,0:T(8,128)(2,1)S(1)} %shard_map.87.pair), channel_id=1, source_target_pairs={{0,3},{1,2},{2,1},{3,0},{4,7},{5,6},{6,5},{7,4},{8,11},{9,10},{10,... | collective-permute-start | bytes 98312 | tf_op jit(solution)/shard_map/ppermute | solution.py:204
  10.6 3.0 %collective-permute-start.4 = (bf16[512,256]{1,0:T(8,128)(2,1)S(1)}, bf16[512,256]{1,0:T(8,128)(2,1)S(1)}, u32[]{:S(2)}, u32[]{:S(2)}) collective-permute-start(bf16[512,256]{1,0:T(8,128)(2,1)S(1)} %get-tuple-element.31.refs_0_), channel_id=1, source_target_pairs={{0,1},{1,0},{2,3},{3,2},{4,5},{5,4},{6,7},{7,6},{8,9},{9,8},{10,11... | collective-permute-start | bytes 786440 | tf_op jit(solution)/shard_map/ppermute | solution.py:204
  10.7 2.9 %collective-permute-start.5 = (bf16[512,512]{1,0:T(8,128)(2,1)S(1)}, bf16[512,512]{1,0:T(8,128)(2,1)S(1)}, u32[]{:S(2)}, u32[]{:S(2)}) collective-permute-start(bf16[512,512]{1,0:T(8,128)(2,1)S(1)} %get-tuple-element.33), channel_id=1, source_target_pairs={{0,1},{1,0},{2,3},{3,2},{4,5},{5,4},{6,7},{7,6},{8,9},{9,8},{10,11... | collective-permute-start | bytes 1572872 | tf_op jit(solution)/shard_map/ppermute | solution.py:204
  14.3 3.4 %collective-permute-start.13 = (bf16[512,256]{1,0:T(8,128)(2,1)S(1)}, bf16[512,256]{1,0:T(8,128)(2,1)S(1)}, u32[]{:S(2)}, u32[]{:S(2)}) collective-permute-start(bf16[512,256]{1,0:T(8,128)(2,1)S(1)} %get-tuple-element.43), channel_id=1, source_target_pairs={{0,1},{1,0},{2,3},{3,2},{4,5},{5,4},{6,7},{7,6},{8,9},{9,8},{10,11... | collective-permute-start | bytes 786440 | tf_op jit(solution)/shard_map/ppermute | solution.py:204
  14.6 5.0 %collective-permute-start.6 = (bf16[64,256]{1,0:T(8,128)(2,1)S(1)}, bf16[64,256]{1,0:T(8,128)(2,1)S(1)}, u32[]{:S(2)}, u32[]{:S(2)}) collective-permute-start(bf16[64,256]{1,0:T(8,128)(2,1)S(1)} %get-tuple-element.35), channel_id=1, source_target_pairs={{0,7},{1,6},{2,5},{3,4},{4,3},{5,2},{6,1},{7,0},{8,15},{9,14},{10,... | collective-permute-start | bytes 98312 | tf_op jit(solution)/shard_map/ppermute | solution.py:204
  16.3 3.4 %collective-permute-start.7 = (bf16[64,256]{1,0:T(8,128)(2,1)S(1)}, bf16[64,256]{1,0:T(8,128)(2,1)S(1)}, u32[]{:S(2)}, u32[]{:S(2)}) collective-permute-start(bf16[64,256]{1,0:T(8,128)(2,1)S(1)} %get-tuple-element.36), channel_id=1, source_target_pairs={{0,5},{1,4},{2,7},{3,6},{4,1},{5,0},{6,3},{7,2},{8,13},{9,12},{10,... | collective-permute-start | bytes 98312 | tf_op jit(solution)/shard_map/ppermute | solution.py:204
  16.5 3.4 %collective-permute-start.8 = (bf16[64,256]{1,0:T(8,128)(2,1)S(1)}, bf16[64,256]{1,0:T(8,128)(2,1)S(1)}, u32[]{:S(2)}, u32[]{:S(2)}) collective-permute-start(bf16[64,256]{1,0:T(8,128)(2,1)S(1)} %get-tuple-element.37), channel_id=1, source_target_pairs={{0,3},{1,2},{2,1},{3,0},{4,7},{5,6},{6,5},{7,4},{8,11},{9,10},{10,... | collective-permute-start | bytes 98312 | tf_op jit(solution)/shard_map/ppermute | solution.py:204
  18.0 9.4 %collective-permute-start.14 = (bf16[512,256]{1,0:T(8,128)(2,1)S(1)}, bf16[512,256]{1,0:T(8,128)(2,1)S(1)}, u32[]{:S(2)}, u32[]{:S(2)}) collective-permute-start(bf16[512,256]{1,0:T(8,128)(2,1)S(1)} %shard_map.93.ours), channel_id=1, source_target_pairs={{0,16},{16,0},{1,17},{17,1},{2,18},{18,2},{3,19},{19,3},{4,20},{20... | collective-permute-start | bytes 786440 | tf_op jit(solution)/shard_map/ppermute | solution.py:213
  19.8 7.6 %copy-start = (f32[512,256]{1,0:T(8,128)S(1)}, f32[512,256]{1,0:T(8,128)}, u32[]{:S(2)}) copy-start(f32[512,256]{1,0:T(8,128)} %v.1) | copy-start | bytes 1572868
  19.8 4.3 %collective-permute-start.9 = (bf16[64,256]{1,0:T(8,128)(2,1)S(1)}, bf16[64,256]{1,0:T(8,128)(2,1)S(1)}, u32[]{:S(2)}, u32[]{:S(2)}) collective-permute-start(bf16[64,256]{1,0:T(8,128)(2,1)S(1)} %get-tuple-element.39), channel_id=1, source_target_pairs={{0,9},{1,8},{2,11},{3,10},{4,13},{5,12},{6,15},{7,14},{8,1},{9,0},... | collective-permute-start | bytes 98312 | tf_op jit(solution)/shard_map/ppermute | solution.py:204
  24.2 4.3 %collective-permute-start.12 = (bf16[64,256]{1,0:T(8,128)(2,1)S(1)}, bf16[64,256]{1,0:T(8,128)(2,1)S(1)}, u32[]{:S(2)}, u32[]{:S(2)}) collective-permute-start(bf16[64,256]{1,0:T(8,128)(2,1)S(1)} %get-tuple-element.41.pair.after), channel_id=1, source_target_pairs={{0,7},{1,6},{2,5},{3,4},{4,3},{5,2},{6,1},{7,0},{8,15},{9,14},{10,... | collective-permute-start | bytes 98312 | tf_op jit(solution)/shard_map/ppermute | solution.py:204
  26.5 3.4 %collective-permute-start.11 = (bf16[64,256]{1,0:T(8,128)(2,1)S(1)}, bf16[64,256]{1,0:T(8,128)(2,1)S(1)}, u32[]{:S(2)}, u32[]{:S(2)}) collective-permute-start(bf16[64,256]{1,0:T(8,128)(2,1)S(1)} %get-tuple-element.41.pair.after), channel_id=1, source_target_pairs={{0,5},{1,4},{2,7},{3,6},{4,1},{5,0},{6,3},{7,2},{8,13},{9,12},{10,... | collective-permute-start | bytes 98312 | tf_op jit(solution)/shard_map/ppermute | solution.py:204
  26.7 3.3 %collective-permute-start.10 = (bf16[64,256]{1,0:T(8,128)(2,1)S(1)}, bf16[64,256]{1,0:T(8,128)(2,1)S(1)}, u32[]{:S(2)}, u32[]{:S(2)}) collective-permute-start(bf16[64,256]{1,0:T(8,128)(2,1)S(1)} %get-tuple-element.41.pair.after), channel_id=1, source_target_pairs={{0,3},{1,2},{2,1},{3,0},{4,7},{5,6},{6,5},{7,4},{8,11},{9,10},{10,... | collective-permute-start | bytes 98312 | tf_op jit(solution)/shard_map/ppermute | solution.py:204
  27.5 2.6 %collective-permute-start.15 = (bf16[512,256]{1,0:T(8,128)(2,1)S(1)}, bf16[512,256]{1,0:T(8,128)(2,1)S(1)}, u32[]{:S(2)}, u32[]{:S(2)}) collective-permute-start(bf16[512,256]{1,0:T(8,128)(2,1)S(1)} %get-tuple-element.44.refs_0_), channel_id=1, source_target_pairs={{0,1},{1,0},{2,3},{3,2},{4,5},{5,4},{6,7},{7,6},{8,9},{9,8},{10,11... | collective-permute-start | bytes 786440 | tf_op jit(solution)/shard_map/ppermute | solution.py:204
  30.8 3.2 %collective-permute-start.20 = (bf16[512,256]{1,0:T(8,128)(2,1)S(1)}, bf16[512,256]{1,0:T(8,128)(2,1)S(1)}, u32[]{:S(2)}, u32[]{:S(2)}) collective-permute-start(bf16[512,256]{1,0:T(8,128)(2,1)S(1)} %get-tuple-element.54), channel_id=1, source_target_pairs={{0,1},{1,0},{2,3},{3,2},{4,5},{5,4},{6,7},{7,6},{8,9},{9,8},{10,11... | collective-permute-start | bytes 786440 | tf_op jit(solution)/shard_map/ppermute | solution.py:204
  31.4 5.0 %collective-permute-start.16 = (bf16[128,256]{1,0:T(8,128)(2,1)S(1)}, bf16[128,256]{1,0:T(8,128)(2,1)S(1)}, u32[]{:S(2)}, u32[]{:S(2)}) collective-permute-start(bf16[128,256]{1,0:T(8,128)(2,1)S(1)} %get-tuple-element.48), channel_id=1, source_target_pairs={{0,9},{1,8},{2,11},{3,10},{4,13},{5,12},{6,15},{7,14},{8,1},{9,0},... | collective-permute-start | bytes 196616 | tf_op jit(solution)/shard_map/ppermute | solution.py:204
  34.0 8.7 %collective-permute-start.21 = (bf16[512,256]{1,0:T(8,128)(2,1)S(1)}, bf16[512,256]{1,0:T(8,128)(2,1)S(1)}, u32[]{:S(2)}, u32[]{:S(2)}) collective-permute-start(bf16[512,256]{1,0:T(8,128)(2,1)S(1)} %shard_map.98.ours), channel_id=1, source_target_pairs={{0,16},{16,0},{1,17},{17,1},{2,18},{18,2},{3,19},{19,3},{4,20},{20... | collective-permute-start | bytes 786440 | tf_op jit(solution)/shard_map/ppermute | solution.py:213
  36.4 4.1 %collective-permute-start.17 = (bf16[32,256]{1,0:T(8,128)(2,1)S(1)}, bf16[32,256]{1,0:T(8,128)(2,1)S(1)}, u32[]{:S(2)}, u32[]{:S(2)}) collective-permute-start(bf16[32,256]{1,0:T(8,128)(2,1)S(1)} %get-tuple-element.50), channel_id=1, source_target_pairs={{0,7},{1,6},{2,5},{3,4},{4,3},{5,2},{6,1},{7,0},{8,15},{9,14},{10,... | collective-permute-start | bytes 49160 | tf_op jit(solution)/shard_map/ppermute | solution.py:204
  38.8 3.2 %collective-permute-start.18 = (bf16[32,256]{1,0:T(8,128)(2,1)S(1)}, bf16[32,256]{1,0:T(8,128)(2,1)S(1)}, u32[]{:S(2)}, u32[]{:S(2)}) collective-permute-start(bf16[32,256]{1,0:T(8,128)(2,1)S(1)} %get-tuple-element.51), channel_id=1, source_target_pairs={{0,5},{1,4},{2,7},{3,6},{4,1},{5,0},{6,3},{7,2},{8,13},{9,12},{10,... | collective-permute-start | bytes 49160 | tf_op jit(solution)/shard_map/ppermute | solution.py:204
  38.9 3.2 %collective-permute-start.19 = (bf16[32,256]{1,0:T(8,128)(2,1)S(1)}, bf16[32,256]{1,0:T(8,128)(2,1)S(1)}, u32[]{:S(2)}, u32[]{:S(2)}) collective-permute-start(bf16[32,256]{1,0:T(8,128)(2,1)S(1)} %get-tuple-element.52), channel_id=1, source_target_pairs={{0,3},{1,2},{2,1},{3,0},{4,7},{5,6},{6,5},{7,4},{8,11},{9,10},{10,... | collective-permute-start | bytes 49160 | tf_op jit(solution)/shard_map/ppermute | solution.py:204

commit v7 on v5

--- a/solution.py
+++ b/solution.py
@@ -44,7 +44,7 @@
 
 
 FAR = 9
-NEAR = (0, 3, 5, 7)
+NEAR = (0, 3, 5, 6)
 OTHER_CORE = 1
 
 
@@ -76,7 +76,7 @@
         live = k < count
         for x in range(2):
             at = pl.multiple_of((far * 4 + near * 2 + x) * own, own)
-            core = far ^ (near | x)
+            core = far ^ near ^ x
             for h, out in enumerate((mine, theirs)):
                 rows = pl.ds(pl.multiple_of((low ^ (x * 2 + h) ^ core) * own, own), own)
                 tile = weights[k, rows, :]
@@ -124,7 +124,7 @@
     return gu
 
 
-def near_first_kernel(u, *refs):
+def near_kernel(u, *refs):
     *tiles, keep, send1, send2, send3, e, gv_send, e_theirs = refs
     own = u.shape[0] // 8
     gu = all_gu(u, *tiles, e, gv_send, e_theirs)
@@ -134,12 +134,14 @@
             out[x * own : (x + 1) * own, :] = gu[at : at + own].astype(out.dtype)
 
 
-def far_first_kernel(u, *refs):
+def halving_kernel(u, *refs):
     *tiles, keep, send, e, gv_send, e_theirs = refs
-    n = keep.shape[0]
+    own = u.shape[0] // 8
     gu = all_gu(u, *tiles, e, gv_send, e_theirs)
-    keep[...] = gu[:n]
-    send[...] = gu[n:].astype(BF)
+    for far in range(2):
+        at, to = far * 4 * own, slice(far * 2 * own, (far + 1) * 2 * own)
+        keep[to, :] = gu[at : at + 2 * own]
+        send[to, :] = gu[at + 2 * own : at + 4 * own].astype(BF)
 
 
 def ngram_keep_kernel(e, u, got, ours):
@@ -152,19 +154,19 @@
     total16[...] = now.astype(BF)
 
 
-def far_sum_kernel(keep, got, total, send1, send2, send3):
-    own = total.shape[0]
-    now = keep[...] + got[...].astype(F32)
-    for j, out in enumerate((total, send1, send2, send3)):
-        out[...] = now[j * own : (j + 1) * own].astype(out.dtype)
-
-
-def last_kernel(
-    doc_rate, ngram_rate, doc, total, got1, got2, got3, ours, ngram_got, v, doc_out, v_out
-):
-    v_out[...] = v[...] - ngram_rate * (ours[...].astype(F32) + ngram_got[...].astype(F32))
-    now = total[...] + got1[...].astype(F32) + got2[...].astype(F32) + got3[...].astype(F32)
-    doc_out[...] = doc[...] - doc_rate * now
+def halving_sum_kernel(keep, got, total, send):
+    n = total.shape[0]
+    total[...] = keep[:n, :] + got[:n, :].astype(F32)
+    send[...] = (keep[n:, :] + got[n:, :].astype(F32)).astype(BF)
+
+
+def ngram_last_kernel(rate, ours, got, v, v_out, written):
+    written[...] = jnp.zeros_like(written)
+    v_out[...] = v[...] - rate * (ours[...].astype(F32) + got[...].astype(F32))
+
+
+def doc_last_kernel(rate, doc, total, got, after, doc_out):
+    doc_out[...] = doc[...] - rate * (total[...] + got[...].astype(F32))
 
 
 def pair_update_kernel(rate, doc, other, total, got, doc_out, pair_out):
@@ -243,7 +245,7 @@
         return *outs, ours, swap_group(ours)
 
     keep, *send, ours, ngram_got = gradients(
-        near_first_kernel,
+        near_kernel,
         [shape(2 * own, R, F32)] + [shape(2 * own, R, BF)] * 3,
         pair,
         far,
@@ -273,28 +275,39 @@
     )
     v16_theirs = swap(v16, OTHER_CORE)
 
-    keep, send, ours, ngram_got = gradients(
-        far_first_kernel,
+    total, send, ours, ngram_got = gradients(
+        halving_kernel,
         [shape(half // 2, R, F32), shape(half // 2, R, BF)],
         pair,
         far,
         v16,
         v16_theirs,
     )
-    total, *send = call(
-        far_sum_kernel,
-        [shape(own, R, F32)] + [shape(own, R, BF)] * 3,
-        [VMEM] * 2,
-        (keep, swap(send, FAR)),
-        flops=LONG,
-    )
-    return call(
-        functools.partial(last_kernel, doc_rate, ngram_rate),
-        [shape(own, R, F32), shape(n, R, F32)],
-        [VMEM] * 8,
-        (doc_now, total, *exchange_near(send)[::-1], ours, ngram_got, ngram_now),
+    for mask, rows, hint in ((NEAR[2], 2 * own, LONG), (FAR, own, 0)):
+        total, send = call(
+            halving_sum_kernel,
+            [shape(rows, R, F32), shape(rows, R, BF)],
+            [VMEM] * 2,
+            (total, swap(send, mask)),
+            flops=hint,
+            read=0,
+        )
+    got = swap(send, NEAR[1])
+    ngram_now, written = call(
+        functools.partial(ngram_last_kernel, ngram_rate),
+        [shape(n, R, F32), shape(8, 128, F32)],
+        [VMEM] * 3,
+        (ours, ngram_got, ngram_now),
         read=0,
     )
+    (doc_now,) = call(
+        functools.partial(doc_last_kernel, doc_rate),
+        [shape(own, R, F32)],
+        [VMEM] * 3 + [ANY],
+        (doc_now, total, got, written),
+        read=0,
+    )
+    return doc_now, ngram_now
 
 
 def plain_kernel(docs, ngrams, counts, pmi, weights, u, v, gu, gv, s, e):

time: 44 us -> 43.8 us (level)
  starting transfers between devices: 27.3 us -> 25.6 us
  waiting for transfers between devices: 9.98 us -> 10.8 us
  Pallas kernels: 5.06 us -> 5.7 us
    ppermute x20 -> x19, starting transfers between devices: 24.1 us -> 22.4 us  [swap(): lax.ppermute(x, 'col', [(i, i ^ mask) for i in range(lax.axis_size('col'))])]
    ppermute x20 -> x19, waiting for transfers between devices: 9.07 us -> 9.9 us  [swap(): lax.ppermute(x, 'col', [(i, i ^ mask) for i in range(lax.axis_size('col'))])]
    pallas_call x13 -> x15, Pallas kernels: 5.06 us -> 5.7 us  [call(): pl.pallas_call(kernel, out_shape=outs, in_specs=in_specs, out_specs=[VMEM...]
  transfers between devices with their start and end apart: 22 -> 21, of which waited for: 11 -> 11; matrix products, arithmetic and copies ran while one was open for 0% -> 0% of each run, Pallas kernels for 7% -> 9%
where the time goes in v7:
time: 43.8 us; the launch traced here: 43.6 us
  starting transfers between devices  25.6 us (58%)
  waiting for transfers between devices  10.8 us (25%)
  Pallas kernels  5.7 us (13%)
  between operations  1.45 us (3%)
    ppermute x19, starting transfers between devices, swap(): lax.ppermute(x, 'col', [(i, i ^ mask) for i in range(lax.axis_size('col'))])  22.4 us
    ppermute x19, waiting for transfers between devices, swap(): lax.ppermute(x, 'col', [(i, i ^ mask) for i in range(lax.axis_size('col'))])  9.9 us
    pallas_call x15, Pallas kernels, call(): pl.pallas_call(kernel, out_shape=outs, in_specs=in_specs, out_specs=[VMEM...  5.7 us
    ppermute x2, starting transfers between devices, swap_group(): return lax.ppermute(x, 'grp', [(0, 1), (1, 0)])  3.25 us
    ppermute x2, waiting for transfers between devices, swap_group(): return lax.ppermute(x, 'grp', [(0, 1), (1, 0)])  0.9 us
  transfers between devices with their start and end apart: 21, of which 11 were waited for; matrix products, arithmetic and copies ran while one was open for 0% of the time, Pallas kernels for 9%

profile of v7, /device:TPU:0, one launch (start us, length us, event | category | flops | bytes accessed | tf_op | source)
XLA Modules:
  0.0 43.6 jit_solution(5486991110446866963)
XLA Ops:
  0.7 3.5 %collective-permute-start = (f32[32,256]{1,0:T(8,128)}, f32[32,256]{1,0:T(8,128)S(1)}, u32[]{:S(2)}, u32[]{:S(2)}) collective-permute-start(f32[32,256]{1,0:T(8,128)} %doc.1), channel_id=1, source_target_pairs={{0,9},{1,8},{2,11},{3,10},{4,13},{5,12},{6,15},{7,14},{8,1},{9,0},... | collective-permute-start | bytes 98312 | tf_op jit(solution)/shard_map/ppermute | solution.py:188
  4.9 2.2 %shard_map.86 = (bf16[512,512]{1,0:T(8,128)(2,1)S(1)}, bf16[512,512]{1,0:T(8,128)(2,1)S(1)}, bf16[512,256]{1,0:T(8,128)(2,1)S(1)}) custom-call(s32[1,1,16]{2,1,0:T(1,128)S(1)} %copy-done.2, s32[1,1,16]{2,1,0:T(1,128)S(1)} %copy-done.3, s32[1,1]{1,0:T(1,128)S(6)} %copy.9.counts, bf16[1,1,16,128,128]{4,3,2,1,0:T(8,128)(2,1)} %pmi_hbm.1, ...), custom_call_target="tpu_custom_call" | custom-call | bytes 1572996 | tf_op jit(solution)/shard_map/pallas_call | solution.py:35
  7.0 0.0 collective-permute-done.other
  7.1 2.6 %collective-permute-start.3 = (bf16[64,256]{1,0:T(8,128)(2,1)S(1)}, bf16[64,256]{1,0:T(8,128)(2,1)S(1)}, u32[]{:S(2)}, u32[]{:S(2)}) collective-permute-start(bf16[64,256]{1,0:T(8,128)(2,1)S(1)} %shard_map.87.pair), channel_id=1, source_target_pairs={{0,6},{1,7},{2,4},{3,5},{4,2},{5,3},{6,0},{7,1},{8,14},{9,15},{10,... | collective-permute-start | bytes 98312 | tf_op jit(solution)/shard_map/ppermute | solution.py:188
  9.7 0.5 %collective-permute-start.2 = (bf16[64,256]{1,0:T(8,128)(2,1)S(1)}, bf16[64,256]{1,0:T(8,128)(2,1)S(1)}, u32[]{:S(2)}, u32[]{:S(2)}) collective-permute-start(bf16[64,256]{1,0:T(8,128)(2,1)S(1)} %shard_map.87.pair), channel_id=1, source_target_pairs={{0,5},{1,4},{2,7},{3,6},{4,1},{5,0},{6,3},{7,2},{8,13},{9,12},{10,... | collective-permute-start | bytes 98312 | tf_op jit(solution)/shard_map/ppermute | solution.py:188
  10.1 0.2 collective-permute-start.1
  10.4 0.4 collective-permute-start.4
  10.8 0.1 collective-permute-start.5
  10.9 1.1 %collective-permute-done.3.far3 = bf16[64,256]{1,0:T(8,128)(2,1)S(1)} collective-permute-done((bf16[64,256]{1,0:T(8,128)(2,1)S(1)}, bf16[64,256]{1,0:T(8,128)(2,1)S(1)}, u32[]{:S(2)}, u32[]{:S(2)}) %collective-permute-start.3) | collective-permute-done | bytes 32800 | tf_op jit(solution)/shard_map/ppermute | solution.py:188
  12.0 1.0 %collective-permute-done.2.far2 = bf16[64,256]{1,0:T(8,128)(2,1)S(1)} collective-permute-done((bf16[64,256]{1,0:T(8,128)(2,1)S(1)}, bf16[64,256]{1,0:T(8,128)(2,1)S(1)}, u32[]{:S(2)}, u32[]{:S(2)}) %collective-permute-start.2) | collective-permute-done | bytes 32800 | tf_op jit(solution)/shard_map/ppermute | solution.py:188
  13.0 0.6 %collective-permute-done.1.far1 = bf16[64,256]{1,0:T(8,128)(2,1)S(1)} collective-permute-done((bf16[64,256]{1,0:T(8,128)(2,1)S(1)}, bf16[64,256]{1,0:T(8,128)(2,1)S(1)}, u32[]{:S(2)}, u32[]{:S(2)}) %collective-permute-start.1) | collective-permute-done | bytes 32800 | tf_op jit(solution)/shard_map/ppermute | solution.py:188
  13.6 0.0 collective-permute-done.4.refs_1_
  13.6 0.0 collective-permute-done.5.refs_3_.held
  13.6 0.7 %shard_map.89 = (f32[64,256]{1,0:T(8,128)S(1)}, bf16[64,256]{1,0:T(8,128)(2,1)S(1)}, bf16[64,256]{1,0:T(8,128)(2,1)S(1)}, bf16[64,256]{1,0:T(8,128)(2,1)S(1)}, b...) custom-call(bf16[256,256]{1,0:T(8,128)(2,1)S(1)} %shard_map.88.u, ...), custom_call_target="tpu_custom_call" | custom-call | flops 268435456 | bytes 1703936 | tf_op jit(solution)/shard_map/pallas_call | solution.py:35
  14.3 0.2 collective-permute-start.13
  14.4 1.9 %collective-permute-start.6 = (bf16[64,256]{1,0:T(8,128)(2,1)S(1)}, bf16[64,256]{1,0:T(8,128)(2,1)S(1)}, u32[]{:S(2)}, u32[]{:S(2)}) collective-permute-start(bf16[64,256]{1,0:T(8,128)(2,1)S(1)} %get-tuple-element.35), channel_id=1, source_target_pairs={{0,6},{1,7},{2,4},{3,5},{4,2},{5,3},{6,0},{7,1},{8,14},{9,15},{10,... | collective-permute-start | bytes 98312 | tf_op jit(solution)/shard_map/ppermute | solution.py:188
  16.3 0.0 collective-permute-start.7
  16.3 1.4 %collective-permute-start.8 = (bf16[64,256]{1,0:T(8,128)(2,1)S(1)}, bf16[64,256]{1,0:T(8,128)(2,1)S(1)}, u32[]{:S(2)}, u32[]{:S(2)}) collective-permute-start(bf16[64,256]{1,0:T(8,128)(2,1)S(1)} %get-tuple-element.37), channel_id=1, source_target_pairs={{0,3},{1,2},{2,1},{3,0},{4,7},{5,6},{6,5},{7,4},{8,11},{9,10},{10,... | collective-permute-start | bytes 98312 | tf_op jit(solution)/shard_map/ppermute | solution.py:188
  17.7 0.0 collective-permute-done.13.got
  17.7 0.3 shard_map.93.ours
  18.0 1.6 %collective-permute-start.14 = (bf16[512,256]{1,0:T(8,128)(2,1)S(1)}, bf16[512,256]{1,0:T(8,128)(2,1)S(1)}, u32[]{:S(2)}, u32[]{:S(2)}) collective-permute-start(bf16[512,256]{1,0:T(8,128)(2,1)S(1)} %shard_map.93.ours), channel_id=1, source_target_pairs={{0,16},{16,0},{1,17},{17,1},{2,18},{18,2},{3,19},{19,3},{4,20},{20... | collective-permute-start | bytes 786440 | tf_op jit(solution)/shard_map/ppermute | solution.py:197
  19.5 0.0 collective-permute-done.6.got1
  19.6 0.3 collective-permute-done.7.got2
  19.9 0.0 collective-permute-done.8.got3
  19.9 2.6 %collective-permute-start.9 = (bf16[64,256]{1,0:T(8,128)(2,1)S(1)}, bf16[64,256]{1,0:T(8,128)(2,1)S(1)}, u32[]{:S(2)}, u32[]{:S(2)}) collective-permute-start(bf16[64,256]{1,0:T(8,128)(2,1)S(1)} %get-tuple-element.39), channel_id=1, source_target_pairs={{0,9},{1,8},{2,11},{3,10},{4,13},{5,12},{6,15},{7,14},{8,1},{9,0},... | collective-permute-start | bytes 98312 | tf_op jit(solution)/shard_map/ppermute | solution.py:188
  22.5 1.7 %collective-permute-done.9.got = bf16[64,256]{1,0:T(8,128)(2,1)S(1)} collective-permute-done((bf16[64,256]{1,0:T(8,128)(2,1)S(1)}, bf16[64,256]{1,0:T(8,128)(2,1)S(1)}, u32[]{:S(2)}, u32[]{:S(2)}) %collective-permute-start.9) | collective-permute-done | bytes 32800 | tf_op jit(solution)/shard_map/ppermute | solution.py:188
  24.2 2.6 %collective-permute-start.12 = (bf16[64,256]{1,0:T(8,128)(2,1)S(1)}, bf16[64,256]{1,0:T(8,128)(2,1)S(1)}, u32[]{:S(2)}, u32[]{:S(2)}) collective-permute-start(bf16[64,256]{1,0:T(8,128)(2,1)S(1)} %get-tuple-element.41.pair.after), channel_id=1, source_target_pairs={{0,6},{1,7},{2,4},{3,5},{4,2},{5,3},{6,0},{7,1},{8,14},{9,15},{10,... | collective-permute-start | bytes 98312 | tf_op jit(solution)/shard_map/ppermute | solution.py:188
  26.8 0.0 collective-permute-start.11
  26.8 0.7 %collective-permute-start.10 = (bf16[64,256]{1,0:T(8,128)(2,1)S(1)}, bf16[64,256]{1,0:T(8,128)(2,1)S(1)}, u32[]{:S(2)}, u32[]{:S(2)}) collective-permute-start(bf16[64,256]{1,0:T(8,128)(2,1)S(1)} %get-tuple-element.41.pair.after), channel_id=1, source_target_pairs={{0,3},{1,2},{2,1},{3,0},{4,7},{5,6},{6,5},{7,4},{8,11},{9,10},{10,... | collective-permute-start | bytes 98312 | tf_op jit(solution)/shard_map/ppermute | solution.py:188
  27.5 0.1 shard_map.94
  27.6 0.3 collective-permute-start.15
  27.9 1.2 %collective-permute-done.12.far3 = bf16[64,256]{1,0:T(8,128)(2,1)S(1)} collective-permute-done((bf16[64,256]{1,0:T(8,128)(2,1)S(1)}, bf16[64,256]{1,0:T(8,128)(2,1)S(1)}, u32[]{:S(2)}, u32[]{:S(2)}) %collective-permute-start.12) | collective-permute-done | bytes 32800 | tf_op jit(solution)/shard_map/ppermute | solution.py:188
  29.1 1.3 %collective-permute-done.11.far2 = bf16[64,256]{1,0:T(8,128)(2,1)S(1)} collective-permute-done((bf16[64,256]{1,0:T(8,128)(2,1)S(1)}, bf16[64,256]{1,0:T(8,128)(2,1)S(1)}, u32[]{:S(2)}, u32[]{:S(2)}) %collective-permute-start.11) | collective-permute-done | bytes 32800 | tf_op jit(solution)/shard_map/ppermute | solution.py:188
  30.4 0.0 collective-permute-done.15.refs_1_
  30.4 0.7 %shard_map.95 = (f32[128,256]{1,0:T(8,128)S(1)}, bf16[128,256]{1,0:T(8,128)(2,1)S(1)}, bf16[256,512]{1,0:T(8,128)(2,1)S(1)}, bf16[512,256]{1,0:T(8,128)(2,1)S(1)}) custom-call(bf16[256,256]{1,0:T(8,128)(2,1)S(1)} %shard_map.92.u, bf16[512,256]{1,0:T(8,128)(2,1)S(1)} %get-tuple-element.44.refs_0_, bf16[512,256]{1,0:T(8,128)(2,1)S(1)} %collective-permute-done.15.refs_1_, ...), custom_call_target="tpu_custom_call" | custom-call | flops 268435456 | bytes 1703936 | tf_op jit(solution)/shard_map/pallas_call | solution.py:35
  31.1 0.2 collective-permute-start.19
  31.3 1.4 %collective-permute-start.16 = (bf16[128,256]{1,0:T(8,128)(2,1)S(1)}, bf16[128,256]{1,0:T(8,128)(2,1)S(1)}, u32[]{:S(2)}, u32[]{:S(2)}) collective-permute-start(bf16[128,256]{1,0:T(8,128)(2,1)S(1)} %get-tuple-element.46), channel_id=1, source_target_pairs={{0,5},{1,4},{2,7},{3,6},{4,1},{5,0},{6,3},{7,2},{8,13},{9,12},{10,... | collective-permute-start | bytes 196616 | tf_op jit(solution)/shard_map/ppermute | solution.py:188
  32.7 0.0 collective-permute-done.19.got
  32.7 0.3 shard_map.98.ours
  33.0 1.7 %collective-permute-start.20 = (bf16[512,256]{1,0:T(8,128)(2,1)S(1)}, bf16[512,256]{1,0:T(8,128)(2,1)S(1)}, u32[]{:S(2)}, u32[]{:S(2)}) collective-permute-start(bf16[512,256]{1,0:T(8,128)(2,1)S(1)} %shard_map.98.ours), channel_id=1, source_target_pairs={{0,16},{16,0},{1,17},{17,1},{2,18},{18,2},{3,19},{19,3},{4,20},{20... | collective-permute-start | bytes 786440 | tf_op jit(solution)/shard_map/ppermute | solution.py:197
  34.6 0.6 %collective-permute-done.16.got = bf16[128,256]{1,0:T(8,128)(2,1)S(1)} collective-permute-done((bf16[128,256]{1,0:T(8,128)(2,1)S(1)}, bf16[128,256]{1,0:T(8,128)(2,1)S(1)}, u32[]{:S(2)}, u32[]{:S(2)}) %collective-permute-start.16) | collective-permute-done | bytes 65568 | tf_op jit(solution)/shard_map/ppermute | solution.py:188
  35.3 2.9 %collective-permute-start.17 = (bf16[64,256]{1,0:T(8,128)(2,1)S(1)}, bf16[64,256]{1,0:T(8,128)(2,1)S(1)}, u32[]{:S(2)}, u32[]{:S(2)}) collective-permute-start(bf16[64,256]{1,0:T(8,128)(2,1)S(1)} %get-tuple-element.48), channel_id=1, source_target_pairs={{0,9},{1,8},{2,11},{3,10},{4,13},{5,12},{6,15},{7,14},{8,1},{9,0},... | collective-permute-start | bytes 98312 | tf_op jit(solution)/shard_map/ppermute | solution.py:188
  38.1 1.6 %collective-permute-done.17.got = bf16[64,256]{1,0:T(8,128)(2,1)S(1)} collective-permute-done((bf16[64,256]{1,0:T(8,128)(2,1)S(1)}, bf16[64,256]{1,0:T(8,128)(2,1)S(1)}, u32[]{:S(2)}, u32[]{:S(2)}) %collective-permute-start.17) | collective-permute-done | bytes 32800 | tf_op jit(solution)/shard_map/ppermute | solution.py:188
  39.8 1.0 %collective-permute-start.18 = (bf16[32,256]{1,0:T(8,128)(2,1)S(1)}, bf16[32,256]{1,0:T(8,128)(2,1)S(1)}, u32[]{:S(2)}, u32[]{:S(2)}) collective-permute-start(bf16[32,256]{1,0:T(8,128)(2,1)S(1)} %get-tuple-element.50), channel_id=1, source_target_pairs={{0,3},{1,2},{2,1},{3,0},{4,7},{5,6},{6,5},{7,4},{8,11},{9,10},{10,... | collective-permute-start | bytes 49160 | tf_op jit(solution)/shard_map/ppermute | solution.py:188
  40.8 0.9 %collective-permute-done.20.got = bf16[512,256]{1,0:T(8,128)(2,1)S(1)} collective-permute-done((bf16[512,256]{1,0:T(8,128)(2,1)S(1)}, bf16[512,256]{1,0:T(8,128)(2,1)S(1)}, u32[]{:S(2)}, u32[]{:S(2)}) %collective-permute-start.20) | collective-permute-done | bytes 262176 | tf_op jit(solution)/shard_map/ppermute | solution.py:197
  41.7 0.9 %shard_map.99 = (f32[512,256]{1,0:T(8,128)}, f32[8,128]{1,0:T(8,128)S(1)}) custom-call(bf16[512,256]{1,0:T(8,128)(2,1)S(1)} %shard_map.98.ours, bf16[512,256]{1,0:T(8,128)(2,1)S(1)} %collective-permute-done.20.got, f32[512,256]{1,0:T(8,128)S(1)} %get-tuple-element.53.v), custom_call_target="tpu_custom_call" | custom-call | tf_op jit(solution)/shard_map/pallas_call | solution.py:35
  42.6 0.4 collective-permute-done.18.got
  43.0 0.6 %shard_map.100 = f32[32,256]{1,0:T(8,128)} custom-call(f32[32,256]{1,0:T(8,128)S(1)} %get-tuple-element.40.doc, f32[32,256]{1,0:T(8,128)S(1)} %get-tuple-element.49.total, bf16[32,256]{1,0:T(8,128)(2,1)S(1)} %collective-permute-done.18.got, f32[8,128]{1,0:T(8,128)S(1)} %get-tuple-element.54.after), custom_call_target="tpu_custom_call" | custom-call | tf_op jit(solution)/shard_map/pallas_call | solution.py:35
  (17 shorter events, 0.1 us)
Async XLA Ops:
  0.6 4.2 %copy-start.3 = (s32[1,1,16]{2,1,0:T(1,128)S(1)}, s32[1,1,16]{2,1,0:T(1,128)}, u32[]{:S(2)}) copy-start(s32[1,1,16]{2,1,0:T(1,128)} %ngrams.1) | copy-start | bytes 196
  0.6 4.2 %copy-start.2 = (s32[1,1,16]{2,1,0:T(1,128)S(1)}, s32[1,1,16]{2,1,0:T(1,128)}, u32[]{:S(2)}) copy-start(s32[1,1,16]{2,1,0:T(1,128)} %docs.1) | copy-start | bytes 196
  0.7 6.4 %collective-permute-start = (f32[32,256]{1,0:T(8,128)}, f32[32,256]{1,0:T(8,128)S(1)}, u32[]{:S(2)}, u32[]{:S(2)}) collective-permute-start(f32[32,256]{1,0:T(8,128)} %doc.1), channel_id=1, source_target_pairs={{0,9},{1,8},{2,11},{3,10},{4,13},{5,12},{6,15},{7,14},{8,1},{9,0},... | collective-permute-start | bytes 98312 | tf_op jit(solution)/shard_map/ppermute | solution.py:188
  4.9 2.2 %copy-start.1 = (f32[32,256]{1,0:T(8,128)S(1)}, f32[32,256]{1,0:T(8,128)}, u32[]{:S(2)}) copy-start(f32[32,256]{1,0:T(8,128)} %doc.1) | copy-start | bytes 98308
  7.1 4.9 %collective-permute-start.3 = (bf16[64,256]{1,0:T(8,128)(2,1)S(1)}, bf16[64,256]{1,0:T(8,128)(2,1)S(1)}, u32[]{:S(2)}, u32[]{:S(2)}) collective-permute-start(bf16[64,256]{1,0:T(8,128)(2,1)S(1)} %shard_map.87.pair), channel_id=1, source_target_pairs={{0,6},{1,7},{2,4},{3,5},{4,2},{5,3},{6,0},{7,1},{8,14},{9,15},{10,... | collective-permute-start | bytes 98312 | tf_op jit(solution)/shard_map/ppermute | solution.py:188
  9.7 3.3 %collective-permute-start.2 = (bf16[64,256]{1,0:T(8,128)(2,1)S(1)}, bf16[64,256]{1,0:T(8,128)(2,1)S(1)}, u32[]{:S(2)}, u32[]{:S(2)}) collective-permute-start(bf16[64,256]{1,0:T(8,128)(2,1)S(1)} %shard_map.87.pair), channel_id=1, source_target_pairs={{0,5},{1,4},{2,7},{3,6},{4,1},{5,0},{6,3},{7,2},{8,13},{9,12},{10,... | collective-permute-start | bytes 98312 | tf_op jit(solution)/shard_map/ppermute | solution.py:188
  10.1 3.4 %collective-permute-start.1 = (bf16[64,256]{1,0:T(8,128)(2,1)S(1)}, bf16[64,256]{1,0:T(8,128)(2,1)S(1)}, u32[]{:S(2)}, u32[]{:S(2)}) collective-permute-start(bf16[64,256]{1,0:T(8,128)(2,1)S(1)} %shard_map.87.pair), channel_id=1, source_target_pairs={{0,3},{1,2},{2,1},{3,0},{4,7},{5,6},{6,5},{7,4},{8,11},{9,10},{10,... | collective-permute-start | bytes 98312 | tf_op jit(solution)/shard_map/ppermute | solution.py:188
  10.4 3.2 %collective-permute-start.4 = (bf16[512,256]{1,0:T(8,128)(2,1)S(1)}, bf16[512,256]{1,0:T(8,128)(2,1)S(1)}, u32[]{:S(2)}, u32[]{:S(2)}) collective-permute-start(bf16[512,256]{1,0:T(8,128)(2,1)S(1)} %get-tuple-element.31.refs_0_), channel_id=1, source_target_pairs={{0,1},{1,0},{2,3},{3,2},{4,5},{5,4},{6,7},{7,6},{8,9},{9,8},{10,11... | collective-permute-start | bytes 786440 | tf_op jit(solution)/shard_map/ppermute | solution.py:188
  10.8 2.8 %collective-permute-start.5 = (bf16[512,512]{1,0:T(8,128)(2,1)S(1)}, bf16[512,512]{1,0:T(8,128)(2,1)S(1)}, u32[]{:S(2)}, u32[]{:S(2)}) collective-permute-start(bf16[512,512]{1,0:T(8,128)(2,1)S(1)} %get-tuple-element.33), channel_id=1, source_target_pairs={{0,1},{1,0},{2,3},{3,2},{4,5},{5,4},{6,7},{7,6},{8,9},{9,8},{10,11... | collective-permute-start | bytes 1572872 | tf_op jit(solution)/shard_map/ppermute | solution.py:188
  14.3 3.4 %collective-permute-start.13 = (bf16[512,256]{1,0:T(8,128)(2,1)S(1)}, bf16[512,256]{1,0:T(8,128)(2,1)S(1)}, u32[]{:S(2)}, u32[]{:S(2)}) collective-permute-start(bf16[512,256]{1,0:T(8,128)(2,1)S(1)} %get-tuple-element.43), channel_id=1, source_target_pairs={{0,1},{1,0},{2,3},{3,2},{4,5},{5,4},{6,7},{7,6},{8,9},{9,8},{10,11... | collective-permute-start | bytes 786440 | tf_op jit(solution)/shard_map/ppermute | solution.py:188
  14.4 5.1 %collective-permute-start.6 = (bf16[64,256]{1,0:T(8,128)(2,1)S(1)}, bf16[64,256]{1,0:T(8,128)(2,1)S(1)}, u32[]{:S(2)}, u32[]{:S(2)}) collective-permute-start(bf16[64,256]{1,0:T(8,128)(2,1)S(1)} %get-tuple-element.35), channel_id=1, source_target_pairs={{0,6},{1,7},{2,4},{3,5},{4,2},{5,3},{6,0},{7,1},{8,14},{9,15},{10,... | collective-permute-start | bytes 98312 | tf_op jit(solution)/shard_map/ppermute | solution.py:188
  16.3 3.6 %collective-permute-start.7 = (bf16[64,256]{1,0:T(8,128)(2,1)S(1)}, bf16[64,256]{1,0:T(8,128)(2,1)S(1)}, u32[]{:S(2)}, u32[]{:S(2)}) collective-permute-start(bf16[64,256]{1,0:T(8,128)(2,1)S(1)} %get-tuple-element.36), channel_id=1, source_target_pairs={{0,5},{1,4},{2,7},{3,6},{4,1},{5,0},{6,3},{7,2},{8,13},{9,12},{10,... | collective-permute-start | bytes 98312 | tf_op jit(solution)/shard_map/ppermute | solution.py:188
  16.3 3.6 %collective-permute-start.8 = (bf16[64,256]{1,0:T(8,128)(2,1)S(1)}, bf16[64,256]{1,0:T(8,128)(2,1)S(1)}, u32[]{:S(2)}, u32[]{:S(2)}) collective-permute-start(bf16[64,256]{1,0:T(8,128)(2,1)S(1)} %get-tuple-element.37), channel_id=1, source_target_pairs={{0,3},{1,2},{2,1},{3,0},{4,7},{5,6},{6,5},{7,4},{8,11},{9,10},{10,... | collective-permute-start | bytes 98312 | tf_op jit(solution)/shard_map/ppermute | solution.py:188
  18.0 9.5 %collective-permute-start.14 = (bf16[512,256]{1,0:T(8,128)(2,1)S(1)}, bf16[512,256]{1,0:T(8,128)(2,1)S(1)}, u32[]{:S(2)}, u32[]{:S(2)}) collective-permute-start(bf16[512,256]{1,0:T(8,128)(2,1)S(1)} %shard_map.93.ours), channel_id=1, source_target_pairs={{0,16},{16,0},{1,17},{17,1},{2,18},{18,2},{3,19},{19,3},{4,20},{20... | collective-permute-start | bytes 786440 | tf_op jit(solution)/shard_map/ppermute | solution.py:197
  19.9 7.6 %copy-start = (f32[512,256]{1,0:T(8,128)S(1)}, f32[512,256]{1,0:T(8,128)}, u32[]{:S(2)}) copy-start(f32[512,256]{1,0:T(8,128)} %v.1) | copy-start | bytes 1572868
  19.9 4.3 %collective-permute-start.9 = (bf16[64,256]{1,0:T(8,128)(2,1)S(1)}, bf16[64,256]{1,0:T(8,128)(2,1)S(1)}, u32[]{:S(2)}, u32[]{:S(2)}) collective-permute-start(bf16[64,256]{1,0:T(8,128)(2,1)S(1)} %get-tuple-element.39), channel_id=1, source_target_pairs={{0,9},{1,8},{2,11},{3,10},{4,13},{5,12},{6,15},{7,14},{8,1},{9,0},... | collective-permute-start | bytes 98312 | tf_op jit(solution)/shard_map/ppermute | solution.py:188
  24.2 4.9 %collective-permute-start.12 = (bf16[64,256]{1,0:T(8,128)(2,1)S(1)}, bf16[64,256]{1,0:T(8,128)(2,1)S(1)}, u32[]{:S(2)}, u32[]{:S(2)}) collective-permute-start(bf16[64,256]{1,0:T(8,128)(2,1)S(1)} %get-tuple-element.41.pair.after), channel_id=1, source_target_pairs={{0,6},{1,7},{2,4},{3,5},{4,2},{5,3},{6,0},{7,1},{8,14},{9,15},{10,... | collective-permute-start | bytes 98312 | tf_op jit(solution)/shard_map/ppermute | solution.py:188
  26.8 3.7 %collective-permute-start.11 = (bf16[64,256]{1,0:T(8,128)(2,1)S(1)}, bf16[64,256]{1,0:T(8,128)(2,1)S(1)}, u32[]{:S(2)}, u32[]{:S(2)}) collective-permute-start(bf16[64,256]{1,0:T(8,128)(2,1)S(1)} %get-tuple-element.41.pair.after), channel_id=1, source_target_pairs={{0,5},{1,4},{2,7},{3,6},{4,1},{5,0},{6,3},{7,2},{8,13},{9,12},{10,... | collective-permute-start | bytes 98312 | tf_op jit(solution)/shard_map/ppermute | solution.py:188
  26.8 3.7 %collective-permute-start.10 = (bf16[64,256]{1,0:T(8,128)(2,1)S(1)}, bf16[64,256]{1,0:T(8,128)(2,1)S(1)}, u32[]{:S(2)}, u32[]{:S(2)}) collective-permute-start(bf16[64,256]{1,0:T(8,128)(2,1)S(1)} %get-tuple-element.41.pair.after), channel_id=1, source_target_pairs={{0,3},{1,2},{2,1},{3,0},{4,7},{5,6},{6,5},{7,4},{8,11},{9,10},{10,... | collective-permute-start | bytes 98312 | tf_op jit(solution)/shard_map/ppermute | solution.py:188
  27.6 2.8 %collective-permute-start.15 = (bf16[512,256]{1,0:T(8,128)(2,1)S(1)}, bf16[512,256]{1,0:T(8,128)(2,1)S(1)}, u32[]{:S(2)}, u32[]{:S(2)}) collective-permute-start(bf16[512,256]{1,0:T(8,128)(2,1)S(1)} %get-tuple-element.44.refs_0_), channel_id=1, source_target_pairs={{0,1},{1,0},{2,3},{3,2},{4,5},{5,4},{6,7},{7,6},{8,9},{9,8},{10,11... | collective-permute-start | bytes 786440 | tf_op jit(solution)/shard_map/ppermute | solution.py:188
  31.1 1.6 %collective-permute-start.19 = (bf16[512,256]{1,0:T(8,128)(2,1)S(1)}, bf16[512,256]{1,0:T(8,128)(2,1)S(1)}, u32[]{:S(2)}, u32[]{:S(2)}) collective-permute-start(bf16[512,256]{1,0:T(8,128)(2,1)S(1)} %get-tuple-element.52), channel_id=1, source_target_pairs={{0,1},{1,0},{2,3},{3,2},{4,5},{5,4},{6,7},{7,6},{8,9},{9,8},{10,11... | collective-permute-start | bytes 786440 | tf_op jit(solution)/shard_map/ppermute | solution.py:188
  31.3 3.9 %collective-permute-start.16 = (bf16[128,256]{1,0:T(8,128)(2,1)S(1)}, bf16[128,256]{1,0:T(8,128)(2,1)S(1)}, u32[]{:S(2)}, u32[]{:S(2)}) collective-permute-start(bf16[128,256]{1,0:T(8,128)(2,1)S(1)} %get-tuple-element.46), channel_id=1, source_target_pairs={{0,5},{1,4},{2,7},{3,6},{4,1},{5,0},{6,3},{7,2},{8,13},{9,12},{10,... | collective-permute-start | bytes 196616 | tf_op jit(solution)/shard_map/ppermute | solution.py:188
  33.0 8.7 %collective-permute-start.20 = (bf16[512,256]{1,0:T(8,128)(2,1)S(1)}, bf16[512,256]{1,0:T(8,128)(2,1)S(1)}, u32[]{:S(2)}, u32[]{:S(2)}) collective-permute-start(bf16[512,256]{1,0:T(8,128)(2,1)S(1)} %shard_map.98.ours), channel_id=1, source_target_pairs={{0,16},{16,0},{1,17},{17,1},{2,18},{18,2},{3,19},{19,3},{4,20},{20... | collective-permute-start | bytes 786440 | tf_op jit(solution)/shard_map/ppermute | solution.py:197
  35.3 4.5 %collective-permute-start.17 = (bf16[64,256]{1,0:T(8,128)(2,1)S(1)}, bf16[64,256]{1,0:T(8,128)(2,1)S(1)}, u32[]{:S(2)}, u32[]{:S(2)}) collective-permute-start(bf16[64,256]{1,0:T(8,128)(2,1)S(1)} %get-tuple-element.48), channel_id=1, source_target_pairs={{0,9},{1,8},{2,11},{3,10},{4,13},{5,12},{6,15},{7,14},{8,1},{9,0},... | collective-permute-start | bytes 98312 | tf_op jit(solution)/shard_map/ppermute | solution.py:188
  39.8 3.2 %collective-permute-start.18 = (bf16[32,256]{1,0:T(8,128)(2,1)S(1)}, bf16[32,256]{1,0:T(8,128)(2,1)S(1)}, u32[]{:S(2)}, u32[]{:S(2)}) collective-permute-start(bf16[32,256]{1,0:T(8,128)(2,1)S(1)} %get-tuple-element.50), channel_id=1, source_target_pairs={{0,3},{1,2},{2,1},{3,0},{4,7},{5,6},{6,5},{7,4},{8,11},{9,10},{10,... | collective-permute-start | bytes 49160 | tf_op jit(solution)/shard_map/ppermute | solution.py:188

commit v8 on v6

--- a/solution.py
+++ b/solution.py
@@ -49,18 +49,27 @@
 
 
 def place_kernel(
-    docs, ngrams, counts, pmi_hbm, weights_hbm, v_hbm, mine, theirs, v16, pmi, weights, v, sems, v_sem
+    docs_hbm, ngrams_hbm, counts_hbm, pmi_hbm, weights_hbm, v_hbm, mine, theirs, v16,
+    docs, ngrams, counts, pmi, weights, v, small_sems, sems, v_sem,
 ):
     slots = pmi.shape[0]
     parts = sems.shape[1]
-    v_copy = pltpu.make_async_copy(v_hbm, v, v_sem)
-    v_copy.start()
+    small = [
+        pltpu.make_async_copy(src, dst, small_sems.at[i])
+        for i, (src, dst) in enumerate(((docs_hbm, docs), (ngrams_hbm, ngrams), (counts_hbm, counts)))
+    ]
+    for copy in small:
+        copy.start()
     copies = []
     for a, (src, dst) in enumerate(((weights_hbm, weights), (pmi_hbm, pmi))):
         for i in range(parts):
             some = pl.ds(i * (slots // parts), slots // parts)
             copies.append(pltpu.make_async_copy(src.at[0, 0, some], dst.at[some], sems.at[a, i]))
             copies[-1].start()
+    v_copy = pltpu.make_async_copy(v_hbm, v, v_sem)
+    v_copy.start()
+    for copy in small:
+        copy.wait()
     half = mine.shape[0] // 2
     me = lax.axis_index("col")
     low, my_z = me & 3, me >> 2
@@ -225,12 +234,16 @@
     mine, theirs, v16 = call(
         place_kernel,
         [shape(2 * half, n, BF), shape(2 * half, n, BF), shape(n, R, BF)],
-        [SMEM] * 3 + [HBM] * 3,
+        [HBM] * 6,
         (block_docs, block_ngrams, block_counts, pmi, weights, ngram_now),
         [
+            pltpu.SMEM(block_docs.shape, jnp.int32),
+            pltpu.SMEM(block_ngrams.shape, jnp.int32),
+            pltpu.SMEM(block_counts.shape, jnp.int32),
             pltpu.VMEM((slots, BLK, BLK), BF),
             pltpu.VMEM((slots, BLK, BLK), BF),
             pltpu.VMEM((n, R), F32),
+            pltpu.SemaphoreType.DMA((3,)),
             pltpu.SemaphoreType.DMA((2, 4)),
             pltpu.SemaphoreType.DMA,
         ],

time: 43.8 us -> 43.8 us (level)
  starting transfers between devices: 26.9 us -> 27.9 us
  Pallas kernels: 5.1 us -> 4.58 us
  waiting for transfers between devices: 10.1 us -> 9.62 us
    ppermute x20, starting transfers between devices: 23.7 us -> 24.8 us  [swap(): lax.ppermute(x, 'col', [(i, i ^ mask) for i in range(lax.axis_size('col'))])]
    pallas_call x14, Pallas kernels: 5.1 us -> 4.58 us  [call(): pl.pallas_call(kernel, out_shape=outs, in_specs=in_specs, out_specs=[VMEM...]
    ppermute x20, waiting for transfers between devices: 9.45 us -> 8.93 us  [swap(): lax.ppermute(x, 'col', [(i, i ^ mask) for i in range(lax.axis_size('col'))])]
  transfers between devices with their start and end apart: 22 -> 22, of which waited for: 12 -> 10; matrix products, arithmetic and copies ran while one was open for 0% -> 0% of each run, Pallas kernels for 7% -> 6%
where the time goes in v8:
time: 43.8 us; the launch traced here: 43.6 us
  starting transfers between devices  27.9 us (64%)
  waiting for transfers between devices  9.62 us (22%)
  Pallas kernels  4.58 us (10%)
  between operations  1.45 us (3%)
    ppermute x20, starting transfers between devices, swap(): lax.ppermute(x, 'col', [(i, i ^ mask) for i in range(lax.axis_size('col'))])  24.8 us
    ppermute x20, waiting for transfers between devices, swap(): lax.ppermute(x, 'col', [(i, i ^ mask) for i in range(lax.axis_size('col'))])  8.93 us
    pallas_call x14, Pallas kernels, call(): pl.pallas_call(kernel, out_shape=outs, in_specs=in_specs, out_specs=[VMEM...  4.58 us
    ppermute x2, starting transfers between devices, swap_group(): return lax.ppermute(x, 'grp', [(0, 1), (1, 0)])  3.18 us
  transfers between devices with their start and end apart: 22, of which 10 were waited for; matrix products, arithmetic and copies ran while one was open for 0% of the time, Pallas kernels for 6%

profile of v8, /device:TPU:0, one launch (start us, length us, event | category | flops | bytes accessed | tf_op | source)
XLA Modules:
  0.0 43.6 jit_solution(4575372078667010047)
XLA Ops:
  0.7 3.5 %collective-permute-start = (f32[32,256]{1,0:T(8,128)}, f32[32,256]{1,0:T(8,128)S(1)}, u32[]{:S(2)}, u32[]{:S(2)}) collective-permute-start(f32[32,256]{1,0:T(8,128)} %doc.1), channel_id=1, source_target_pairs={{0,9},{1,8},{2,11},{3,10},{4,13},{5,12},{6,15},{7,14},{8,1},{9,0},... | collective-permute-start | bytes 98312 | tf_op jit(solution)/shard_map/ppermute | solution.py:213
  4.9 1.6 %shard_map.86 = (bf16[512,512]{1,0:T(8,128)(2,1)S(1)}, bf16[512,512]{1,0:T(8,128)(2,1)S(1)}, bf16[512,256]{1,0:T(8,128)(2,1)S(1)}) custom-call(s32[1,1,16]{2,1,0:T(1,128)S(1)} %copy-done.2, s32[1,1,16]{2,1,0:T(1,128)S(1)} %copy-done.3, s32[1,1]{1,0:T(1,128)S(6)} %copy.9.counts_hbm, bf16[1,1,16,128,128]{4,3,2,1,0:T(8,128)(2,1)} %pmi_hbm.1, ...), custom_call_target="tpu_custom_call" | custom-call | bytes 1572996 | tf_op jit(solution)/shard_map/pallas_call | solution.py:35
  6.5 0.0 collective-permute-done.other
  6.6 2.8 %collective-permute-start.3 = (bf16[64,256]{1,0:T(8,128)(2,1)S(1)}, bf16[64,256]{1,0:T(8,128)(2,1)S(1)}, u32[]{:S(2)}, u32[]{:S(2)}) collective-permute-start(bf16[64,256]{1,0:T(8,128)(2,1)S(1)} %shard_map.87.pair), channel_id=1, source_target_pairs={{0,7},{1,6},{2,5},{3,4},{4,3},{5,2},{6,1},{7,0},{8,15},{9,14},{10,... | collective-permute-start | bytes 98312 | tf_op jit(solution)/shard_map/ppermute | solution.py:213
  9.4 0.1 collective-permute-start.2
  9.5 0.7 %collective-permute-start.1 = (bf16[64,256]{1,0:T(8,128)(2,1)S(1)}, bf16[64,256]{1,0:T(8,128)(2,1)S(1)}, u32[]{:S(2)}, u32[]{:S(2)}) collective-permute-start(bf16[64,256]{1,0:T(8,128)(2,1)S(1)} %shard_map.87.pair), channel_id=1, source_target_pairs={{0,3},{1,2},{2,1},{3,0},{4,7},{5,6},{6,5},{7,4},{8,11},{9,10},{10,... | collective-permute-start | bytes 98312 | tf_op jit(solution)/shard_map/ppermute | solution.py:213
  10.1 0.1 collective-permute-start.4
  10.2 0.5 %collective-permute-start.5 = (bf16[512,512]{1,0:T(8,128)(2,1)S(1)}, bf16[512,512]{1,0:T(8,128)(2,1)S(1)}, u32[]{:S(2)}, u32[]{:S(2)}) collective-permute-start(bf16[512,512]{1,0:T(8,128)(2,1)S(1)} %get-tuple-element.33), channel_id=1, source_target_pairs={{0,1},{1,0},{2,3},{3,2},{4,5},{5,4},{6,7},{7,6},{8,9},{9,8},{10,11... | collective-permute-start | bytes 1572872 | tf_op jit(solution)/shard_map/ppermute | solution.py:213
  10.6 0.4 %collective-permute-done.3.far3 = bf16[64,256]{1,0:T(8,128)(2,1)S(1)} collective-permute-done((bf16[64,256]{1,0:T(8,128)(2,1)S(1)}, bf16[64,256]{1,0:T(8,128)(2,1)S(1)}, u32[]{:S(2)}, u32[]{:S(2)}) %collective-permute-start.3) | collective-permute-done | bytes 32800 | tf_op jit(solution)/shard_map/ppermute | solution.py:213
  11.1 1.9 %collective-permute-done.2.far2 = bf16[64,256]{1,0:T(8,128)(2,1)S(1)} collective-permute-done((bf16[64,256]{1,0:T(8,128)(2,1)S(1)}, bf16[64,256]{1,0:T(8,128)(2,1)S(1)}, u32[]{:S(2)}, u32[]{:S(2)}) %collective-permute-start.2) | collective-permute-done | bytes 32800 | tf_op jit(solution)/shard_map/ppermute | solution.py:213
  12.9 0.0 collective-permute-done.1.far1
  12.9 0.0 collective-permute-done.4.refs_1_
  13.0 0.0 collective-permute-done.5.refs_3_.held
  13.0 0.6 %shard_map.89 = (f32[64,256]{1,0:T(8,128)S(1)}, bf16[64,256]{1,0:T(8,128)(2,1)S(1)}, bf16[64,256]{1,0:T(8,128)(2,1)S(1)}, bf16[64,256]{1,0:T(8,128)(2,1)S(1)}, b...) custom-call(bf16[256,256]{1,0:T(8,128)(2,1)S(1)} %shard_map.88.u, ...), custom_call_target="tpu_custom_call" | custom-call | flops 268435456 | bytes 1703936 | tf_op jit(solution)/shard_map/pallas_call | solution.py:35
  13.6 0.5 %collective-permute-start.13 = (bf16[512,256]{1,0:T(8,128)(2,1)S(1)}, bf16[512,256]{1,0:T(8,128)(2,1)S(1)}, u32[]{:S(2)}, u32[]{:S(2)}) collective-permute-start(bf16[512,256]{1,0:T(8,128)(2,1)S(1)} %get-tuple-element.43), channel_id=1, source_target_pairs={{0,1},{1,0},{2,3},{3,2},{4,5},{5,4},{6,7},{7,6},{8,9},{9,8},{10,11... | collective-permute-start | bytes 786440 | tf_op jit(solution)/shard_map/ppermute | solution.py:213
  14.1 1.7 %collective-permute-start.6 = (bf16[64,256]{1,0:T(8,128)(2,1)S(1)}, bf16[64,256]{1,0:T(8,128)(2,1)S(1)}, u32[]{:S(2)}, u32[]{:S(2)}) collective-permute-start(bf16[64,256]{1,0:T(8,128)(2,1)S(1)} %get-tuple-element.35), channel_id=1, source_target_pairs={{0,7},{1,6},{2,5},{3,4},{4,3},{5,2},{6,1},{7,0},{8,15},{9,14},{10,... | collective-permute-start | bytes 98312 | tf_op jit(solution)/shard_map/ppermute | solution.py:213
  15.7 0.2 collective-permute-start.7
  15.9 1.1 %collective-permute-start.8 = (bf16[64,256]{1,0:T(8,128)(2,1)S(1)}, bf16[64,256]{1,0:T(8,128)(2,1)S(1)}, u32[]{:S(2)}, u32[]{:S(2)}) collective-permute-start(bf16[64,256]{1,0:T(8,128)(2,1)S(1)} %get-tuple-element.37), channel_id=1, source_target_pairs={{0,3},{1,2},{2,1},{3,0},{4,7},{5,6},{6,5},{7,4},{8,11},{9,10},{10,... | collective-permute-start | bytes 98312 | tf_op jit(solution)/shard_map/ppermute | solution.py:213
  17.0 0.3 shard_map.93.ours
  17.3 1.6 %collective-permute-start.14 = (bf16[512,256]{1,0:T(8,128)(2,1)S(1)}, bf16[512,256]{1,0:T(8,128)(2,1)S(1)}, u32[]{:S(2)}, u32[]{:S(2)}) collective-permute-start(bf16[512,256]{1,0:T(8,128)(2,1)S(1)} %shard_map.93.ours), channel_id=1, source_target_pairs={{0,16},{16,0},{1,17},{17,1},{2,18},{18,2},{3,19},{19,3},{4,20},{20... | collective-permute-start | bytes 786440 | tf_op jit(solution)/shard_map/ppermute | solution.py:222
  18.9 0.0 collective-permute-done.6.got1
  18.9 0.2 collective-permute-done.7.got2
  19.1 0.2 collective-permute-done.8.got3
  19.3 2.9 %collective-permute-start.9 = (bf16[64,256]{1,0:T(8,128)(2,1)S(1)}, bf16[64,256]{1,0:T(8,128)(2,1)S(1)}, u32[]{:S(2)}, u32[]{:S(2)}) collective-permute-start(bf16[64,256]{1,0:T(8,128)(2,1)S(1)} %get-tuple-element.39), channel_id=1, source_target_pairs={{0,9},{1,8},{2,11},{3,10},{4,13},{5,12},{6,15},{7,14},{8,1},{9,0},... | collective-permute-start | bytes 98312 | tf_op jit(solution)/shard_map/ppermute | solution.py:213
  22.2 1.6 %collective-permute-done.9.got = bf16[64,256]{1,0:T(8,128)(2,1)S(1)} collective-permute-done((bf16[64,256]{1,0:T(8,128)(2,1)S(1)}, bf16[64,256]{1,0:T(8,128)(2,1)S(1)}, u32[]{:S(2)}, u32[]{:S(2)}) %collective-permute-start.9) | collective-permute-done | bytes 32800 | tf_op jit(solution)/shard_map/ppermute | solution.py:213
  23.9 2.6 %collective-permute-start.12 = (bf16[64,256]{1,0:T(8,128)(2,1)S(1)}, bf16[64,256]{1,0:T(8,128)(2,1)S(1)}, u32[]{:S(2)}, u32[]{:S(2)}) collective-permute-start(bf16[64,256]{1,0:T(8,128)(2,1)S(1)} %get-tuple-element.41.pair.after), channel_id=1, source_target_pairs={{0,7},{1,6},{2,5},{3,4},{4,3},{5,2},{6,1},{7,0},{8,15},{9,14},{10,... | collective-permute-start | bytes 98312 | tf_op jit(solution)/shard_map/ppermute | solution.py:213
  26.4 0.0 collective-permute-start.11
  26.4 0.7 %collective-permute-start.10 = (bf16[64,256]{1,0:T(8,128)(2,1)S(1)}, bf16[64,256]{1,0:T(8,128)(2,1)S(1)}, u32[]{:S(2)}, u32[]{:S(2)}) collective-permute-start(bf16[64,256]{1,0:T(8,128)(2,1)S(1)} %get-tuple-element.41.pair.after), channel_id=1, source_target_pairs={{0,3},{1,2},{2,1},{3,0},{4,7},{5,6},{6,5},{7,4},{8,11},{9,10},{10,... | collective-permute-start | bytes 98312 | tf_op jit(solution)/shard_map/ppermute | solution.py:213
  27.1 0.0 collective-permute-done.14.got
  27.1 0.1 shard_map.94
  27.2 0.2 collective-permute-start.15
  27.5 0.8 %collective-permute-done.12.far3 = bf16[64,256]{1,0:T(8,128)(2,1)S(1)} collective-permute-done((bf16[64,256]{1,0:T(8,128)(2,1)S(1)}, bf16[64,256]{1,0:T(8,128)(2,1)S(1)}, u32[]{:S(2)}, u32[]{:S(2)}) %collective-permute-start.12) | collective-permute-done | bytes 32800 | tf_op jit(solution)/shard_map/ppermute | solution.py:213
  28.2 1.6 %collective-permute-done.11.far2 = bf16[64,256]{1,0:T(8,128)(2,1)S(1)} collective-permute-done((bf16[64,256]{1,0:T(8,128)(2,1)S(1)}, bf16[64,256]{1,0:T(8,128)(2,1)S(1)}, u32[]{:S(2)}, u32[]{:S(2)}) %collective-permute-start.11) | collective-permute-done | bytes 32800 | tf_op jit(solution)/shard_map/ppermute | solution.py:213
  29.8 0.0 collective-permute-done.10.far1
  29.8 0.0 collective-permute-done.15.refs_1_
  29.8 0.6 %shard_map.95 = (f32[128,256]{1,0:T(8,128)S(1)}, bf16[128,256]{1,0:T(8,128)(2,1)S(1)}, bf16[256,512]{1,0:T(8,128)(2,1)S(1)}, bf16[512,256]{1,0:T(8,128)(2,1)S(1)}) custom-call(bf16[256,256]{1,0:T(8,128)(2,1)S(1)} %shard_map.92.u, bf16[512,256]{1,0:T(8,128)(2,1)S(1)} %get-tuple-element.44.refs_0_, bf16[512,256]{1,0:T(8,128)(2,1)S(1)} %collective-permute-done.15.refs_1_, ...), custom_call_target="tpu_custom_call" | custom-call | flops 268435456 | bytes 1703936 | tf_op jit(solution)/shard_map/pallas_call | solution.py:35
  30.5 0.5 %collective-permute-start.20 = (bf16[512,256]{1,0:T(8,128)(2,1)S(1)}, bf16[512,256]{1,0:T(8,128)(2,1)S(1)}, u32[]{:S(2)}, u32[]{:S(2)}) collective-permute-start(bf16[512,256]{1,0:T(8,128)(2,1)S(1)} %get-tuple-element.54), channel_id=1, source_target_pairs={{0,1},{1,0},{2,3},{3,2},{4,5},{5,4},{6,7},{7,6},{8,9},{9,8},{10,11... | collective-permute-start | bytes 786440 | tf_op jit(solution)/shard_map/ppermute | solution.py:213
  30.9 0.3 shard_map.96.part
  31.2 2.7 %collective-permute-start.16 = (bf16[128,256]{1,0:T(8,128)(2,1)S(1)}, bf16[128,256]{1,0:T(8,128)(2,1)S(1)}, u32[]{:S(2)}, u32[]{:S(2)}) collective-permute-start(bf16[128,256]{1,0:T(8,128)(2,1)S(1)} %get-tuple-element.48), channel_id=1, source_target_pairs={{0,9},{1,8},{2,11},{3,10},{4,13},{5,12},{6,15},{7,14},{8,1},{9,0},... | collective-permute-start | bytes 196616 | tf_op jit(solution)/shard_map/ppermute | solution.py:213
  34.0 1.6 %collective-permute-start.21 = (bf16[512,256]{1,0:T(8,128)(2,1)S(1)}, bf16[512,256]{1,0:T(8,128)(2,1)S(1)}, u32[]{:S(2)}, u32[]{:S(2)}) collective-permute-start(bf16[512,256]{1,0:T(8,128)(2,1)S(1)} %shard_map.98.ours), channel_id=1, source_target_pairs={{0,16},{16,0},{1,17},{17,1},{2,18},{18,2},{3,19},{19,3},{4,20},{20... | collective-permute-start | bytes 786440 | tf_op jit(solution)/shard_map/ppermute | solution.py:222
  35.6 0.6 %collective-permute-done.16.got = bf16[128,256]{1,0:T(8,128)(2,1)S(1)} collective-permute-done((bf16[128,256]{1,0:T(8,128)(2,1)S(1)}, bf16[128,256]{1,0:T(8,128)(2,1)S(1)}, u32[]{:S(2)}, u32[]{:S(2)}) %collective-permute-start.16) | collective-permute-done | bytes 65568 | tf_op jit(solution)/shard_map/ppermute | solution.py:213
  36.2 2.7 %collective-permute-start.17 = (bf16[32,256]{1,0:T(8,128)(2,1)S(1)}, bf16[32,256]{1,0:T(8,128)(2,1)S(1)}, u32[]{:S(2)}, u32[]{:S(2)}) collective-permute-start(bf16[32,256]{1,0:T(8,128)(2,1)S(1)} %get-tuple-element.50), channel_id=1, source_target_pairs={{0,7},{1,6},{2,5},{3,4},{4,3},{5,2},{6,1},{7,0},{8,15},{9,14},{10,... | collective-permute-start | bytes 49160 | tf_op jit(solution)/shard_map/ppermute | solution.py:213
  38.8 0.0 collective-permute-start.18
  38.9 1.5 %collective-permute-start.19 = (bf16[32,256]{1,0:T(8,128)(2,1)S(1)}, bf16[32,256]{1,0:T(8,128)(2,1)S(1)}, u32[]{:S(2)}, u32[]{:S(2)}) collective-permute-start(bf16[32,256]{1,0:T(8,128)(2,1)S(1)} %get-tuple-element.52), channel_id=1, source_target_pairs={{0,3},{1,2},{2,1},{3,0},{4,7},{5,6},{6,5},{7,4},{8,11},{9,10},{10,... | collective-permute-start | bytes 49160 | tf_op jit(solution)/shard_map/ppermute | solution.py:213
  40.3 1.7 %collective-permute-done.18.got2 = bf16[32,256]{1,0:T(8,128)(2,1)S(1)} collective-permute-done((bf16[32,256]{1,0:T(8,128)(2,1)S(1)}, bf16[32,256]{1,0:T(8,128)(2,1)S(1)}, u32[]{:S(2)}, u32[]{:S(2)}) %collective-permute-start.18) | collective-permute-done | bytes 16416 | tf_op jit(solution)/shard_map/ppermute | solution.py:213
  42.0 0.0 collective-permute-done.19.got3
  42.0 0.7 %collective-permute-done.21.ngram_got = bf16[512,256]{1,0:T(8,128)(2,1)S(1)} collective-permute-done((bf16[512,256]{1,0:T(8,128)(2,1)S(1)}, bf16[512,256]{1,0:T(8,128)(2,1)S(1)}, u32[]{:S(2)}, u32[]{:S(2)}) %collective-permute-start.21) | collective-permute-done | bytes 262176 | tf_op jit(solution)/shard_map/ppermute | solution.py:222
  42.7 0.9 %shard_map.99 = (f32[32,256]{1,0:T(8,128)}, f32[512,256]{1,0:T(8,128)}) custom-call(f32[32,256]{1,0:T(8,128)S(1)} %get-tuple-element.40.doc, f32[32,256]{1,0:T(8,128)S(1)} %get-tuple-element.49.total, bf16[32,256]{1,0:T(8,128)(2,1)S(1)} %collective-permute-done.17.got1, bf16[32,256]{1,0:T(8,128)(2,1)S(1)} %collective-permute-done.18.got2, ...), custom_call_target="tpu_custom_call" | custom-call | tf_op jit(solution)/shard_map/pallas_call | solution.py:35
  (18 shorter events, 0.1 us)
Async XLA Ops:
  0.6 4.2 %copy-start.3 = (s32[1,1,16]{2,1,0:T(1,128)S(1)}, s32[1,1,16]{2,1,0:T(1,128)}, u32[]{:S(2)}) copy-start(s32[1,1,16]{2,1,0:T(1,128)} %ngrams_hbm.1) | copy-start | bytes 196
  0.6 4.2 %copy-start.2 = (s32[1,1,16]{2,1,0:T(1,128)S(1)}, s32[1,1,16]{2,1,0:T(1,128)}, u32[]{:S(2)}) copy-start(s32[1,1,16]{2,1,0:T(1,128)} %docs_hbm.1) | copy-start | bytes 196
  0.7 5.9 %collective-permute-start = (f32[32,256]{1,0:T(8,128)}, f32[32,256]{1,0:T(8,128)S(1)}, u32[]{:S(2)}, u32[]{:S(2)}) collective-permute-start(f32[32,256]{1,0:T(8,128)} %doc.1), channel_id=1, source_target_pairs={{0,9},{1,8},{2,11},{3,10},{4,13},{5,12},{6,15},{7,14},{8,1},{9,0},... | collective-permute-start | bytes 98312 | tf_op jit(solution)/shard_map/ppermute | solution.py:213
  4.9 1.7 %copy-start.1 = (f32[32,256]{1,0:T(8,128)S(1)}, f32[32,256]{1,0:T(8,128)}, u32[]{:S(2)}) copy-start(f32[32,256]{1,0:T(8,128)} %doc.1) | copy-start | bytes 98308
  6.6 4.5 %collective-permute-start.3 = (bf16[64,256]{1,0:T(8,128)(2,1)S(1)}, bf16[64,256]{1,0:T(8,128)(2,1)S(1)}, u32[]{:S(2)}, u32[]{:S(2)}) collective-permute-start(bf16[64,256]{1,0:T(8,128)(2,1)S(1)} %shard_map.87.pair), channel_id=1, source_target_pairs={{0,7},{1,6},{2,5},{3,4},{4,3},{5,2},{6,1},{7,0},{8,15},{9,14},{10,... | collective-permute-start | bytes 98312 | tf_op jit(solution)/shard_map/ppermute | solution.py:213
  9.4 3.5 %collective-permute-start.2 = (bf16[64,256]{1,0:T(8,128)(2,1)S(1)}, bf16[64,256]{1,0:T(8,128)(2,1)S(1)}, u32[]{:S(2)}, u32[]{:S(2)}) collective-permute-start(bf16[64,256]{1,0:T(8,128)(2,1)S(1)} %shard_map.87.pair), channel_id=1, source_target_pairs={{0,5},{1,4},{2,7},{3,6},{4,1},{5,0},{6,3},{7,2},{8,13},{9,12},{10,... | collective-permute-start | bytes 98312 | tf_op jit(solution)/shard_map/ppermute | solution.py:213
  9.5 3.5 %collective-permute-start.1 = (bf16[64,256]{1,0:T(8,128)(2,1)S(1)}, bf16[64,256]{1,0:T(8,128)(2,1)S(1)}, u32[]{:S(2)}, u32[]{:S(2)}) collective-permute-start(bf16[64,256]{1,0:T(8,128)(2,1)S(1)} %shard_map.87.pair), channel_id=1, source_target_pairs={{0,3},{1,2},{2,1},{3,0},{4,7},{5,6},{6,5},{7,4},{8,11},{9,10},{10,... | collective-permute-start | bytes 98312 | tf_op jit(solution)/shard_map/ppermute | solution.py:213
  10.1 2.8 %collective-permute-start.4 = (bf16[512,256]{1,0:T(8,128)(2,1)S(1)}, bf16[512,256]{1,0:T(8,128)(2,1)S(1)}, u32[]{:S(2)}, u32[]{:S(2)}) collective-permute-start(bf16[512,256]{1,0:T(8,128)(2,1)S(1)} %get-tuple-element.31.refs_0_), channel_id=1, source_target_pairs={{0,1},{1,0},{2,3},{3,2},{4,5},{5,4},{6,7},{7,6},{8,9},{9,8},{10,11... | collective-permute-start | bytes 786440 | tf_op jit(solution)/shard_map/ppermute | solution.py:213
  10.2 2.8 %collective-permute-start.5 = (bf16[512,512]{1,0:T(8,128)(2,1)S(1)}, bf16[512,512]{1,0:T(8,128)(2,1)S(1)}, u32[]{:S(2)}, u32[]{:S(2)}) collective-permute-start(bf16[512,512]{1,0:T(8,128)(2,1)S(1)} %get-tuple-element.33), channel_id=1, source_target_pairs={{0,1},{1,0},{2,3},{3,2},{4,5},{5,4},{6,7},{7,6},{8,9},{9,8},{10,11... | collective-permute-start | bytes 1572872 | tf_op jit(solution)/shard_map/ppermute | solution.py:213
  13.6 3.4 %collective-permute-start.13 = (bf16[512,256]{1,0:T(8,128)(2,1)S(1)}, bf16[512,256]{1,0:T(8,128)(2,1)S(1)}, u32[]{:S(2)}, u32[]{:S(2)}) collective-permute-start(bf16[512,256]{1,0:T(8,128)(2,1)S(1)} %get-tuple-element.43), channel_id=1, source_target_pairs={{0,1},{1,0},{2,3},{3,2},{4,5},{5,4},{6,7},{7,6},{8,9},{9,8},{10,11... | collective-permute-start | bytes 786440 | tf_op jit(solution)/shard_map/ppermute | solution.py:213
  14.1 4.8 %collective-permute-start.6 = (bf16[64,256]{1,0:T(8,128)(2,1)S(1)}, bf16[64,256]{1,0:T(8,128)(2,1)S(1)}, u32[]{:S(2)}, u32[]{:S(2)}) collective-permute-start(bf16[64,256]{1,0:T(8,128)(2,1)S(1)} %get-tuple-element.35), channel_id=1, source_target_pairs={{0,7},{1,6},{2,5},{3,4},{4,3},{5,2},{6,1},{7,0},{8,15},{9,14},{10,... | collective-permute-start | bytes 98312 | tf_op jit(solution)/shard_map/ppermute | solution.py:213
  15.7 3.4 %collective-permute-start.7 = (bf16[64,256]{1,0:T(8,128)(2,1)S(1)}, bf16[64,256]{1,0:T(8,128)(2,1)S(1)}, u32[]{:S(2)}, u32[]{:S(2)}) collective-permute-start(bf16[64,256]{1,0:T(8,128)(2,1)S(1)} %get-tuple-element.36), channel_id=1, source_target_pairs={{0,5},{1,4},{2,7},{3,6},{4,1},{5,0},{6,3},{7,2},{8,13},{9,12},{10,... | collective-permute-start | bytes 98312 | tf_op jit(solution)/shard_map/ppermute | solution.py:213
  15.9 3.4 %collective-permute-start.8 = (bf16[64,256]{1,0:T(8,128)(2,1)S(1)}, bf16[64,256]{1,0:T(8,128)(2,1)S(1)}, u32[]{:S(2)}, u32[]{:S(2)}) collective-permute-start(bf16[64,256]{1,0:T(8,128)(2,1)S(1)} %get-tuple-element.37), channel_id=1, source_target_pairs={{0,3},{1,2},{2,1},{3,0},{4,7},{5,6},{6,5},{7,4},{8,11},{9,10},{10,... | collective-permute-start | bytes 98312 | tf_op jit(solution)/shard_map/ppermute | solution.py:213
  17.3 9.8 %collective-permute-start.14 = (bf16[512,256]{1,0:T(8,128)(2,1)S(1)}, bf16[512,256]{1,0:T(8,128)(2,1)S(1)}, u32[]{:S(2)}, u32[]{:S(2)}) collective-permute-start(bf16[512,256]{1,0:T(8,128)(2,1)S(1)} %shard_map.93.ours), channel_id=1, source_target_pairs={{0,16},{16,0},{1,17},{17,1},{2,18},{18,2},{3,19},{19,3},{4,20},{20... | collective-permute-start | bytes 786440 | tf_op jit(solution)/shard_map/ppermute | solution.py:222
  19.3 7.8 %copy-start = (f32[512,256]{1,0:T(8,128)S(1)}, f32[512,256]{1,0:T(8,128)}, u32[]{:S(2)}) copy-start(f32[512,256]{1,0:T(8,128)} %v.1) | copy-start | bytes 1572868
  19.3 4.5 %collective-permute-start.9 = (bf16[64,256]{1,0:T(8,128)(2,1)S(1)}, bf16[64,256]{1,0:T(8,128)(2,1)S(1)}, u32[]{:S(2)}, u32[]{:S(2)}) collective-permute-start(bf16[64,256]{1,0:T(8,128)(2,1)S(1)} %get-tuple-element.39), channel_id=1, source_target_pairs={{0,9},{1,8},{2,11},{3,10},{4,13},{5,12},{6,15},{7,14},{8,1},{9,0},... | collective-permute-start | bytes 98312 | tf_op jit(solution)/shard_map/ppermute | solution.py:213
  23.9 4.4 %collective-permute-start.12 = (bf16[64,256]{1,0:T(8,128)(2,1)S(1)}, bf16[64,256]{1,0:T(8,128)(2,1)S(1)}, u32[]{:S(2)}, u32[]{:S(2)}) collective-permute-start(bf16[64,256]{1,0:T(8,128)(2,1)S(1)} %get-tuple-element.41.pair.after), channel_id=1, source_target_pairs={{0,7},{1,6},{2,5},{3,4},{4,3},{5,2},{6,1},{7,0},{8,15},{9,14},{10,... | collective-permute-start | bytes 98312 | tf_op jit(solution)/shard_map/ppermute | solution.py:213
  26.4 3.3 %collective-permute-start.11 = (bf16[64,256]{1,0:T(8,128)(2,1)S(1)}, bf16[64,256]{1,0:T(8,128)(2,1)S(1)}, u32[]{:S(2)}, u32[]{:S(2)}) collective-permute-start(bf16[64,256]{1,0:T(8,128)(2,1)S(1)} %get-tuple-element.41.pair.after), channel_id=1, source_target_pairs={{0,5},{1,4},{2,7},{3,6},{4,1},{5,0},{6,3},{7,2},{8,13},{9,12},{10,... | collective-permute-start | bytes 98312 | tf_op jit(solution)/shard_map/ppermute | solution.py:213
  26.4 3.4 %collective-permute-start.10 = (bf16[64,256]{1,0:T(8,128)(2,1)S(1)}, bf16[64,256]{1,0:T(8,128)(2,1)S(1)}, u32[]{:S(2)}, u32[]{:S(2)}) collective-permute-start(bf16[64,256]{1,0:T(8,128)(2,1)S(1)} %get-tuple-element.41.pair.after), channel_id=1, source_target_pairs={{0,3},{1,2},{2,1},{3,0},{4,7},{5,6},{6,5},{7,4},{8,11},{9,10},{10,... | collective-permute-start | bytes 98312 | tf_op jit(solution)/shard_map/ppermute | solution.py:213
  27.2 2.6 %collective-permute-start.15 = (bf16[512,256]{1,0:T(8,128)(2,1)S(1)}, bf16[512,256]{1,0:T(8,128)(2,1)S(1)}, u32[]{:S(2)}, u32[]{:S(2)}) collective-permute-start(bf16[512,256]{1,0:T(8,128)(2,1)S(1)} %get-tuple-element.44.refs_0_), channel_id=1, source_target_pairs={{0,1},{1,0},{2,3},{3,2},{4,5},{5,4},{6,7},{7,6},{8,9},{9,8},{10,11... | collective-permute-start | bytes 786440 | tf_op jit(solution)/shard_map/ppermute | solution.py:213
  30.5 3.5 %collective-permute-start.20 = (bf16[512,256]{1,0:T(8,128)(2,1)S(1)}, bf16[512,256]{1,0:T(8,128)(2,1)S(1)}, u32[]{:S(2)}, u32[]{:S(2)}) collective-permute-start(bf16[512,256]{1,0:T(8,128)(2,1)S(1)} %get-tuple-element.54), channel_id=1, source_target_pairs={{0,1},{1,0},{2,3},{3,2},{4,5},{5,4},{6,7},{7,6},{8,9},{9,8},{10,11... | collective-permute-start | bytes 786440 | tf_op jit(solution)/shard_map/ppermute | solution.py:213
  31.2 4.9 %collective-permute-start.16 = (bf16[128,256]{1,0:T(8,128)(2,1)S(1)}, bf16[128,256]{1,0:T(8,128)(2,1)S(1)}, u32[]{:S(2)}, u32[]{:S(2)}) collective-permute-start(bf16[128,256]{1,0:T(8,128)(2,1)S(1)} %get-tuple-element.48), channel_id=1, source_target_pairs={{0,9},{1,8},{2,11},{3,10},{4,13},{5,12},{6,15},{7,14},{8,1},{9,0},... | collective-permute-start | bytes 196616 | tf_op jit(solution)/shard_map/ppermute | solution.py:213
  34.0 8.7 %collective-permute-start.21 = (bf16[512,256]{1,0:T(8,128)(2,1)S(1)}, bf16[512,256]{1,0:T(8,128)(2,1)S(1)}, u32[]{:S(2)}, u32[]{:S(2)}) collective-permute-start(bf16[512,256]{1,0:T(8,128)(2,1)S(1)} %shard_map.98.ours), channel_id=1, source_target_pairs={{0,16},{16,0},{1,17},{17,1},{2,18},{18,2},{3,19},{19,3},{4,20},{20... | collective-permute-start | bytes 786440 | tf_op jit(solution)/shard_map/ppermute | solution.py:222
  36.2 4.1 %collective-permute-start.17 = (bf16[32,256]{1,0:T(8,128)(2,1)S(1)}, bf16[32,256]{1,0:T(8,128)(2,1)S(1)}, u32[]{:S(2)}, u32[]{:S(2)}) collective-permute-start(bf16[32,256]{1,0:T(8,128)(2,1)S(1)} %get-tuple-element.50), channel_id=1, source_target_pairs={{0,7},{1,6},{2,5},{3,4},{4,3},{5,2},{6,1},{7,0},{8,15},{9,14},{10,... | collective-permute-start | bytes 49160 | tf_op jit(solution)/shard_map/ppermute | solution.py:213
  38.8 3.2 %collective-permute-start.18 = (bf16[32,256]{1,0:T(8,128)(2,1)S(1)}, bf16[32,256]{1,0:T(8,128)(2,1)S(1)}, u32[]{:S(2)}, u32[]{:S(2)}) collective-permute-start(bf16[32,256]{1,0:T(8,128)(2,1)S(1)} %get-tuple-element.51), channel_id=1, source_target_pairs={{0,5},{1,4},{2,7},{3,6},{4,1},{5,0},{6,3},{7,2},{8,13},{9,12},{10,... | collective-permute-start | bytes 49160 | tf_op jit(solution)/shard_map/ppermute | solution.py:213
  38.9 3.2 %collective-permute-start.19 = (bf16[32,256]{1,0:T(8,128)(2,1)S(1)}, bf16[32,256]{1,0:T(8,128)(2,1)S(1)}, u32[]{:S(2)}, u32[]{:S(2)}) collective-permute-start(bf16[32,256]{1,0:T(8,128)(2,1)S(1)} %get-tuple-element.52), channel_id=1, source_target_pairs={{0,3},{1,2},{2,1},{3,0},{4,7},{5,6},{6,5},{7,4},{8,11},{9,10},{10,... | collective-permute-start | bytes 49160 | tf_op jit(solution)/shard_map/ppermute | solution.py:213
